TPU v7x, 32 devices: a whole 2x2x4 slice. The times are simulated.
32 devices in a mesh: gx: 2 (over core), gy: 16 (over z, y, x).
Axes of the slice: x: 2, y: 2, z: 4, core: 2. Of those that a mesh axis runs over, the one named last changes fastest.
Arguments:
- density: float32 [64, 16, 2048], P('gx', None, 'gy'), may hold values from 0.5 to 2
- velocity: float32 [3, 64, 16, 2048], P(None, 'gx', None, 'gy'), may hold values from -1.2 to 1.2
- bfield: float32 [3, 64, 16, 2048], P(None, 'gx', None, 'gy'), may hold values from -1.2 to 1.2
- pressure: float32 [64, 16, 2048], P('gx', None, 'gy'), may hold values from 0.5 to 2
- shear_shift: int32 [], replicated, may hold values from 0 to 2047
- remap_weight: int32 [], replicated, may hold values from 0 to 65535
Outputs:
- state: float32 [8, 64, 16, 2048], P(None, 'gx', None, 'gy')
All inputs are finite; a program needn't handle non-finite values.
Results may differ from a plain program's by a relative error of at most 0.0003.
Values sent between devices are 32-bit elements; how exact they have to be, the bound alone decides.
No kernel may reach another device: no remote copies, remote signals or barrier semaphores. Data moves between devices by JAX's collectives and lax.ppermute only.
A program may use at most 128 MiB of HBM per device.

v0:
```python
import functools

import jax
import jax.numpy as jnp
from jax import lax
from jax.experimental import pallas as pl
from jax.experimental.pallas import tpu as pltpu
from jax.sharding import PartitionSpec as P

GAMMA = 5.0 / 3.0
SHEAR_Q = 1.5
TIME_STEP = 0.03
WEIGHT_SCALE = 1.0 / 65536.0
TINY = 1e-30
FIELDS = 8


def root(x):
    return x * lax.rsqrt(jnp.maximum(x, TINY))


def side(state, normal):
    rho, pressure = state[0], state[7]
    vel, mag = state[1:4], state[4:7]
    one, two = [c for c in range(3) if c != normal]
    mom = [rho * v for v in vel]
    vn, bn = vel[normal], mag[normal]
    mn = mom[normal]
    mnvn = mn * vn
    kinetic = 0.5 * ((mnvn + mom[one] * vel[one]) + mom[two] * vel[two])
    bn2 = bn * bn
    bt2 = mag[one] * mag[one] + mag[two] * mag[two]
    half_b2 = 0.5 * (bt2 + bn2)
    inner = kinetic + 1.5 * pressure
    energy = inner + half_b2
    ind_one = vn * mag[one] - bn * vel[one]
    ind_two = vn * mag[two] - bn * vel[two]
    flux = [None] * FIELDS
    flux[0] = mn
    flux[1 + normal] = mnvn + (pressure + half_b2) - bn2
    flux[1 + one] = mn * vel[one] - bn * mag[one]
    flux[1 + two] = mn * vel[two] - bn * mag[two]
    flux[4 + one] = ind_one
    flux[4 + two] = ind_two
    flux[7] = vn * (inner + pressure) + (mag[one] * ind_one + mag[two] * ind_two)
    cons = [rho] + mom + list(mag) + [energy]
    half_gp = (0.5 * GAMMA) * pressure
    spread = half_gp - half_b2
    disc = spread * spread + (GAMMA * pressure) * bt2
    fast = (half_gp + half_b2) + root(disc)
    speed = jnp.abs(vn) + fast * lax.rsqrt(jnp.maximum(rho * fast, TINY))
    return flux, cons, speed


def face(left, right, normal):
    fl, ul, sl = side(left, normal)
    fr, ur, sr = side(right, normal)
    speed = jnp.maximum(sl, sr)
    out = []
    for f in range(FIELDS):
        jump = speed * (ur[f] - ul[f])
        out.append(-jump if fl[f] is None else (fl[f] + fr[f]) - jump)
    return out


def limited(up, down):
    return jnp.maximum(jnp.minimum(up, down), jnp.minimum(jnp.maximum(up, down), 0.0))


def shifted(x, by, axis):
    return pltpu.roll(x, by % x.shape[axis], axis)


def to_conserved(w):
    rho = w[0]
    mom = [rho * v for v in w[1:4]]
    kinetic = 0.5 * (mom[0] * w[1] + mom[1] * w[2] + mom[2] * w[3])
    magnetic = 0.5 * (w[4] * w[4] + w[5] * w[5] + w[6] * w[6])
    return [rho] + mom + list(w[4:7]) + [1.5 * w[7] + kinetic + magnetic]


def to_primitive(u):
    inverse = 1.0 / u[0]
    vel = [m * inverse for m in u[1:4]]
    kinetic = 0.5 * (u[1] * vel[0] + u[2] * vel[1] + u[3] * vel[2])
    magnetic = 0.5 * (u[4] * u[4] + u[5] * u[5] + u[6] * u[6])
    return [u[0]] + vel + list(u[4:7]) + [(GAMMA - 1.0) * (u[7] - kinetic - magnetic)]


def lanes_of(shape):
    return lax.broadcasted_iota(jnp.int32, shape, 1)


def load_row(ref, i):
    return [ref[f, i] for f in range(FIELDS)]


def pack_edges(ref, out_ref):
    rows, high, width = ref.shape[1:]
    lane = lanes_of((high, width))
    per_tile = width // 8
    for f in range(FIELDS):
        for i in range(rows):
            at = 8 * (i % per_tile)
            moved = shifted(ref[f, i], at + 4, 1)
            packed = moved if at == 0 else jnp.where(lane >= at, moved, packed)
            if at == 8 * (per_tile - 1) or i == rows - 1:
                out_ref[f, i // per_tile] = packed


def halves(pack_ref, last_ref, first_ref):
    lane = lanes_of(pack_ref.shape[2:])
    low = lane % 8 < 4
    for f in range(FIELDS):
        one, two = pack_ref[f, 0], pack_ref[f, 1]
        last_ref[f] = jnp.where(low, one, shifted(two, 4, 1))
        first_ref[f] = jnp.where(low, shifted(one, -4, 1), two)


def send_edges(flags, w_ref, pack_ref, last_ref, first_ref, shear_ref, swap_refs):
    rows = w_ref.shape[1]
    pack_edges(w_ref, pack_ref)
    halves(pack_ref, last_ref, first_ref)
    first = flags[0] == 1
    for k in range(2):
        low, high = load_row(w_ref, k), load_row(w_ref, rows - 2 + k)
        if len(swap_refs) == 1:
            for f in range(FIELDS):
                swap_refs[0][f, k] = jnp.where(first, high[f], low[f])
        else:
            for f in range(FIELDS):
                swap_refs[0][f, k] = low[f]
                swap_refs[1][f, k] = high[f]
        outer = to_conserved([jnp.where(first, low[f], high[f]) for f in range(FIELDS)])
        for f in range(FIELDS):
            shear_ref[f, k] = outer[f]


def prepare_kernel(flags, radial0, rho_hbm, vel_hbm, mag_hbm, pres_hbm, w_ref, *rest):
    *sends, sems = rest
    rows = w_ref.shape[1]
    parts = sems.shape[1]
    size = rows // parts
    copies = []
    for part in range(parts):
        at = pl.ds(part * size, size)
        copies.append(
            [
                pltpu.make_async_copy(rho_hbm.at[at], w_ref.at[0, at], sems.at[0, part]),
                pltpu.make_async_copy(vel_hbm.at[:, at], w_ref.at[pl.ds(1, 3), at], sems.at[1, part]),
                pltpu.make_async_copy(mag_hbm.at[:, at], w_ref.at[pl.ds(4, 3), at], sems.at[2, part]),
                pltpu.make_async_copy(pres_hbm.at[at], w_ref.at[7, at], sems.at[3, part]),
            ]
        )
        for copy in copies[-1]:
            copy.start()
    for part in range(parts):
        for copy in copies[part]:
            copy.wait()
        for i in range(part * size, (part + 1) * size):
            w_ref[2, i] = w_ref[2, i] - radial0[1] * (radial0[0] + float(i))
    send_edges(flags, w_ref, *sends[:4], sends[4:])


def axis_states(w, half):
    left, right = [], []
    for f in range(FIELDS):
        up = shifted(half[f], -1, 1) - half[f]
        slope = limited(up, shifted(up, 1, 1))
        left.append(w[f] + slope)
        right.append(w[f] - slope)
    return left, right


def wrapped(ref, f, value, before, after):
    high = value.shape[0]
    ref[f, 8 : 8 + high] = value
    if before:
        ref[f, 0:8] = value[high - 8 : high]
    if after:
        ref[f, 8 + high : 16 + high] = value[0:8]


def interior_kernel(second, radial0, w_ref, *refs):
    if second:
        w0_ref, u1_ref = refs[:2]
        refs = refs[2:]
    v_ref, hz_ref, rz_ref, fz_ref, wl_ref, dx_ref, fx_ref = refs
    rows, high, width = w_ref.shape[1:]
    step = 0.5 * TIME_STEP if second else TIME_STEP
    coef = 0.5 * step
    lane = lanes_of(w_ref.shape[2:])
    inner = jnp.logical_and(lane >= 1, lane < width - 2)
    omega_q = radial0[1]
    omega = omega_q / SHEAR_Q
    next_row, last_row = slice(9, 9 + high), slice(7, 7 + high)

    for f in range(FIELDS):
        blank = jnp.zeros((high, width), jnp.float32)
        dx_ref[f], fx_ref[f], wl_ref[f] = blank, blank, w_ref[f, 0]

    def body(i, carry):
        w = load_row(w_ref, i)
        half = [0.5 * x for x in w]

        left = []
        for f in range(FIELDS):
            wrapped(hz_ref, f, half[f], True, True)
            slope = limited(hz_ref[f, next_row] - half[f], half[f] - hz_ref[f, last_row])
            left.append(w[f] + slope)
            wrapped(rz_ref, f, w[f] - slope, False, True)
        fz = face(left, [rz_ref[f, next_row] for f in range(FIELDS)], 2)
        total = []
        for f in range(FIELDS):
            wrapped(fz_ref, f, fz[f], True, False)
            total.append(fz[f] - fz_ref[f, last_row])

        left, right = axis_states(w, half)
        fy = face(left, [shifted(r, -1, 1) for r in right], 1)
        fy = [jnp.where(inner, f, 0.0) for f in fy]
        total = [total[f] + (fy[f] - shifted(fy[f], 1, 1)) for f in range(FIELDS)]

        after, before = jnp.minimum(i + 1, rows - 1), jnp.maximum(i - 1, 0)
        right, wl = [], [wl_ref[f] for f in range(FIELDS)]
        for f in range(FIELDS):
            up = 0.5 * w_ref[f, after] - half[f]
            slope = limited(up, dx_ref[f])
            dx_ref[f] = up
            wl_ref[f] = w[f] + slope
            right.append(w[f] - slope)
        fx = face(wl, right, 0)
        valid = jnp.logical_and(i >= 2, i <= rows - 2)
        for f in range(FIELDS):
            here = jnp.where(valid, fx[f], 0.0)
            v_ref[f, before] = v_ref[f, before] - coef * (here - fx_ref[f])
            fx_ref[f] = here

        x = radial0[0] + i.astype(jnp.float32)
        cons = to_conserved(w)
        if second:
            base = [0.5 * (a + u1_ref[f, i]) for f, a in enumerate(to_conserved(load_row(w0_ref, i)))]
        else:
            base = cons
        tidal = 2.0 * omega * omega_q * x
        value = [base[f] - coef * total[f] for f in range(FIELDS)]
        value[1] = value[1] + ((step * 2.0) * omega * cons[2] + (step * tidal) * cons[0])
        value[2] = value[2] - ((step * 2.0) * omega) * cons[1]
        value[7] = value[7] + (step * tidal) * cons[1]
        for f in range(FIELDS):
            v_ref[f, i] = value[f]
        return carry

    lax.fori_loop(0, rows, body, 0)


def sheared_rows(flags, weights, near_ref, next_ref):
    first = flags[0] == 1
    high, width = near_ref.shape[2:]
    start = flags[2]
    lane = lanes_of((high, width))

    def taken(one, two, at):
        back = lax.rem(2 * width - at, width)
        return jnp.where(lane < width - at, pltpu.roll(one, back, 1), pltpu.roll(two, back, 1))

    rows = []
    for k in range(2):
        ghost = []
        for f in range(FIELDS):
            near, following = near_ref[f, k], next_ref[f, k]
            one = jnp.where(first, following, near)
            two = jnp.where(first, near, following)
            ghost.append(weights[0] * taken(one, two, start + 1) + weights[1] * taken(one, two, start))
        delta = weights[2]
        boosted = list(ghost)
        boosted[2] = ghost[2] + ghost[0] * delta
        boosted[7] = ghost[7] + ghost[2] * delta + 0.5 * ghost[0] * delta * delta
        rows.append(to_primitive(boosted))
    return rows


def edge_kernel(
    second, flags, weights, v_ref, w_ref, own_ref, low_ref, high_ref, xl_ref, xr_ref, near_ref, next_ref, *refs
):
    rows, high, width = w_ref.shape[1:]
    step = 0.5 * TIME_STEP if second else TIME_STEP
    coef = 0.5 * step
    if second:
        out_ref, d_ref = refs
    else:
        w1_ref, out_ref, *sends, d_ref = refs
    first, last = flags[0] == 1, flags[1] == 1
    lane = lanes_of((high, width))
    place = lane % 8
    low = place < 4

    for part in range(2):
        own = [own_ref[f, part] for f in range(FIELDS)]
        a = [low_ref[f] if part == 0 else shifted(low_ref[f], -4, 1) for f in range(FIELDS)]
        b = [shifted(high_ref[f], 4, 1) if part == 0 else high_ref[f] for f in range(FIELDS)]
        a = [jnp.where(low, a[f], own[f]) for f in range(FIELDS)]
        b = [jnp.where(low, own[f], b[f]) for f in range(FIELDS)]
        left, right = axis_states(a, [0.5 * x for x in a])
        fa = face(left, [shifted(r, -1, 1) for r in right], 1)
        left, right = axis_states(b, [0.5 * x for x in b])
        fb = face(left, [shifted(r, -1, 1) for r in right], 1)
        upper_at = jnp.logical_and(place >= 2, place <= 4)
        lower_at = jnp.logical_and(place >= 3, place <= 5)
        for f in range(FIELDS):
            upper = jnp.where(upper_at, jnp.where(low, fb[f], fa[f]), 0.0)
            lower = shifted(jnp.where(place == 2, fb[f], fa[f]), 1, 1)
            d_ref[f, part] = coef * (upper - jnp.where(lower_at, lower, 0.0))

    def x_states(cells):
        left, right = [], []
        for f in range(FIELDS):
            before, here, after = (c[f] for c in cells)
            slope = limited(0.5 * (after - here), 0.5 * (here - before))
            left.append(here + slope)
            right.append(here - slope)
        return left, right

    ghost = sheared_rows(flags, weights, near_ref, next_ref)
    ghost_low = [[jnp.where(first, ghost[k][f], xl_ref[f, k]) for f in range(FIELDS)] for k in range(2)]
    cells = ghost_low + [load_row(w_ref, i) for i in range(3)]
    sides = [x_states(cells[k : k + 3]) for k in range(3)]
    outer = face(sides[0][0], sides[1][1], 0)
    inner_face = face(sides[1][0], sides[2][1], 0)
    for f in range(FIELDS):
        v_ref[f, 0] = v_ref[f, 0] - coef * (inner_face[f] - outer[f])
        v_ref[f, 1] = v_ref[f, 1] + coef * inner_face[f]
    ghost_high = [[jnp.where(last, ghost[k][f], xr_ref[f, k]) for f in range(FIELDS)] for k in range(2)]
    cells = [load_row(w_ref, rows - 3 + i) for i in range(3)] + ghost_high
    sides = [x_states(cells[k : k + 3]) for k in range(3)]
    inner_face = face(sides[0][0], sides[1][1], 0)
    outer = face(sides[1][0], sides[2][1], 0)
    for f in range(FIELDS):
        v_ref[f, rows - 2] = v_ref[f, rows - 2] - coef * inner_face[f]
        v_ref[f, rows - 1] = v_ref[f, rows - 1] - coef * (outer[f] - inner_face[f])

    edge = jnp.logical_or(lane < 2, lane >= width - 2)
    per_tile = width // 8
    for f in range(FIELDS):
        for i in range(rows):
            move = shifted(d_ref[f, i // per_tile], -4 - 8 * (i % per_tile), 1)
            out_ref[f, i] = v_ref[f, i] - jnp.where(edge, move, 0.0)
    if not second:

        def body(i, carry):
            prim = to_primitive(load_row(out_ref, i))
            for f in range(FIELDS):
                w1_ref[f, i] = prim[f]
            return carry

        lax.fori_loop(0, rows, body, 0, unroll=4)
        send_edges(flags, w1_ref, *sends[:4], sends[4:])


def call(kernel, name, scalars, arrays, shapes, scratch=(), in_hbm=False):
    smem = pl.BlockSpec(memory_space=pltpu.SMEM)
    vmem = pl.BlockSpec(memory_space=pltpu.VMEM)
    return pl.pallas_call(
        kernel,
        name=name,
        out_shape=[jax.ShapeDtypeStruct(s, jnp.float32) for s in shapes],
        in_specs=[smem] * len(scalars) + [pl.BlockSpec(memory_space=pltpu.HBM) if in_hbm else vmem] * len(arrays),
        out_specs=[vmem] * len(shapes),
        scratch_shapes=[pltpu.VMEM(s, jnp.float32) if isinstance(s, tuple) else s for s in scratch],
        compiler_params=pltpu.CompilerParams(vmem_limit_bytes=16 * 1024 * 1024),
    )(*scalars, *arrays)


def exchange(last, first, swap):
    count_x, count_y = lax.axis_size("gx"), lax.axis_size("gy")
    low = lax.ppermute(last, "gy", [(i, (i + 1) % count_y) for i in range(count_y)])
    high = lax.ppermute(first, "gy", [((i + 1) % count_y, i) for i in range(count_y)])
    if len(swap) == 1:
        x_low = x_high = lax.ppermute(swap[0], "gx", [(0, 1), (1, 0)])
    else:
        x_low = lax.ppermute(swap[1], "gx", [(i, i + 1) for i in range(count_x - 1)])
        x_high = lax.ppermute(swap[0], "gx", [(i + 1, i) for i in range(count_x - 1)])
    return low, high, x_low, x_high


def crossing(by, shear):
    count_x, count_y = lax.axis_size("gx"), lax.axis_size("gy")
    last = (count_x - 1) * count_y
    pairs = []
    for gy in range(count_y):
        pairs.append((last + gy, (gy + by) % count_y))
        pairs.append((gy, last + (gy - by) % count_y))
    return lax.ppermute(shear, ("gx", "gy"), pairs)


def inner_part(second, block, radial0, shear, *states):
    full = states[0].shape
    high, width = full[2:]
    tile = (FIELDS, high, width)
    padded = (FIELDS, high + 16, width)
    scratch = [padded, padded, padded, tile, tile, tile]

    def branch(by):
        def run(radial0, shear, *states):
            near, following = crossing(by, shear), crossing(by + 1, shear)
            kernel = functools.partial(interior_kernel, second)
            (v,) = call(kernel, "inner_2" if second else "inner_1", [radial0], list(states), [full], scratch)
            return v, near, following

        return run

    branches = [branch(by) for by in range(lax.axis_size("gy"))]
    return lax.switch(block, branches, radial0, shear, *states)


def sections(block, flags, weights, radial0, w0, pack, last, first, shear, *swap):
    full = w0.shape
    moves = [pack.shape]
    sends = [x.shape for x in (pack, last, first, shear, *swap)]
    got = exchange(last, first, swap)
    v, *sheared = inner_part(False, block, radial0, shear, w0)
    w1, u1, pack1, last1, first1, shear1, *swap1 = call(
        functools.partial(edge_kernel, False),
        "edge_1",
        [flags, weights],
        [v, w0, pack, *got, *sheared],
        [full, full] + sends,
        moves,
    )
    got = exchange(last1, first1, swap1)
    v, *sheared = inner_part(True, block, radial0, shear1, w1, w0, u1)
    (out,) = call(
        functools.partial(edge_kernel, True),
        "edge_2",
        [flags, weights],
        [v, w1, pack1, *got, *sheared],
        [full],
        moves,
    )
    return out


def on_device(density, velocity, bfield, pressure, shear_shift, remap_weight):
    rows, high, width = density.shape
    count_x, count_y = lax.axis_size("gx"), lax.axis_size("gy")
    total_x = rows * count_x
    omega = 1.0 / (SHEAR_Q * total_x)
    row = lax.axis_index("gx")
    is_first, is_last = row == 0, row == count_x - 1
    radial0 = (row * rows).astype(jnp.float32) + 0.5 - 0.5 * total_x
    radial0 = jnp.stack([radial0, jnp.float32(SHEAR_Q * omega)])
    weight = remap_weight.astype(jnp.float32) * WEIGHT_SCALE
    block, rest = shear_shift // width, shear_shift % width
    start = jnp.where(is_first, width - 1 - rest, rest)
    flags = jnp.stack([is_first.astype(jnp.int32), is_last.astype(jnp.int32), start.astype(jnp.int32)])
    other = 1.0 - weight
    weights = jnp.stack(
        [
            jnp.where(is_first, 1.0 - weight, 1.0 - other),
            jnp.where(is_first, weight, other),
            jnp.where(is_first, 1.0, -1.0),
        ]
    )
    full = (FIELDS, rows, high, width)
    slab = (FIELDS, 2, high, width)
    packed = (FIELDS, 8 * rows // width, high, width)
    tile = (FIELDS, high, width)
    sends = [packed, tile, tile, slab] + [slab] * (1 if count_x == 2 else 2)
    start_state = call(
        prepare_kernel,
        "prepare",
        [flags, radial0],
        [density, velocity, bfield, pressure],
        [full] + sends,
        [pltpu.SemaphoreType.DMA((4, 2))],
        in_hbm=True,
    )
    return sections(block, flags, weights, radial0, *start_state)


def solution(mesh):
    placed = (
        P("gx", None, "gy"),
        P(None, "gx", None, "gy"),
        P(None, "gx", None, "gy"),
        P("gx", None, "gy"),
        P(),
        P(),
    )
    return jax.shard_map(
        on_device, mesh=mesh, in_specs=placed, out_specs=P(None, "gx", None, "gy"), check_vma=False
    )
```

profile of v0, /device:TPU:1, one launch (start us, length us, event | category | flops | bytes accessed | tf_op | source)
XLA Modules:
  0.0 62.3 jit_solution(8973646534755802280)
XLA Ops:
  0.7 0.1 pad_maximum_fusion.1.radial0
  0.8 0.1 pad_add_fusion.flags
  0.8 0.0 copy-start
  0.8 1.1 %copy-done = f32[3,32,16,128]{3,2,1,0:T(8,128)S(1)} copy-done((f32[3,32,16,128]{3,2,1,0:T(8,128)S(1)}, f32[3,32,16,128]{3,2,1,0:T(8,128)}, u32[]{:S(2)}) %copy-start) | copy-done | bytes 786456
  2.0 0.0 copy-start.1
  2.0 1.1 %copy-done.1 = f32[3,32,16,128]{3,2,1,0:T(8,128)S(1)} copy-done((f32[3,32,16,128]{3,2,1,0:T(8,128)S(1)}, f32[3,32,16,128]{3,2,1,0:T(8,128)}, u32[]{:S(2)}) %copy-start.1) | copy-done | bytes 786456
  3.1 0.0 copy-start.2
  3.1 0.9 %copy-done.2 = f32[32,16,128]{2,1,0:T(8,128)S(1)} copy-done((f32[32,16,128]{2,1,0:T(8,128)S(1)}, f32[32,16,128]{2,1,0:T(8,128)}, u32[]{:S(2)}) %copy-start.2) | copy-done | bytes 262168
  4.1 0.0 copy-start.3
  4.1 0.9 %copy-done.3 = f32[32,16,128]{2,1,0:T(8,128)S(1)} copy-done((f32[32,16,128]{2,1,0:T(8,128)S(1)}, f32[32,16,128]{2,1,0:T(8,128)}, u32[]{:S(2)}) %copy-start.3) | copy-done | bytes 262168
  5.0 2.2 %prepare.1 = (f32[8,32,16,128]{3,2,1,0:T(8,128)S(1)}, f32[8,2,16,128]{3,2,1,0:T(8,128)S(1)}, f32[8,16,128]{2,1,0:T(8,128)S(1)}, f32[8,16,128]{2,1,0:T(8,128)S(1)...) custom-call(s32[3]{0:T(128)S(1)} %pad_add_fusion.flags, f32[2]{0:T(128)S(1)} %pad_maximum_fusion.1.radial0, ...), custom_call_target="tpu_custom_call" | custom-call | tf_op jit(solution)/shard_map/prepare/pallas_call | solution.py:362
  7.3 0.1 collective-permute-start.66
  7.4 2.7 %collective-permute-start.64 = (f32[8,16,128]{2,1,0:T(8,128)S(1)}, f32[8,16,128]{2,1,0:T(8,128)S(1)}, u32[]{:S(2)}, u32[]{:S(2)}) collective-permute-start(f32[8,16,128]{2,1,0:T(8,128)S(1)} %get-tuple-element.412), channel_id=1, source_target_pairs={{0,1},{1,2},{2,3},{3,4},{4,5},{5,6},{6,7},{7,8},{8,9},{9,10},{10,1... | collective-permute-start | bytes 196616 | tf_op jit(solution)/shard_map/ppermute | solution.py:375
  10.0 4.0 %collective-permute-start.65 = (f32[8,16,128]{2,1,0:T(8,128)S(1)}, f32[8,16,128]{2,1,0:T(8,128)S(1)}, u32[]{:S(2)}, u32[]{:S(2)}) collective-permute-start(f32[8,16,128]{2,1,0:T(8,128)S(1)} %get-tuple-element.413), channel_id=1, source_target_pairs={{1,0},{2,1},{3,2},{4,3},{5,4},{6,5},{7,6},{8,7},{9,8},{10,9},{11,1... | collective-permute-start | bytes 196616 | tf_op jit(solution)/shard_map/ppermute | solution.py:376
  14.7 14.8 %conditional.2 = (f32[8,32,16,128]{3,2,1,0:T(8,128)S(1)}, f32[8,2,16,128]{3,2,1,0:T(8,128)}, f32[8,2,16,128]{3,2,1,0:T(8,128)}) conditional(s32[]{:T(128)} %clamp.4, (f32[2]{0:T(128)S(1)}, f32[8,32,16,128]{3,2,1,0:T(8,128)S(1)}, f32[8,2,16,128]{3,2,1,0:T(8,128)S(1)}) %tuple.133, (f32[2]{0:T(128)S(1)}, ...), branch_computations={%region_0.1_spmd, %region_1.2_spmd, %region_2.3_spmd, %region_3.4_... | conditional | bytes 1048680 | solution.py:412
  14.8 0.1 collective-permute-start.5
  14.8 2.0 %collective-permute-start.4 = (f32[8,2,16,128]{3,2,1,0:T(8,128)S(1)}, f32[8,2,16,128]{3,2,1,0:T(8,128)}, u32[]{:S(2)}, u32[]{:S(2)}) collective-permute-start(f32[8,2,16,128]{3,2,1,0:T(8,128)S(1)} %get-tuple-element.269), channel_id=1, source_target_pairs={{16,2},{0,30},{17,3},{1,31},{18,4},{2,16},{19,5},{3,17},{20,6},{4,... | collective-permute-start | bytes 393224 | tf_op jit(solution)/shard_map/cond/branch_2_fun/ppermute | solution.py:392
  16.9 12.6 %inner_1.18 = f32[8,32,16,128]{3,2,1,0:T(8,128)S(1)} custom-call(f32[2]{0:T(128)S(1)} %get-tuple-element.267.radial0, f32[8,32,16,128]{3,2,1,0:T(8,128)S(1)} %get-tuple-element.268.w_ref), custom_call_target="tpu_custom_call" | custom-call | tf_op jit(solution)/shard_map/cond/branch_2_fun/inner_1/pallas_call | solution.py:362
  29.5 0.0 collective-permute-done.5
  29.5 0.0 collective-permute-done.4
  29.5 0.0 copy-start.4
  29.5 0.1 pad_maximum_fusion.weights
  29.6 0.0 collective-permute-done.64.low_ref
  29.6 0.0 collective-permute-done.65.high_ref
  29.6 0.0 collective-permute-done.66.xl_ref.xr_ref
  29.6 1.2 %copy-done.4 = f32[8,32,16,128]{3,2,1,0:T(8,128)} copy-done((f32[8,32,16,128]{3,2,1,0:T(8,128)}, f32[8,32,16,128]{3,2,1,0:T(8,128)S(1)}, u32[]{:S(2)}) %copy-start.4) | copy-done | bytes 2097176
  30.8 5.7 %edge_1.1 = (f32[8,32,16,128]{3,2,1,0:T(8,128)}, f32[8,32,16,128]{3,2,1,0:T(8,128)S(1)}, f32[8,2,16,128]{3,2,1,0:T(8,128)S(1)}, f32[8,16,128]{2,1,0:T(8,128)S(1)...) custom-call(s32[3]{0:T(128)S(1)} %pad_add_fusion.flags, ...), custom_call_target="tpu_custom_call" | custom-call | tf_op jit(solution)/shard_map/edge_1/pallas_call | solution.py:362
  36.6 0.2 collective-permute-start.69
  36.8 1.2 %collective-permute-start.67 = (f32[8,16,128]{2,1,0:T(8,128)S(1)}, f32[8,16,128]{2,1,0:T(8,128)S(1)}, u32[]{:S(2)}, u32[]{:S(2)}) collective-permute-start(f32[8,16,128]{2,1,0:T(8,128)S(1)} %get-tuple-element.422), channel_id=1, source_target_pairs={{0,1},{1,2},{2,3},{3,4},{4,5},{5,6},{6,7},{7,8},{8,9},{9,10},{10,1... | collective-permute-start | bytes 196616 | tf_op jit(solution)/shard_map/ppermute | solution.py:375
  38.0 3.9 %collective-permute-start.68 = (f32[8,16,128]{2,1,0:T(8,128)S(1)}, f32[8,16,128]{2,1,0:T(8,128)S(1)}, u32[]{:S(2)}, u32[]{:S(2)}) collective-permute-start(f32[8,16,128]{2,1,0:T(8,128)S(1)} %get-tuple-element.423), channel_id=1, source_target_pairs={{1,0},{2,1},{3,2},{4,3},{5,4},{6,5},{7,6},{8,7},{9,8},{10,9},{11,1... | collective-permute-start | bytes 196616 | tf_op jit(solution)/shard_map/ppermute | solution.py:376
  41.9 15.4 %conditional.3 = (f32[8,32,16,128]{3,2,1,0:T(8,128)S(1)}, f32[8,2,16,128]{3,2,1,0:T(8,128)}, f32[8,2,16,128]{3,2,1,0:T(8,128)}) conditional(s32[]{:T(128)} %clamp.4, (f32[2]{0:T(128)S(1)}, f32[8,32,16,128]{3,2,1,0:T(8,128)}, f32[8,32,16,128]{3,2,1,0:T(8,128)S(1)}, f32[8,32,16,128]{3,2,1,0:T(8,128)S(1)}, ...), branch_computations={%region_16.17_spmd, %region_17.18_spmd, %region_18.19_spmd, %regio... | conditional | bytes 1048680 | solution.py:412
  41.9 0.0 collective-permute-start.37
  41.9 1.5 %collective-permute-start.36 = (f32[8,2,16,128]{3,2,1,0:T(8,128)S(1)}, f32[8,2,16,128]{3,2,1,0:T(8,128)}, u32[]{:S(2)}, u32[]{:S(2)}) collective-permute-start(f32[8,2,16,128]{3,2,1,0:T(8,128)S(1)} %get-tuple-element.323), channel_id=1, source_target_pairs={{16,2},{0,30},{17,3},{1,31},{18,4},{2,16},{19,5},{3,17},{20,6},{4,... | collective-permute-start | bytes 393224 | tf_op jit(solution)/shard_map/cond/branch_2_fun/ppermute | solution.py:392
  43.4 13.7 %inner_2.18 = f32[8,32,16,128]{3,2,1,0:T(8,128)S(1)} custom-call(f32[2]{0:T(128)S(1)} %get-tuple-element.319.radial0, f32[8,32,16,128]{3,2,1,0:T(8,128)} %get-tuple-element.320.w_ref, f32[8,32,16,128]{3,2,1,0:T(8,128)S(1)} %get-tuple-element.321.refs_0_, f32[8,32,16,128]{3,2,1,0:T(8,128)S(1)} %get-tuple-element.322.refs_1_), custom_call_target="tpu_custom_call" | custom-call | tf_op jit(solution)/shard_map/cond/branch_2_fun/inner_2/pallas_call | solution.py:362
  57.0 0.0 collective-permute-done.37
  57.0 0.0 collective-permute-done.36
  57.2 0.0 collective-permute-done.67.low_ref
  57.2 0.0 collective-permute-done.68.high_ref
  57.3 0.0 collective-permute-done.69.xl_ref.xr_ref
  57.3 5.0 %edge_2.1 = f32[8,32,16,128]{3,2,1,0:T(8,128)} custom-call(s32[3]{0:T(128)S(1)} %pad_add_fusion.flags, f32[3]{0:T(128)S(1)} %pad_maximum_fusion.weights, f32[8,32,16,128]{3,2,1,0:T(8,128)S(1)} %get-tuple-element.420.v_ref, f32[8,32,16,128]{3,2,1,0:T(8,128)} %get-tuple-element.417.w_ref, f32[8,2,16,128]{3,2,1,0:T(8,128)S(1)} %get-tuple-element.421.own_ref, ...), custom_call_target="tpu_custom_call" | custom-call | tf_op jit(solution)/shard_map/edge_2/pallas_call | solution.py:362
Async XLA Ops:
  0.8 1.1 %copy-start = (f32[3,32,16,128]{3,2,1,0:T(8,128)S(1)}, f32[3,32,16,128]{3,2,1,0:T(8,128)}, u32[]{:S(2)}) copy-start(f32[3,32,16,128]{3,2,1,0:T(8,128)} %vel_hbm.1) | copy-start | bytes 2359300
  2.0 1.1 %copy-start.1 = (f32[3,32,16,128]{3,2,1,0:T(8,128)S(1)}, f32[3,32,16,128]{3,2,1,0:T(8,128)}, u32[]{:S(2)}) copy-start(f32[3,32,16,128]{3,2,1,0:T(8,128)} %mag_hbm.1) | copy-start | bytes 2359300
  3.1 0.9 %copy-start.2 = (f32[32,16,128]{2,1,0:T(8,128)S(1)}, f32[32,16,128]{2,1,0:T(8,128)}, u32[]{:S(2)}) copy-start(f32[32,16,128]{2,1,0:T(8,128)} %rho_hbm.1) | copy-start | bytes 786436
  4.1 0.9 %copy-start.3 = (f32[32,16,128]{2,1,0:T(8,128)S(1)}, f32[32,16,128]{2,1,0:T(8,128)}, u32[]{:S(2)}) copy-start(f32[32,16,128]{2,1,0:T(8,128)} %pres_hbm.1) | copy-start | bytes 786436
  7.3 22.4 %collective-permute-start.66 = (f32[8,2,16,128]{3,2,1,0:T(8,128)S(1)}, f32[8,2,16,128]{3,2,1,0:T(8,128)S(1)}, u32[]{:S(2)}, u32[]{:S(2)}) collective-permute-start(f32[8,2,16,128]{3,2,1,0:T(8,128)S(1)} %get-tuple-element.414), channel_id=1, source_target_pairs={{0,16},{16,0},{1,17},{17,1},{2,18},{18,2},{3,19},{19,3},{4,20},{20... | collective-permute-start | bytes 393224 | tf_op jit(solution)/shard_map/ppermute | solution.py:378
  7.4 22.2 %collective-permute-start.64 = (f32[8,16,128]{2,1,0:T(8,128)S(1)}, f32[8,16,128]{2,1,0:T(8,128)S(1)}, u32[]{:S(2)}, u32[]{:S(2)}) collective-permute-start(f32[8,16,128]{2,1,0:T(8,128)S(1)} %get-tuple-element.412), channel_id=1, source_target_pairs={{0,1},{1,2},{2,3},{3,4},{4,5},{5,6},{6,7},{7,8},{8,9},{9,10},{10,1... | collective-permute-start | bytes 196616 | tf_op jit(solution)/shard_map/ppermute | solution.py:375
  10.0 19.6 %collective-permute-start.65 = (f32[8,16,128]{2,1,0:T(8,128)S(1)}, f32[8,16,128]{2,1,0:T(8,128)S(1)}, u32[]{:S(2)}, u32[]{:S(2)}) collective-permute-start(f32[8,16,128]{2,1,0:T(8,128)S(1)} %get-tuple-element.413), channel_id=1, source_target_pairs={{1,0},{2,1},{3,2},{4,3},{5,4},{6,5},{7,6},{8,7},{9,8},{10,9},{11,1... | collective-permute-start | bytes 196616 | tf_op jit(solution)/shard_map/ppermute | solution.py:376
  14.8 14.7 %collective-permute-start.5 = (f32[8,2,16,128]{3,2,1,0:T(8,128)S(1)}, f32[8,2,16,128]{3,2,1,0:T(8,128)}, u32[]{:S(2)}, u32[]{:S(2)}) collective-permute-start(f32[8,2,16,128]{3,2,1,0:T(8,128)S(1)} %get-tuple-element.269), channel_id=1, source_target_pairs={{16,3},{0,29},{17,4},{1,30},{18,5},{2,31},{19,6},{3,16},{20,7},{4,... | collective-permute-start | bytes 393224 | tf_op jit(solution)/shard_map/cond/branch_2_fun/ppermute | solution.py:392
  14.8 14.7 %collective-permute-start.4 = (f32[8,2,16,128]{3,2,1,0:T(8,128)S(1)}, f32[8,2,16,128]{3,2,1,0:T(8,128)}, u32[]{:S(2)}, u32[]{:S(2)}) collective-permute-start(f32[8,2,16,128]{3,2,1,0:T(8,128)S(1)} %get-tuple-element.269), channel_id=1, source_target_pairs={{16,2},{0,30},{17,3},{1,31},{18,4},{2,16},{19,5},{3,17},{20,6},{4,... | collective-permute-start | bytes 393224 | tf_op jit(solution)/shard_map/cond/branch_2_fun/ppermute | solution.py:392
  29.5 1.3 %copy-start.4 = (f32[8,32,16,128]{3,2,1,0:T(8,128)}, f32[8,32,16,128]{3,2,1,0:T(8,128)S(1)}, u32[]{:S(2)}) copy-start(f32[8,32,16,128]{3,2,1,0:T(8,128)S(1)} %get-tuple-element.410.v_ref) | copy-start | bytes 6291460
  36.6 20.7 %collective-permute-start.69 = (f32[8,2,16,128]{3,2,1,0:T(8,128)S(1)}, f32[8,2,16,128]{3,2,1,0:T(8,128)S(1)}, u32[]{:S(2)}, u32[]{:S(2)}) collective-permute-start(f32[8,2,16,128]{3,2,1,0:T(8,128)S(1)} %get-tuple-element.424), channel_id=1, source_target_pairs={{0,16},{16,0},{1,17},{17,1},{2,18},{18,2},{3,19},{19,3},{4,20},{20... | collective-permute-start | bytes 393224 | tf_op jit(solution)/shard_map/ppermute | solution.py:378
  36.8 20.4 %collective-permute-start.67 = (f32[8,16,128]{2,1,0:T(8,128)S(1)}, f32[8,16,128]{2,1,0:T(8,128)S(1)}, u32[]{:S(2)}, u32[]{:S(2)}) collective-permute-start(f32[8,16,128]{2,1,0:T(8,128)S(1)} %get-tuple-element.422), channel_id=1, source_target_pairs={{0,1},{1,2},{2,3},{3,4},{4,5},{5,6},{6,7},{7,8},{8,9},{9,10},{10,1... | collective-permute-start | bytes 196616 | tf_op jit(solution)/shard_map/ppermute | solution.py:375
  38.0 19.2 %collective-permute-start.68 = (f32[8,16,128]{2,1,0:T(8,128)S(1)}, f32[8,16,128]{2,1,0:T(8,128)S(1)}, u32[]{:S(2)}, u32[]{:S(2)}) collective-permute-start(f32[8,16,128]{2,1,0:T(8,128)S(1)} %get-tuple-element.423), channel_id=1, source_target_pairs={{1,0},{2,1},{3,2},{4,3},{5,4},{6,5},{7,6},{8,7},{9,8},{10,9},{11,1... | collective-permute-start | bytes 196616 | tf_op jit(solution)/shard_map/ppermute | solution.py:376
  41.9 15.2 %collective-permute-start.37 = (f32[8,2,16,128]{3,2,1,0:T(8,128)S(1)}, f32[8,2,16,128]{3,2,1,0:T(8,128)}, u32[]{:S(2)}, u32[]{:S(2)}) collective-permute-start(f32[8,2,16,128]{3,2,1,0:T(8,128)S(1)} %get-tuple-element.323), channel_id=1, source_target_pairs={{16,3},{0,29},{17,4},{1,30},{18,5},{2,31},{19,6},{3,16},{20,7},{4,... | collective-permute-start | bytes 393224 | tf_op jit(solution)/shard_map/cond/branch_2_fun/ppermute | solution.py:392
  41.9 15.2 %collective-permute-start.36 = (f32[8,2,16,128]{3,2,1,0:T(8,128)S(1)}, f32[8,2,16,128]{3,2,1,0:T(8,128)}, u32[]{:S(2)}, u32[]{:S(2)}) collective-permute-start(f32[8,2,16,128]{3,2,1,0:T(8,128)S(1)} %get-tuple-element.323), channel_id=1, source_target_pairs={{16,2},{0,30},{17,3},{1,31},{18,4},{2,16},{19,5},{3,17},{20,6},{4,... | collective-permute-start | bytes 393224 | tf_op jit(solution)/shard_map/cond/branch_2_fun/ppermute | solution.py:392
where the time goes:
time: 63 us; the launch traced here: 62.3 us
  Pallas kernels  39.2 us (62%)
  starting transfers between devices  15.6 us (25%)
  local copies, waits for them, and re-layouts  5.38 us (9%)
  between operations  1.45 us (2%)
    pallas_call x5, Pallas kernels, call(): pl.pallas_call(kernel, name=name, out_shape=[jax.ShapeDtypeStruct(s, jnp....  39.2 us
    ppermute x2, starting transfers between devices, exchange(): lax.ppermute(first, 'gy', [((i + 1) % count_y, i) for i in range(count_y)])  7.85 us
    unnamed x10, local copies, waits for them, and re-layouts  5.38 us
    ppermute x2, starting transfers between devices, exchange(): lax.ppermute(last, 'gy', [(i, (i + 1) % count_y) for i in range(count_y)])  3.87 us
    ppermute x4, starting transfers between devices, crossing(): return lax.ppermute(shear, ('gx', 'gy'), pairs)  3.58 us
  transfers between devices with their start and end apart: 10, of which 0 were waited for; matrix products, arithmetic and copies ran while one was open for 0% of the time, Pallas kernels for 42%

commit v1 on v0

--- a/solution.py
+++ b/solution.py
@@ -13,6 +13,7 @@
 WEIGHT_SCALE = 1.0 / 65536.0
 TINY = 1e-30
 FIELDS = 8
+PAD = 8
 
 
 def root(x):
@@ -67,10 +68,6 @@
     return jnp.maximum(jnp.minimum(up, down), jnp.minimum(jnp.maximum(up, down), 0.0))
 
 
-def shifted(x, by, axis):
-    return pltpu.roll(x, by % x.shape[axis], axis)
-
-
 def to_conserved(w):
     rho = w[0]
     mom = [rho * v for v in w[1:4]]
@@ -95,32 +92,25 @@
     return [ref[f, i] for f in range(FIELDS)]
 
 
-def pack_edges(ref, out_ref):
-    rows, high, width = ref.shape[1:]
-    lane = lanes_of((high, width))
-    per_tile = width // 8
-    for f in range(FIELDS):
-        for i in range(rows):
-            at = 8 * (i % per_tile)
-            moved = shifted(ref[f, i], at + 4, 1)
-            packed = moved if at == 0 else jnp.where(lane >= at, moved, packed)
-            if at == 8 * (per_tile - 1) or i == rows - 1:
-                out_ref[f, i // per_tile] = packed
-
-
-def halves(pack_ref, last_ref, first_ref):
-    lane = lanes_of(pack_ref.shape[2:])
-    low = lane % 8 < 4
-    for f in range(FIELDS):
-        one, two = pack_ref[f, 0], pack_ref[f, 1]
-        last_ref[f] = jnp.where(low, one, shifted(two, 4, 1))
-        first_ref[f] = jnp.where(low, shifted(one, -4, 1), two)
-
-
-def send_edges(flags, w_ref, pack_ref, last_ref, first_ref, shear_ref, swap_refs):
+def turn(w_ref, f, g, wt_ref):
+    high, width = w_ref.shape[2:]
+    size = width // high
+    tile = w_ref[f, g * size : (g + 1) * size].reshape(width, width)
+    wt_ref[f, g, PAD : PAD + width] = tile.T
+
+
+def send_columns(wt_ref, last_ref, first_ref):
+    groups, rows = wt_ref.shape[1:3]
+    for f in range(FIELDS):
+        for k in range(2):
+            for g in range(groups):
+                to = slice(k * groups + g, k * groups + g + 1)
+                first_ref[f, to] = wt_ref[f, g, PAD + k : PAD + k + 1]
+                last_ref[f, to] = wt_ref[f, g, rows - PAD - 2 + k : rows - PAD - 1 + k]
+
+
+def send_rows(flags, w_ref, shear_ref, *swap_refs):
     rows = w_ref.shape[1]
-    pack_edges(w_ref, pack_ref)
-    halves(pack_ref, last_ref, first_ref)
     first = flags[0] == 1
     for k in range(2):
         low, high = load_row(w_ref, k), load_row(w_ref, rows - 2 + k)
@@ -136,7 +126,7 @@
             shear_ref[f, k] = outer[f]
 
 
-def prepare_kernel(flags, radial0, rho_hbm, vel_hbm, mag_hbm, pres_hbm, w_ref, *rest):
+def prepare_kernel(flags, radial0, rho_hbm, vel_hbm, mag_hbm, pres_hbm, w_ref, wt_ref, last_ref, first_ref, *rest):
     *sends, sems = rest
     rows = w_ref.shape[1]
     parts = sems.shape[1]
@@ -159,16 +149,19 @@
             copy.wait()
         for i in range(part * size, (part + 1) * size):
             w_ref[2, i] = w_ref[2, i] - radial0[1] * (radial0[0] + float(i))
-    send_edges(flags, w_ref, *sends[:4], sends[4:])
-
-
-def axis_states(w, half):
+        for f in range(FIELDS):
+            turn(w_ref, f, part, wt_ref)
+    send_columns(wt_ref, last_ref, first_ref)
+    send_rows(flags, w_ref, *sends)
+
+
+def three_states(cells):
     left, right = [], []
     for f in range(FIELDS):
-        up = shifted(half[f], -1, 1) - half[f]
-        slope = limited(up, shifted(up, 1, 1))
-        left.append(w[f] + slope)
-        right.append(w[f] - slope)
+        before, here, after = (c[f] for c in cells)
+        slope = limited(0.5 * (after - here), 0.5 * (here - before))
+        left.append(here + slope)
+        right.append(here - slope)
     return left, right
 
 
@@ -181,16 +174,23 @@
         ref[f, 8 + high : 16 + high] = value[0:8]
 
 
-def interior_kernel(second, radial0, w_ref, *refs):
+def behind(ref, f, value):
+    high = value.shape[0]
+    ref[f, 8 : 8 + high] = value
+    result = ref[f, 7 : 7 + high]
+    ref[f, 0:8] = value[high - 8 : high]
+    return result
+
+
+def interior_kernel(second, radial0, w_ref, wt_ref, *refs):
     if second:
         w0_ref, u1_ref = refs[:2]
         refs = refs[2:]
-    v_ref, hz_ref, rz_ref, fz_ref, wl_ref, dx_ref, fx_ref = refs
+    v_ref, dy_ref, hz_ref, rz_ref, fz_ref, wl_ref, dx_ref, fx_ref = refs
     rows, high, width = w_ref.shape[1:]
+    groups = wt_ref.shape[1]
     step = 0.5 * TIME_STEP if second else TIME_STEP
     coef = 0.5 * step
-    lane = lanes_of(w_ref.shape[2:])
-    inner = jnp.logical_and(lane >= 1, lane < width - 2)
     omega_q = radial0[1]
     omega = omega_q / SHEAR_Q
     next_row, last_row = slice(9, 9 + high), slice(7, 7 + high)
@@ -214,11 +214,6 @@
         for f in range(FIELDS):
             wrapped(fz_ref, f, fz[f], True, False)
             total.append(fz[f] - fz_ref[f, last_row])
-
-        left, right = axis_states(w, half)
-        fy = face(left, [shifted(r, -1, 1) for r in right], 1)
-        fy = [jnp.where(inner, f, 0.0) for f in fy]
-        total = [total[f] + (fy[f] - shifted(fy[f], 1, 1)) for f in range(FIELDS)]
 
         after, before = jnp.minimum(i + 1, rows - 1), jnp.maximum(i - 1, 0)
         right, wl = [], [wl_ref[f] for f in range(FIELDS)]
@@ -252,6 +247,33 @@
 
     lax.fori_loop(0, rows, body, 0)
 
+    size = 16
+    strips = width // size
+    row = lax.broadcasted_iota(jnp.int32, (size, width), 0)
+
+    def body_y(n, carry):
+        g, start = lax.div(n, strips), size * lax.rem(n, strips)
+        at = pl.multiple_of(start + PAD, 8)
+        left, right = [], []
+        for f in range(FIELDS):
+            w = wt_ref[f, g, pl.ds(at, size)]
+            up = 0.5 * (wt_ref[f, g, pl.ds(at + 1, size)] - w)
+            slope = limited(up, behind(hz_ref, f, up))
+            left.append(behind(rz_ref, f, w + slope))
+            right.append(w - slope)
+        fy = face(left, right, 1)
+        cell = row + start
+        valid = jnp.logical_and(cell >= 2, cell <= width - 2)
+        for f in range(FIELDS):
+            here = jnp.where(valid, fy[f], 0.0)
+            dy_ref[f, g, pl.ds(at - 1, size)] = coef * (here - behind(fz_ref, f, here))
+        return carry
+
+    lax.fori_loop(0, groups * strips, body_y, 0)
+    for f in range(FIELDS):
+        for g in range(groups):
+            dy_ref[f, g, PAD + width - 1 : PAD + width] = jnp.zeros((1, width), jnp.float32)
+
 
 def sheared_rows(flags, weights, near_ref, next_ref):
     first = flags[0] == 1
@@ -279,81 +301,88 @@
     return rows
 
 
-def edge_kernel(
-    second, flags, weights, v_ref, w_ref, own_ref, low_ref, high_ref, xl_ref, xr_ref, near_ref, next_ref, *refs
-):
+def edge_kernel(second, flags, weights, v_ref, dy_ref, w_ref, wt_ref, low_ref, high_ref, xl_ref, xr_ref, near_ref, next_ref, *refs):
     rows, high, width = w_ref.shape[1:]
+    groups = wt_ref.shape[1]
     step = 0.5 * TIME_STEP if second else TIME_STEP
     coef = 0.5 * step
     if second:
-        out_ref, d_ref = refs
+        out_ref, e_ref, a_ref, c_ref = refs
     else:
-        w1_ref, out_ref, *sends, d_ref = refs
+        w1_ref, wt1_ref, out_ref, last_ref, first_ref, *sends, e_ref, a_ref, c_ref = refs
     first, last = flags[0] == 1, flags[1] == 1
-    lane = lanes_of((high, width))
-    place = lane % 8
-    low = place < 4
-
-    for part in range(2):
-        own = [own_ref[f, part] for f in range(FIELDS)]
-        a = [low_ref[f] if part == 0 else shifted(low_ref[f], -4, 1) for f in range(FIELDS)]
-        b = [shifted(high_ref[f], 4, 1) if part == 0 else high_ref[f] for f in range(FIELDS)]
-        a = [jnp.where(low, a[f], own[f]) for f in range(FIELDS)]
-        b = [jnp.where(low, own[f], b[f]) for f in range(FIELDS)]
-        left, right = axis_states(a, [0.5 * x for x in a])
-        fa = face(left, [shifted(r, -1, 1) for r in right], 1)
-        left, right = axis_states(b, [0.5 * x for x in b])
-        fb = face(left, [shifted(r, -1, 1) for r in right], 1)
-        upper_at = jnp.logical_and(place >= 2, place <= 4)
-        lower_at = jnp.logical_and(place >= 3, place <= 5)
-        for f in range(FIELDS):
-            upper = jnp.where(upper_at, jnp.where(low, fb[f], fa[f]), 0.0)
-            lower = shifted(jnp.where(place == 2, fb[f], fa[f]), 1, 1)
-            d_ref[f, part] = coef * (upper - jnp.where(lower_at, lower, 0.0))
-
-    def x_states(cells):
-        left, right = [], []
-        for f in range(FIELDS):
-            before, here, after = (c[f] for c in cells)
-            slope = limited(0.5 * (after - here), 0.5 * (here - before))
-            left.append(here + slope)
-            right.append(here - slope)
-        return left, right
+
+    for f in range(FIELDS):
+        for k in range(5):
+            cell = k - 2
+            if cell < 0:
+                e_ref[f, k, 0:groups] = low_ref[f, k * groups : (k + 1) * groups]
+            else:
+                for g in range(groups):
+                    e_ref[f, k, g : g + 1] = wt_ref[f, g, PAD + cell : PAD + cell + 1]
+            cell = width - 3 + k
+            if cell >= width:
+                at = (cell - width) * groups
+                e_ref[f, k, groups : 2 * groups] = high_ref[f, at : at + groups]
+            else:
+                for g in range(groups):
+                    e_ref[f, k, groups + g : groups + g + 1] = wt_ref[f, g, PAD + cell : PAD + cell + 1]
+    cells = [[e_ref[f, k] for f in range(FIELDS)] for k in range(5)]
+    sides = [three_states(cells[k : k + 3]) for k in range(3)]
+    one = face(sides[0][0], sides[1][1], 1)
+    two = face(sides[1][0], sides[2][1], 1)
+    low_end = lax.broadcasted_iota(jnp.int32, one[0].shape, 0) < groups
+    for f in range(FIELDS):
+        a_ref[f, 0] = coef * (two[f] - one[f])
+        a_ref[f, 1] = coef * jnp.where(low_end, -two[f], one[f])
+        for g in range(groups):
+            c_ref[f, g] = jnp.zeros((2 * PAD, width), jnp.float32)
+            c_ref[f, g, 0:1] = a_ref[f, 0, g : g + 1]
+            c_ref[f, g, 1:2] = a_ref[f, 1, g : g + 1]
+            c_ref[f, g, 2 * PAD - 2 : 2 * PAD - 1] = a_ref[f, 1, groups + g : groups + g + 1]
+            c_ref[f, g, 2 * PAD - 1 : 2 * PAD] = a_ref[f, 0, groups + g : groups + g + 1]
+
+    size = rows // groups
+    for g in range(groups):
+        at = slice(g * size, (g + 1) * size)
+        for f in range(FIELDS):
+            head = dy_ref[f, g, PAD : 2 * PAD] + c_ref[f, g, 0:PAD]
+            tail = dy_ref[f, g, width : PAD + width] + c_ref[f, g, PAD : 2 * PAD]
+            strip = jnp.concatenate([head, dy_ref[f, g, 2 * PAD : width], tail], axis=0)
+            out_ref[f, at] = v_ref[f, at] - strip.T.reshape(size, high, width)
 
     ghost = sheared_rows(flags, weights, near_ref, next_ref)
     ghost_low = [[jnp.where(first, ghost[k][f], xl_ref[f, k]) for f in range(FIELDS)] for k in range(2)]
     cells = ghost_low + [load_row(w_ref, i) for i in range(3)]
-    sides = [x_states(cells[k : k + 3]) for k in range(3)]
+    sides = [three_states(cells[k : k + 3]) for k in range(3)]
     outer = face(sides[0][0], sides[1][1], 0)
-    inner_face = face(sides[1][0], sides[2][1], 0)
-    for f in range(FIELDS):
-        v_ref[f, 0] = v_ref[f, 0] - coef * (inner_face[f] - outer[f])
-        v_ref[f, 1] = v_ref[f, 1] + coef * inner_face[f]
+    inner = face(sides[1][0], sides[2][1], 0)
+    for f in range(FIELDS):
+        out_ref[f, 0] = out_ref[f, 0] - coef * (inner[f] - outer[f])
+        out_ref[f, 1] = out_ref[f, 1] + coef * inner[f]
     ghost_high = [[jnp.where(last, ghost[k][f], xr_ref[f, k]) for f in range(FIELDS)] for k in range(2)]
     cells = [load_row(w_ref, rows - 3 + i) for i in range(3)] + ghost_high
-    sides = [x_states(cells[k : k + 3]) for k in range(3)]
-    inner_face = face(sides[0][0], sides[1][1], 0)
+    sides = [three_states(cells[k : k + 3]) for k in range(3)]
+    inner = face(sides[0][0], sides[1][1], 0)
     outer = face(sides[1][0], sides[2][1], 0)
     for f in range(FIELDS):
-        v_ref[f, rows - 2] = v_ref[f, rows - 2] - coef * inner_face[f]
-        v_ref[f, rows - 1] = v_ref[f, rows - 1] - coef * (outer[f] - inner_face[f])
-
-    edge = jnp.logical_or(lane < 2, lane >= width - 2)
-    per_tile = width // 8
-    for f in range(FIELDS):
-        for i in range(rows):
-            move = shifted(d_ref[f, i // per_tile], -4 - 8 * (i % per_tile), 1)
-            out_ref[f, i] = v_ref[f, i] - jnp.where(edge, move, 0.0)
-    if not second:
-
-        def body(i, carry):
-            prim = to_primitive(load_row(out_ref, i))
-            for f in range(FIELDS):
-                w1_ref[f, i] = prim[f]
-            return carry
-
-        lax.fori_loop(0, rows, body, 0, unroll=4)
-        send_edges(flags, w1_ref, *sends[:4], sends[4:])
+        out_ref[f, rows - 2] = out_ref[f, rows - 2] - coef * inner[f]
+        out_ref[f, rows - 1] = out_ref[f, rows - 1] - coef * (outer[f] - inner[f])
+    if second:
+        return
+
+    def body(i, carry):
+        prim = to_primitive(load_row(out_ref, i))
+        for f in range(FIELDS):
+            w1_ref[f, i] = prim[f]
+        return carry
+
+    lax.fori_loop(0, rows, body, 0, unroll=4)
+    for g in range(groups):
+        for f in range(FIELDS):
+            turn(w1_ref, f, g, wt1_ref)
+    send_columns(wt1_ref, last_ref, first_ref)
+    send_rows(flags, w1_ref, *sends)
 
 
 def call(kernel, name, scalars, arrays, shapes, scratch=(), in_hbm=False):
@@ -366,7 +395,7 @@
         in_specs=[smem] * len(scalars) + [pl.BlockSpec(memory_space=pltpu.HBM) if in_hbm else vmem] * len(arrays),
         out_specs=[vmem] * len(shapes),
         scratch_shapes=[pltpu.VMEM(s, jnp.float32) if isinstance(s, tuple) else s for s in scratch],
-        compiler_params=pltpu.CompilerParams(vmem_limit_bytes=16 * 1024 * 1024),
+        compiler_params=pltpu.CompilerParams(vmem_limit_bytes=20 * 1024 * 1024),
     )(*scalars, *arrays)
 
 
@@ -392,19 +421,23 @@
     return lax.ppermute(shear, ("gx", "gy"), pairs)
 
 
-def inner_part(second, block, radial0, shear, *states):
-    full = states[0].shape
+def inner_scratch(full):
     high, width = full[2:]
     tile = (FIELDS, high, width)
-    padded = (FIELDS, high + 16, width)
-    scratch = [padded, padded, padded, tile, tile, tile]
+    padded = (FIELDS, high + 2 * PAD, width)
+    return [padded, padded, padded, tile, tile, tile]
+
+
+def inner_part(second, block, radial0, shear, *states):
+    full, turned = states[0].shape, states[1].shape
 
     def branch(by):
         def run(radial0, shear, *states):
             near, following = crossing(by, shear), crossing(by + 1, shear)
             kernel = functools.partial(interior_kernel, second)
-            (v,) = call(kernel, "inner_2" if second else "inner_1", [radial0], list(states), [full], scratch)
-            return v, near, following
+            name = "inner_2" if second else "inner_1"
+            v, dy = call(kernel, name, [radial0], list(states), [full, turned], inner_scratch(full))
+            return v, dy, near, following
 
         return run
 
@@ -412,29 +445,30 @@
     return lax.switch(block, branches, radial0, shear, *states)
 
 
-def sections(block, flags, weights, radial0, w0, pack, last, first, shear, *swap):
-    full = w0.shape
-    moves = [pack.shape]
-    sends = [x.shape for x in (pack, last, first, shear, *swap)]
+def sections(block, flags, weights, radial0, w0, wt0, last, first, shear, *swap):
+    full, turned = w0.shape, wt0.shape
+    groups, width = turned[1], full[3]
+    scratch = [(FIELDS, 5, 2 * groups, width), (FIELDS, 2, 2 * groups, width), (FIELDS, groups, 2 * PAD, width)]
+    sends = [x.shape for x in (last, first, shear, *swap)]
     got = exchange(last, first, swap)
-    v, *sheared = inner_part(False, block, radial0, shear, w0)
-    w1, u1, pack1, last1, first1, shear1, *swap1 = call(
+    v, dy, *sheared = inner_part(False, block, radial0, shear, w0, wt0)
+    w1, wt1, u1, last, first, shear, *swap = call(
         functools.partial(edge_kernel, False),
         "edge_1",
         [flags, weights],
-        [v, w0, pack, *got, *sheared],
-        [full, full] + sends,
-        moves,
+        [v, dy, w0, wt0, *got, *sheared],
+        [full, turned, full] + sends,
+        scratch,
     )
-    got = exchange(last1, first1, swap1)
-    v, *sheared = inner_part(True, block, radial0, shear1, w1, w0, u1)
+    got = exchange(last, first, swap)
+    v, dy, *sheared = inner_part(True, block, radial0, shear, w1, wt1, w0, u1)
     (out,) = call(
         functools.partial(edge_kernel, True),
         "edge_2",
         [flags, weights],
-        [v, w1, pack1, *got, *sheared],
+        [v, dy, w1, wt1, *got, *sheared],
         [full],
-        moves,
+        scratch,
     )
     return out
 
@@ -462,16 +496,17 @@
     )
     full = (FIELDS, rows, high, width)
     slab = (FIELDS, 2, high, width)
-    packed = (FIELDS, 8 * rows // width, high, width)
-    tile = (FIELDS, high, width)
-    sends = [packed, tile, tile, slab] + [slab] * (1 if count_x == 2 else 2)
+    groups = rows * high // width
+    turned = (FIELDS, groups, width + 2 * PAD, width)
+    ends = (FIELDS, 2 * groups, width)
+    sends = [ends, ends, slab] + [slab] * (1 if count_x == 2 else 2)
     start_state = call(
         prepare_kernel,
         "prepare",
         [flags, radial0],
         [density, velocity, bfield, pressure],
-        [full] + sends,
-        [pltpu.SemaphoreType.DMA((4, 2))],
+        [full, turned] + sends,
+        [pltpu.SemaphoreType.DMA((4, groups))],
         in_hbm=True,
     )
     return sections(block, flags, weights, radial0, *start_state)

time: 63 us -> 60.9 us (0.967)
  local copies, waits for them, and re-layouts: 5.38 us -> 4.17 us
  starting transfers between devices: 15.6 us -> 14.9 us
    unnamed x10 -> x8, local copies, waits for them, and re-layouts: 5.38 us -> 4.17 us
  transfers between devices with their start and end apart: 10 -> 10, of which waited for: 0 -> 0; matrix products, arithmetic and copies ran while one was open for 0% -> 0% of each run, Pallas kernels for 42% -> 39%
where the time goes in v1:
time: 60.9 us; the launch traced here: 60.3 us
  Pallas kernels  39.3 us (65%)
  starting transfers between devices  14.9 us (24%)
  local copies, waits for them, and re-layouts  4.17 us (7%)
  between operations  1.42 us (2%)
    pallas_call x5, Pallas kernels, call(): pl.pallas_call(kernel, name=name, out_shape=[jax.ShapeDtypeStruct(s, jnp....  39.3 us
    ppermute x2, starting transfers between devices, exchange(): lax.ppermute(first, 'gy', [((i + 1) % count_y, i) for i in range(count_y)])  7.62 us
    unnamed x8, local copies, waits for them, and re-layouts  4.17 us
    ppermute x2, starting transfers between devices, exchange(): lax.ppermute(last, 'gy', [(i, (i + 1) % count_y) for i in range(count_y)])  4.09 us
    ppermute x4, starting transfers between devices, crossing(): return lax.ppermute(shear, ('gx', 'gy'), pairs)  3.08 us
  transfers between devices with their start and end apart: 10, of which 0 were waited for; matrix products, arithmetic and copies ran while one was open for 0% of the time, Pallas kernels for 39%

profile of v1, /device:TPU:1, one launch (start us, length us, event | category | flops | bytes accessed | tf_op | source)
XLA Modules:
  0.0 60.3 jit_solution(3836501354289157133)
XLA Ops:
  0.7 0.1 pad_maximum_fusion.1.radial0
  0.8 0.1 pad_add_fusion.flags
  0.8 0.0 copy-start
  0.8 1.1 %copy-done = f32[3,32,16,128]{3,2,1,0:T(8,128)S(1)} copy-done((f32[3,32,16,128]{3,2,1,0:T(8,128)S(1)}, f32[3,32,16,128]{3,2,1,0:T(8,128)}, u32[]{:S(2)}) %copy-start) | copy-done | bytes 786456
  2.0 0.0 copy-start.1
  2.0 1.1 %copy-done.1 = f32[3,32,16,128]{3,2,1,0:T(8,128)S(1)} copy-done((f32[3,32,16,128]{3,2,1,0:T(8,128)S(1)}, f32[3,32,16,128]{3,2,1,0:T(8,128)}, u32[]{:S(2)}) %copy-start.1) | copy-done | bytes 786456
  3.1 0.0 copy-start.2
  3.1 0.9 %copy-done.2 = f32[32,16,128]{2,1,0:T(8,128)S(1)} copy-done((f32[32,16,128]{2,1,0:T(8,128)S(1)}, f32[32,16,128]{2,1,0:T(8,128)}, u32[]{:S(2)}) %copy-start.2) | copy-done | bytes 262168
  4.1 0.0 copy-start.3
  4.1 0.9 %copy-done.3 = f32[32,16,128]{2,1,0:T(8,128)S(1)} copy-done((f32[32,16,128]{2,1,0:T(8,128)S(1)}, f32[32,16,128]{2,1,0:T(8,128)}, u32[]{:S(2)}) %copy-start.3) | copy-done | bytes 262168
  5.0 4.3 %prepare.1 = (f32[8,32,16,128]{3,2,1,0:T(8,128)S(1)}, f32[8,4,144,128]{3,2,1,0:T(8,128)}, f32[8,8,128]{2,1,0:T(8,128)S(1)}, f32[8,8,128]{2,1,0:T(8,128)S(1)}, f3...) custom-call(s32[3]{0:T(128)S(1)} %pad_add_fusion.flags, f32[2]{0:T(128)S(1)} %pad_maximum_fusion.1.radial0, ...), custom_call_target="tpu_custom_call" | custom-call | tf_op jit(solution)/shard_map/prepare/pallas_call | solution.py:391
  9.3 0.1 collective-permute-start.66
  9.4 2.7 %collective-permute-start.64 = (f32[8,8,128]{2,1,0:T(8,128)S(1)}, f32[8,8,128]{2,1,0:T(8,128)S(1)}, u32[]{:S(2)}, u32[]{:S(2)}) collective-permute-start(f32[8,8,128]{2,1,0:T(8,128)S(1)} %get-tuple-element.575), channel_id=1, source_target_pairs={{0,1},{1,2},{2,3},{3,4},{4,5},{5,6},{6,7},{7,8},{8,9},{9,10},{10,1... | collective-permute-start | bytes 98312 | tf_op jit(solution)/shard_map/ppermute | solution.py:404
  12.1 4.0 %collective-permute-start.65 = (f32[8,8,128]{2,1,0:T(8,128)S(1)}, f32[8,8,128]{2,1,0:T(8,128)S(1)}, u32[]{:S(2)}, u32[]{:S(2)}) collective-permute-start(f32[8,8,128]{2,1,0:T(8,128)S(1)} %get-tuple-element.576), channel_id=1, source_target_pairs={{1,0},{2,1},{3,2},{4,3},{5,4},{6,5},{7,6},{8,7},{9,8},{10,9},{11,1... | collective-permute-start | bytes 98312 | tf_op jit(solution)/shard_map/ppermute | solution.py:405
  16.7 0.1 pad_maximum_fusion.weights
  16.8 14.6 %conditional.2 = (f32[8,32,16,128]{3,2,1,0:T(8,128)}, f32[8,4,144,128]{3,2,1,0:T(8,128)}, f32[8,2,16,128]{3,2,1,0:T(8,128)}, f32[8,2,16,128]{3,2,1,0:T(8,128)}) conditional(s32[]{:T(128)} %clamp.4, (f32[2]{0:T(128)S(1)}, f32[8,32,16,128]{3,2,1,0:T(8,128)S(1)}, f32[8,4,144,128]{3,2,1,0:T(8,128)}, ...), branch_computations={%region_0.1_spmd, %region_1.2_spmd, %region_2.3_spmd, %region_3.4_... | conditional | bytes 1048688 | solution.py:445
  16.8 0.1 collective-permute-start.7
  16.9 2.0 %collective-permute-start.6 = (f32[8,2,16,128]{3,2,1,0:T(8,128)S(1)}, f32[8,2,16,128]{3,2,1,0:T(8,128)}, u32[]{:S(2)}, u32[]{:S(2)}) collective-permute-start(f32[8,2,16,128]{3,2,1,0:T(8,128)S(1)} %get-tuple-element.348), channel_id=1, source_target_pairs={{16,3},{0,29},{17,4},{1,30},{18,5},{2,31},{19,6},{3,16},{20,7},{4,... | collective-permute-start | bytes 393224 | tf_op jit(solution)/shard_map/cond/branch_3_fun/ppermute | solution.py:421
  18.9 12.5 %inner_1.19 = (f32[8,32,16,128]{3,2,1,0:T(8,128)}, f32[8,4,144,128]{3,2,1,0:T(8,128)}) custom-call(f32[2]{0:T(128)S(1)} %get-tuple-element.343.radial0, f32[8,32,16,128]{3,2,1,0:T(8,128)S(1)} %get-tuple-element.344.w_ref, f32[8,4,144,128]{3,2,1,0:T(8,128)} %get-tuple-element.345.wt_ref), custom_call_target="tpu_custom_call" | custom-call | tf_op jit(solution)/shard_map/cond/branch_3_fun/inner_1/pallas_call | solution.py:391
  31.4 0.0 collective-permute-done.7
  31.4 0.0 collective-permute-done.6
  31.4 0.0 collective-permute-done.64.low_ref
  31.4 0.0 collective-permute-done.65.high_ref
  31.4 0.0 collective-permute-done.66.xl_ref.xr_ref
  31.4 6.7 %edge_1.1 = (f32[8,32,16,128]{3,2,1,0:T(8,128)}, f32[8,4,144,128]{3,2,1,0:T(8,128)}, f32[8,32,16,128]{3,2,1,0:T(8,128)S(1)}, f32[8,8,128]{2,1,0:T(8,128)S(1)}, f...) custom-call(s32[3]{0:T(128)S(1)} %pad_add_fusion.flags, ...), custom_call_target="tpu_custom_call" | custom-call | tf_op jit(solution)/shard_map/edge_1/pallas_call | solution.py:391
  38.1 0.0 collective-permute-start.69
  38.1 1.4 %collective-permute-start.67 = (f32[8,8,128]{2,1,0:T(8,128)S(1)}, f32[8,8,128]{2,1,0:T(8,128)S(1)}, u32[]{:S(2)}, u32[]{:S(2)}) collective-permute-start(f32[8,8,128]{2,1,0:T(8,128)S(1)} %get-tuple-element.586), channel_id=1, source_target_pairs={{0,1},{1,2},{2,3},{3,4},{4,5},{5,6},{6,7},{7,8},{8,9},{9,10},{10,1... | collective-permute-start | bytes 98312 | tf_op jit(solution)/shard_map/ppermute | solution.py:404
  39.5 3.6 %collective-permute-start.68 = (f32[8,8,128]{2,1,0:T(8,128)S(1)}, f32[8,8,128]{2,1,0:T(8,128)S(1)}, u32[]{:S(2)}, u32[]{:S(2)}) collective-permute-start(f32[8,8,128]{2,1,0:T(8,128)S(1)} %get-tuple-element.587), channel_id=1, source_target_pairs={{1,0},{2,1},{3,2},{4,3},{5,4},{6,5},{7,6},{8,7},{9,8},{10,9},{11,1... | collective-permute-start | bytes 98312 | tf_op jit(solution)/shard_map/ppermute | solution.py:405
  43.2 12.3 %conditional.3 = (f32[8,32,16,128]{3,2,1,0:T(8,128)S(1)}, f32[8,4,144,128]{3,2,1,0:T(8,128)S(1)}, f32[8,2,16,128]{3,2,1,0:T(8,128)}, f32[8,2,16,128]{3,2,1,0:T(8,128)}) conditional(s32[]{:T(128)} %clamp.4, (f32[2]{0:T(128)S(1)}, f32[8,32,16,128]{3,2,1,0:T(8,128)}, f32[8,4,144,128]{3,2,1,0:T(8,128)}, ...), branch_computations={%region_16.17_spmd, %region_17.18_spmd, %region_18.19_spmd, %regio... | conditional | bytes 1048688 | solution.py:445
  43.2 0.0 collective-permute-start.39
  43.2 1.0 %collective-permute-start.38 = (f32[8,2,16,128]{3,2,1,0:T(8,128)S(1)}, f32[8,2,16,128]{3,2,1,0:T(8,128)}, u32[]{:S(2)}, u32[]{:S(2)}) collective-permute-start(f32[8,2,16,128]{3,2,1,0:T(8,128)S(1)} %get-tuple-element.452), channel_id=1, source_target_pairs={{16,3},{0,29},{17,4},{1,30},{18,5},{2,31},{19,6},{3,16},{20,7},{4,... | collective-permute-start | bytes 393224 | tf_op jit(solution)/shard_map/cond/branch_3_fun/ppermute | solution.py:421
  44.2 11.1 %inner_2.19 = (f32[8,32,16,128]{3,2,1,0:T(8,128)S(1)}, f32[8,4,144,128]{3,2,1,0:T(8,128)S(1)}) custom-call(f32[2]{0:T(128)S(1)} %get-tuple-element.445.radial0, f32[8,32,16,128]{3,2,1,0:T(8,128)} %get-tuple-element.446.w_ref, f32[8,4,144,128]{3,2,1,0:T(8,128)} %get-tuple-element.447.wt_ref, f32[8,32,16,128]{3,2,1,0:T(8,128)S(1)} %get-tuple-element.448.refs_0_, ...), custom_call_target="tpu_custom_call" | custom-call | tf_op jit(solution)/shard_map/cond/branch_3_fun/inner_2/pallas_call | solution.py:391
  55.2 0.0 collective-permute-done.39
  55.2 0.0 collective-permute-done.38
  55.5 0.0 collective-permute-done.67.low_ref
  55.5 0.0 collective-permute-done.68.high_ref
  55.5 0.0 collective-permute-done.69.xl_ref.xr_ref
  55.5 4.8 %edge_2.1 = f32[8,32,16,128]{3,2,1,0:T(8,128)} custom-call(s32[3]{0:T(128)S(1)} %pad_add_fusion.flags, f32[3]{0:T(128)S(1)} %pad_maximum_fusion.weights, f32[8,32,16,128]{3,2,1,0:T(8,128)S(1)} %get-tuple-element.584.v_ref, f32[8,4,144,128]{3,2,1,0:T(8,128)S(1)} %get-tuple-element.585.dy_ref, f32[8,32,16,128]{3,2,1,0:T(8,128)} %get-tuple-element.580.w_ref, ...), custom_call_target="tpu_custom_call" | custom-call | tf_op jit(solution)/shard_map/edge_2/pallas_call | solution.py:391
Async XLA Ops:
  0.8 1.1 %copy-start = (f32[3,32,16,128]{3,2,1,0:T(8,128)S(1)}, f32[3,32,16,128]{3,2,1,0:T(8,128)}, u32[]{:S(2)}) copy-start(f32[3,32,16,128]{3,2,1,0:T(8,128)} %vel_hbm.1) | copy-start | bytes 2359300
  2.0 1.1 %copy-start.1 = (f32[3,32,16,128]{3,2,1,0:T(8,128)S(1)}, f32[3,32,16,128]{3,2,1,0:T(8,128)}, u32[]{:S(2)}) copy-start(f32[3,32,16,128]{3,2,1,0:T(8,128)} %mag_hbm.1) | copy-start | bytes 2359300
  3.1 0.9 %copy-start.2 = (f32[32,16,128]{2,1,0:T(8,128)S(1)}, f32[32,16,128]{2,1,0:T(8,128)}, u32[]{:S(2)}) copy-start(f32[32,16,128]{2,1,0:T(8,128)} %rho_hbm.1) | copy-start | bytes 786436
  4.1 0.9 %copy-start.3 = (f32[32,16,128]{2,1,0:T(8,128)S(1)}, f32[32,16,128]{2,1,0:T(8,128)}, u32[]{:S(2)}) copy-start(f32[32,16,128]{2,1,0:T(8,128)} %pres_hbm.1) | copy-start | bytes 786436
  9.3 22.1 %collective-permute-start.66 = (f32[8,2,16,128]{3,2,1,0:T(8,128)S(1)}, f32[8,2,16,128]{3,2,1,0:T(8,128)S(1)}, u32[]{:S(2)}, u32[]{:S(2)}) collective-permute-start(f32[8,2,16,128]{3,2,1,0:T(8,128)S(1)} %get-tuple-element.577), channel_id=1, source_target_pairs={{0,16},{16,0},{1,17},{17,1},{2,18},{18,2},{3,19},{19,3},{4,20},{20... | collective-permute-start | bytes 393224 | tf_op jit(solution)/shard_map/ppermute | solution.py:407
  9.4 22.0 %collective-permute-start.64 = (f32[8,8,128]{2,1,0:T(8,128)S(1)}, f32[8,8,128]{2,1,0:T(8,128)S(1)}, u32[]{:S(2)}, u32[]{:S(2)}) collective-permute-start(f32[8,8,128]{2,1,0:T(8,128)S(1)} %get-tuple-element.575), channel_id=1, source_target_pairs={{0,1},{1,2},{2,3},{3,4},{4,5},{5,6},{6,7},{7,8},{8,9},{9,10},{10,1... | collective-permute-start | bytes 98312 | tf_op jit(solution)/shard_map/ppermute | solution.py:404
  12.1 19.3 %collective-permute-start.65 = (f32[8,8,128]{2,1,0:T(8,128)S(1)}, f32[8,8,128]{2,1,0:T(8,128)S(1)}, u32[]{:S(2)}, u32[]{:S(2)}) collective-permute-start(f32[8,8,128]{2,1,0:T(8,128)S(1)} %get-tuple-element.576), channel_id=1, source_target_pairs={{1,0},{2,1},{3,2},{4,3},{5,4},{6,5},{7,6},{8,7},{9,8},{10,9},{11,1... | collective-permute-start | bytes 98312 | tf_op jit(solution)/shard_map/ppermute | solution.py:405
  16.8 14.6 %collective-permute-start.7 = (f32[8,2,16,128]{3,2,1,0:T(8,128)S(1)}, f32[8,2,16,128]{3,2,1,0:T(8,128)}, u32[]{:S(2)}, u32[]{:S(2)}) collective-permute-start(f32[8,2,16,128]{3,2,1,0:T(8,128)S(1)} %get-tuple-element.348), channel_id=1, source_target_pairs={{16,4},{0,28},{17,5},{1,29},{18,6},{2,30},{19,7},{3,31},{20,8},{4,... | collective-permute-start | bytes 393224 | tf_op jit(solution)/shard_map/cond/branch_3_fun/ppermute | solution.py:421
  16.9 14.5 %collective-permute-start.6 = (f32[8,2,16,128]{3,2,1,0:T(8,128)S(1)}, f32[8,2,16,128]{3,2,1,0:T(8,128)}, u32[]{:S(2)}, u32[]{:S(2)}) collective-permute-start(f32[8,2,16,128]{3,2,1,0:T(8,128)S(1)} %get-tuple-element.348), channel_id=1, source_target_pairs={{16,3},{0,29},{17,4},{1,30},{18,5},{2,31},{19,6},{3,16},{20,7},{4,... | collective-permute-start | bytes 393224 | tf_op jit(solution)/shard_map/cond/branch_3_fun/ppermute | solution.py:421
  38.1 17.4 %collective-permute-start.69 = (f32[8,2,16,128]{3,2,1,0:T(8,128)S(1)}, f32[8,2,16,128]{3,2,1,0:T(8,128)S(1)}, u32[]{:S(2)}, u32[]{:S(2)}) collective-permute-start(f32[8,2,16,128]{3,2,1,0:T(8,128)S(1)} %get-tuple-element.588), channel_id=1, source_target_pairs={{0,16},{16,0},{1,17},{17,1},{2,18},{18,2},{3,19},{19,3},{4,20},{20... | collective-permute-start | bytes 393224 | tf_op jit(solution)/shard_map/ppermute | solution.py:407
  38.1 17.3 %collective-permute-start.67 = (f32[8,8,128]{2,1,0:T(8,128)S(1)}, f32[8,8,128]{2,1,0:T(8,128)S(1)}, u32[]{:S(2)}, u32[]{:S(2)}) collective-permute-start(f32[8,8,128]{2,1,0:T(8,128)S(1)} %get-tuple-element.586), channel_id=1, source_target_pairs={{0,1},{1,2},{2,3},{3,4},{4,5},{5,6},{6,7},{7,8},{8,9},{9,10},{10,1... | collective-permute-start | bytes 98312 | tf_op jit(solution)/shard_map/ppermute | solution.py:404
  39.5 15.9 %collective-permute-start.68 = (f32[8,8,128]{2,1,0:T(8,128)S(1)}, f32[8,8,128]{2,1,0:T(8,128)S(1)}, u32[]{:S(2)}, u32[]{:S(2)}) collective-permute-start(f32[8,8,128]{2,1,0:T(8,128)S(1)} %get-tuple-element.587), channel_id=1, source_target_pairs={{1,0},{2,1},{3,2},{4,3},{5,4},{6,5},{7,6},{8,7},{9,8},{10,9},{11,1... | collective-permute-start | bytes 98312 | tf_op jit(solution)/shard_map/ppermute | solution.py:405
  43.2 12.1 %collective-permute-start.39 = (f32[8,2,16,128]{3,2,1,0:T(8,128)S(1)}, f32[8,2,16,128]{3,2,1,0:T(8,128)}, u32[]{:S(2)}, u32[]{:S(2)}) collective-permute-start(f32[8,2,16,128]{3,2,1,0:T(8,128)S(1)} %get-tuple-element.452), channel_id=1, source_target_pairs={{16,4},{0,28},{17,5},{1,29},{18,6},{2,30},{19,7},{3,31},{20,8},{4,... | collective-permute-start | bytes 393224 | tf_op jit(solution)/shard_map/cond/branch_3_fun/ppermute | solution.py:421
  43.2 12.1 %collective-permute-start.38 = (f32[8,2,16,128]{3,2,1,0:T(8,128)S(1)}, f32[8,2,16,128]{3,2,1,0:T(8,128)}, u32[]{:S(2)}, u32[]{:S(2)}) collective-permute-start(f32[8,2,16,128]{3,2,1,0:T(8,128)S(1)} %get-tuple-element.452), channel_id=1, source_target_pairs={{16,3},{0,29},{17,4},{1,30},{18,5},{2,31},{19,6},{3,16},{20,7},{4,... | collective-permute-start | bytes 393224 | tf_op jit(solution)/shard_map/cond/branch_3_fun/ppermute | solution.py:421

commit v2 on v1

--- a/solution.py
+++ b/solution.py
@@ -95,24 +95,37 @@
 def turn(w_ref, f, g, wt_ref):
     high, width = w_ref.shape[2:]
     size = width // high
-    tile = w_ref[f, g * size : (g + 1) * size].reshape(width, width)
+    tile = w_ref[f, pl.ds(g * size, size)].reshape(width, width)
     wt_ref[f, g, PAD : PAD + width] = tile.T
 
 
-def send_columns(wt_ref, last_ref, first_ref):
+def send_columns(wt_ref, cols_ref, last_ref, first_ref):
     groups, rows = wt_ref.shape[1:3]
-    for f in range(FIELDS):
-        for k in range(2):
+    cells = [PAD, PAD + 1, PAD + 2, rows - PAD - 3, rows - PAD - 2, rows - PAD - 1]
+
+    def body(f, carry):
+        for k, cell in enumerate(cells):
             for g in range(groups):
-                to = slice(k * groups + g, k * groups + g + 1)
-                first_ref[f, to] = wt_ref[f, g, PAD + k : PAD + k + 1]
-                last_ref[f, to] = wt_ref[f, g, rows - PAD - 2 + k : rows - PAD - 1 + k]
-
-
-def send_rows(flags, w_ref, shear_ref, *swap_refs):
+                cols_ref[f, k * groups + g : k * groups + g + 1] = wt_ref[f, g, cell : cell + 1]
+        first_ref[f] = cols_ref[f, 0 : 2 * groups]
+        last_ref[f] = cols_ref[f, 4 * groups : 6 * groups]
+        return carry
+
+    lax.fori_loop(0, FIELDS, body, 0)
+
+
+def send_rows(flags, w_ref, rows_ref, shear_ref, *swap_refs):
     rows = w_ref.shape[1]
     first = flags[0] == 1
-    for k in range(2):
+
+    def copy(f, carry):
+        rows_ref[f, 0:3] = w_ref[f, 0:3]
+        rows_ref[f, 3:6] = w_ref[f, rows - 3 : rows]
+        return carry
+
+    lax.fori_loop(0, FIELDS, copy, 0)
+
+    def body(k, carry):
         low, high = load_row(w_ref, k), load_row(w_ref, rows - 2 + k)
         if len(swap_refs) == 1:
             for f in range(FIELDS):
@@ -124,9 +137,12 @@
         outer = to_conserved([jnp.where(first, low[f], high[f]) for f in range(FIELDS)])
         for f in range(FIELDS):
             shear_ref[f, k] = outer[f]
-
-
-def prepare_kernel(flags, radial0, rho_hbm, vel_hbm, mag_hbm, pres_hbm, w_ref, wt_ref, last_ref, first_ref, *rest):
+        return carry
+
+    lax.fori_loop(0, 2, body, 0)
+
+
+def prepare_kernel(flags, radial0, rho_hbm, vel_hbm, mag_hbm, pres_hbm, w_ref, wt_ref, cols_ref, last_ref, first_ref, *rest):
     *sends, sems = rest
     rows = w_ref.shape[1]
     parts = sems.shape[1]
@@ -149,9 +165,14 @@
             copy.wait()
         for i in range(part * size, (part + 1) * size):
             w_ref[2, i] = w_ref[2, i] - radial0[1] * (radial0[0] + float(i))
-        for f in range(FIELDS):
-            turn(w_ref, f, part, wt_ref)
-    send_columns(wt_ref, last_ref, first_ref)
+
+        def turn_fields(n, carry, part=part):
+            for f in range(4):
+                turn(w_ref, 4 * n + f, part, wt_ref)
+            return carry
+
+        lax.fori_loop(0, FIELDS // 4, turn_fields, 0)
+    send_columns(wt_ref, cols_ref, last_ref, first_ref)
     send_rows(flags, w_ref, *sends)
 
 
@@ -275,58 +296,58 @@
             dy_ref[f, g, PAD + width - 1 : PAD + width] = jnp.zeros((1, width), jnp.float32)
 
 
-def sheared_rows(flags, weights, near_ref, next_ref):
+def sheared_rows(flags, weights, near_ref, next_ref, ghost_ref):
     first = flags[0] == 1
     high, width = near_ref.shape[2:]
     start = flags[2]
+    back = lax.rem(width - start, width)
     lane = lanes_of((high, width))
 
-    def taken(one, two, at):
-        back = lax.rem(2 * width - at, width)
-        return jnp.where(lane < width - at, pltpu.roll(one, back, 1), pltpu.roll(two, back, 1))
-
-    rows = []
-    for k in range(2):
+    def body(k, carry):
         ghost = []
         for f in range(FIELDS):
             near, following = near_ref[f, k], next_ref[f, k]
             one = jnp.where(first, following, near)
             two = jnp.where(first, near, following)
-            ghost.append(weights[0] * taken(one, two, start + 1) + weights[1] * taken(one, two, start))
+            one_up, two_up = pltpu.roll(one, width - 1, 1), pltpu.roll(two, width - 1, 1)
+            one = weights[0] * jnp.where(lane < width - 1, one_up, two_up) + weights[1] * one
+            two = weights[0] * two_up + weights[1] * two
+            ghost.append(jnp.where(lane < width - start, pltpu.roll(one, back, 1), pltpu.roll(two, back, 1)))
         delta = weights[2]
         boosted = list(ghost)
         boosted[2] = ghost[2] + ghost[0] * delta
         boosted[7] = ghost[7] + ghost[2] * delta + 0.5 * ghost[0] * delta * delta
-        rows.append(to_primitive(boosted))
-    return rows
-
-
-def edge_kernel(second, flags, weights, v_ref, dy_ref, w_ref, wt_ref, low_ref, high_ref, xl_ref, xr_ref, near_ref, next_ref, *refs):
-    rows, high, width = w_ref.shape[1:]
-    groups = wt_ref.shape[1]
+        prim = to_primitive(boosted)
+        for f in range(FIELDS):
+            ghost_ref[f, k] = prim[f]
+        return carry
+
+    lax.fori_loop(0, 2, body, 0)
+
+
+def edge_kernel(second, beside, flags, weights, v_ref, dy_ref, rows_ref, cols_ref, low_ref, high_ref, near_ref, next_ref, *refs):
+    beside, refs = refs[:beside], refs[beside:]
+    xl_ref, xr_ref = beside[0], beside[-1]
+    rows, high, width = v_ref.shape[1:]
+    groups = dy_ref.shape[1]
+    size = rows // groups
     step = 0.5 * TIME_STEP if second else TIME_STEP
     coef = 0.5 * step
     if second:
-        out_ref, e_ref, a_ref, c_ref = refs
+        out_hbm, e_ref, a_ref, c_ref, x_ref, ghost_ref, out_ref, sems = refs
     else:
-        w1_ref, wt1_ref, out_ref, last_ref, first_ref, *sends, e_ref, a_ref, c_ref = refs
+        w1_ref, wt1_ref, out_ref, cols1_ref, last_ref, first_ref, *sends, e_ref, a_ref, c_ref, x_ref, ghost_ref = refs
     first, last = flags[0] == 1, flags[1] == 1
 
-    for f in range(FIELDS):
+    def gather(f, carry):
         for k in range(5):
-            cell = k - 2
-            if cell < 0:
-                e_ref[f, k, 0:groups] = low_ref[f, k * groups : (k + 1) * groups]
-            else:
-                for g in range(groups):
-                    e_ref[f, k, g : g + 1] = wt_ref[f, g, PAD + cell : PAD + cell + 1]
-            cell = width - 3 + k
-            if cell >= width:
-                at = (cell - width) * groups
-                e_ref[f, k, groups : 2 * groups] = high_ref[f, at : at + groups]
-            else:
-                for g in range(groups):
-                    e_ref[f, k, groups + g : groups + g + 1] = wt_ref[f, g, PAD + cell : PAD + cell + 1]
+            at = slice(k % 2 * groups, k % 2 * groups + groups) if k < 2 else slice((k - 2) * groups, (k - 1) * groups)
+            e_ref[f, k, 0:groups] = low_ref[f, at] if k < 2 else cols_ref[f, at]
+            at = slice((k + 3) * groups, (k + 4) * groups) if k < 3 else slice((k - 3) * groups, (k - 2) * groups)
+            e_ref[f, k, groups : 2 * groups] = cols_ref[f, at] if k < 3 else high_ref[f, at]
+        return carry
+
+    lax.fori_loop(0, FIELDS, gather, 0)
     cells = [[e_ref[f, k] for f in range(FIELDS)] for k in range(5)]
     sides = [three_states(cells[k : k + 3]) for k in range(3)]
     one = face(sides[0][0], sides[1][1], 1)
@@ -335,65 +356,107 @@
     for f in range(FIELDS):
         a_ref[f, 0] = coef * (two[f] - one[f])
         a_ref[f, 1] = coef * jnp.where(low_end, -two[f], one[f])
+
+    def scatter(f, carry):
         for g in range(groups):
             c_ref[f, g] = jnp.zeros((2 * PAD, width), jnp.float32)
             c_ref[f, g, 0:1] = a_ref[f, 0, g : g + 1]
             c_ref[f, g, 1:2] = a_ref[f, 1, g : g + 1]
             c_ref[f, g, 2 * PAD - 2 : 2 * PAD - 1] = a_ref[f, 1, groups + g : groups + g + 1]
             c_ref[f, g, 2 * PAD - 1 : 2 * PAD] = a_ref[f, 0, groups + g : groups + g + 1]
-
-    size = rows // groups
-    for g in range(groups):
-        at = slice(g * size, (g + 1) * size)
-        for f in range(FIELDS):
+        return carry
+
+    lax.fori_loop(0, FIELDS, scatter, 0)
+
+    sheared_rows(flags, weights, near_ref, next_ref, ghost_ref)
+    def place(f, carry):
+        x_ref[0, f, 0:2] = jnp.where(first, ghost_ref[f], xl_ref[f])
+        x_ref[1, f, 3:5] = jnp.where(last, ghost_ref[f], xr_ref[f])
+        x_ref[0, f, 2:5] = rows_ref[f, 0:3]
+        x_ref[1, f, 0:3] = rows_ref[f, 3:6]
+        return carry
+
+    lax.fori_loop(0, FIELDS, place, 0)
+
+    def radial(n, carry):
+        end = lax.div(n, 2)
+        at = pl.ds(pl.multiple_of(lax.rem(n, 2) * (high // 2), 8), high // 2)
+        cells = [[x_ref[end, f, k, at] for f in range(FIELDS)] for k in range(5)]
+        sides = [three_states(cells[k : k + 3]) for k in range(3)]
+        one = face(sides[0][0], sides[1][1], 0)
+        two = face(sides[1][0], sides[2][1], 0)
+        for f in range(FIELDS):
+            x_ref[end, f, 0, at] = coef * (two[f] - one[f])
+            x_ref[end, f, 1, at] = coef * jnp.where(end == 0, -two[f], one[f])
+        return carry
+
+    lax.fori_loop(0, 4, radial, 0)
+    batch = FIELDS // 2
+
+    def finish(n, carry):
+        g = lax.div(n, 2)
+        at = pl.ds(g * size, size)
+        fields = [lax.rem(n, 2) * batch + f for f in range(batch)]
+        for f in fields:
             head = dy_ref[f, g, PAD : 2 * PAD] + c_ref[f, g, 0:PAD]
             tail = dy_ref[f, g, width : PAD + width] + c_ref[f, g, PAD : 2 * PAD]
             strip = jnp.concatenate([head, dy_ref[f, g, 2 * PAD : width], tail], axis=0)
             out_ref[f, at] = v_ref[f, at] - strip.T.reshape(size, high, width)
 
-    ghost = sheared_rows(flags, weights, near_ref, next_ref)
-    ghost_low = [[jnp.where(first, ghost[k][f], xl_ref[f, k]) for f in range(FIELDS)] for k in range(2)]
-    cells = ghost_low + [load_row(w_ref, i) for i in range(3)]
-    sides = [three_states(cells[k : k + 3]) for k in range(3)]
-    outer = face(sides[0][0], sides[1][1], 0)
-    inner = face(sides[1][0], sides[2][1], 0)
-    for f in range(FIELDS):
-        out_ref[f, 0] = out_ref[f, 0] - coef * (inner[f] - outer[f])
-        out_ref[f, 1] = out_ref[f, 1] + coef * inner[f]
-    ghost_high = [[jnp.where(last, ghost[k][f], xr_ref[f, k]) for f in range(FIELDS)] for k in range(2)]
-    cells = [load_row(w_ref, rows - 3 + i) for i in range(3)] + ghost_high
-    sides = [three_states(cells[k : k + 3]) for k in range(3)]
-    inner = face(sides[0][0], sides[1][1], 0)
-    outer = face(sides[1][0], sides[2][1], 0)
-    for f in range(FIELDS):
-        out_ref[f, rows - 2] = out_ref[f, rows - 2] - coef * inner[f]
-        out_ref[f, rows - 1] = out_ref[f, rows - 1] - coef * (outer[f] - inner[f])
+        @pl.when(g == 0)
+        def _():
+            for f in fields:
+                out_ref[f, 0] = out_ref[f, 0] - x_ref[0, f, 0]
+                out_ref[f, 1] = out_ref[f, 1] - x_ref[0, f, 1]
+
+        @pl.when(g == groups - 1)
+        def _():
+            for f in fields:
+                out_ref[f, rows - 1] = out_ref[f, rows - 1] - x_ref[1, f, 0]
+                out_ref[f, rows - 2] = out_ref[f, rows - 2] - x_ref[1, f, 1]
+
+        if second:
+            part = pl.ds(fields[0], batch)
+            pltpu.make_async_copy(out_ref.at[part, at], out_hbm.at[part, at], sems.at[n]).start()
+        return carry
+
+    lax.fori_loop(0, 2 * groups, finish, 0)
     if second:
+        for n in range(2 * groups):
+            at, part = pl.ds(n // 2 * size, size), pl.ds(n % 2 * batch, batch)
+            pltpu.make_async_copy(out_ref.at[part, at], out_hbm.at[part, at], sems.at[n]).wait()
         return
 
-    def body(i, carry):
+    def primitives(i, carry):
         prim = to_primitive(load_row(out_ref, i))
         for f in range(FIELDS):
             w1_ref[f, i] = prim[f]
         return carry
 
-    lax.fori_loop(0, rows, body, 0, unroll=4)
-    for g in range(groups):
-        for f in range(FIELDS):
-            turn(w1_ref, f, g, wt1_ref)
-    send_columns(wt1_ref, last_ref, first_ref)
+    lax.fori_loop(0, rows, primitives, 0, unroll=4)
+
+    def turn_group(n, carry):
+        for f in range(batch):
+            turn(w1_ref, lax.rem(n, 2) * batch + f, lax.div(n, 2), wt1_ref)
+        return carry
+
+    lax.fori_loop(0, 2 * groups, turn_group, 0)
+    send_columns(wt1_ref, cols1_ref, last_ref, first_ref)
     send_rows(flags, w1_ref, *sends)
 
 
-def call(kernel, name, scalars, arrays, shapes, scratch=(), in_hbm=False):
+def call(kernel, name, scalars, arrays, shapes, scratch=(), in_hbm=False, out_hbm=False):
     smem = pl.BlockSpec(memory_space=pltpu.SMEM)
     vmem = pl.BlockSpec(memory_space=pltpu.VMEM)
+    hbm = pl.BlockSpec(memory_space=pltpu.HBM)
+    if in_hbm:
+        arrays = [pltpu.with_memory_space_constraint(x, pltpu.HBM) for x in arrays]
     return pl.pallas_call(
         kernel,
         name=name,
         out_shape=[jax.ShapeDtypeStruct(s, jnp.float32) for s in shapes],
-        in_specs=[smem] * len(scalars) + [pl.BlockSpec(memory_space=pltpu.HBM) if in_hbm else vmem] * len(arrays),
-        out_specs=[vmem] * len(shapes),
+        in_specs=[smem] * len(scalars) + [hbm if in_hbm else vmem] * len(arrays),
+        out_specs=[hbm if out_hbm else vmem] * len(shapes),
         scratch_shapes=[pltpu.VMEM(s, jnp.float32) if isinstance(s, tuple) else s for s in scratch],
         compiler_params=pltpu.CompilerParams(vmem_limit_bytes=20 * 1024 * 1024),
     )(*scalars, *arrays)
@@ -404,10 +467,9 @@
     low = lax.ppermute(last, "gy", [(i, (i + 1) % count_y) for i in range(count_y)])
     high = lax.ppermute(first, "gy", [((i + 1) % count_y, i) for i in range(count_y)])
     if len(swap) == 1:
-        x_low = x_high = lax.ppermute(swap[0], "gx", [(0, 1), (1, 0)])
-    else:
-        x_low = lax.ppermute(swap[1], "gx", [(i, i + 1) for i in range(count_x - 1)])
-        x_high = lax.ppermute(swap[0], "gx", [(i + 1, i) for i in range(count_x - 1)])
+        return low, high, lax.ppermute(swap[0], "gx", [(0, 1), (1, 0)])
+    x_low = lax.ppermute(swap[1], "gx", [(i, i + 1) for i in range(count_x - 1)])
+    x_high = lax.ppermute(swap[0], "gx", [(i + 1, i) for i in range(count_x - 1)])
     return low, high, x_low, x_high
 
 
@@ -428,47 +490,57 @@
     return [padded, padded, padded, tile, tile, tile]
 
 
-def inner_part(second, block, radial0, shear, *states):
-    full, turned = states[0].shape, states[1].shape
+def edge_scratch(full, groups):
+    high, width = full[2:]
+    return [
+        (FIELDS, 5, 2 * groups, width),
+        (FIELDS, 2, 2 * groups, width),
+        (FIELDS, groups, 2 * PAD, width),
+        (2, FIELDS, 5, high, width),
+        (FIELDS, 2, high, width),
+    ]
+
+
+def sections(block, flags, weights, radial0, w0, wt0, cols, last, first, rows, shear, *swap):
+    full, turned = w0.shape, wt0.shape
+    groups = turned[1]
+    sends = [x.shape for x in (cols, last, first, rows, shear, *swap)]
+    scratch = edge_scratch(full, groups)
 
     def branch(by):
-        def run(radial0, shear, *states):
-            near, following = crossing(by, shear), crossing(by + 1, shear)
-            kernel = functools.partial(interior_kernel, second)
-            name = "inner_2" if second else "inner_1"
-            v, dy = call(kernel, name, [radial0], list(states), [full, turned], inner_scratch(full))
-            return v, dy, near, following
+        def run(flags, weights, radial0, w0, wt0, cols, last, first, rows, shear, *swap):
+            low, high, *beside = exchange(last, first, swap)
+            sheared = crossing(by, shear), crossing(by + 1, shear)
+            kernel = functools.partial(interior_kernel, False)
+            v, dy = call(kernel, "inner_1", [radial0], [w0, wt0], [full, turned], inner_scratch(full))
+            w1, wt1, u1, cols, last, first, rows, shear, *swap = call(
+                functools.partial(edge_kernel, False, len(beside)),
+                "edge_1",
+                [flags, weights],
+                [v, dy, rows, cols, low, high, *sheared, *beside],
+                [full, turned, full] + sends,
+                scratch,
+            )
+            low, high, *beside = exchange(last, first, swap)
+            sheared = crossing(by, shear), crossing(by + 1, shear)
+            kernel = functools.partial(interior_kernel, True)
+            v, dy = call(kernel, "inner_2", [radial0], [w1, wt1, w0, u1], [full, turned], inner_scratch(full))
+            return v, dy, rows, cols, low, high, *sheared, *beside
 
         return run
 
     branches = [branch(by) for by in range(lax.axis_size("gy"))]
-    return lax.switch(block, branches, radial0, shear, *states)
-
-
-def sections(block, flags, weights, radial0, w0, wt0, last, first, shear, *swap):
-    full, turned = w0.shape, wt0.shape
-    groups, width = turned[1], full[3]
-    scratch = [(FIELDS, 5, 2 * groups, width), (FIELDS, 2, 2 * groups, width), (FIELDS, groups, 2 * PAD, width)]
-    sends = [x.shape for x in (last, first, shear, *swap)]
-    got = exchange(last, first, swap)
-    v, dy, *sheared = inner_part(False, block, radial0, shear, w0, wt0)
-    w1, wt1, u1, last, first, shear, *swap = call(
-        functools.partial(edge_kernel, False),
-        "edge_1",
-        [flags, weights],
-        [v, dy, w0, wt0, *got, *sheared],
-        [full, turned, full] + sends,
-        scratch,
+    arrays = lax.switch(
+        block, branches, flags, weights, radial0, w0, wt0, cols, last, first, rows, shear, *swap
     )
-    got = exchange(last, first, swap)
-    v, dy, *sheared = inner_part(True, block, radial0, shear, w1, wt1, w0, u1)
     (out,) = call(
-        functools.partial(edge_kernel, True),
+        functools.partial(edge_kernel, True, 1 if lax.axis_size("gx") == 2 else 2),
         "edge_2",
         [flags, weights],
-        [v, dy, w1, wt1, *got, *sheared],
+        arrays,
         [full],
-        scratch,
+        scratch + [full, pltpu.SemaphoreType.DMA((2 * groups,))],
+        out_hbm=True,
     )
     return out
 
@@ -499,7 +571,8 @@
     groups = rows * high // width
     turned = (FIELDS, groups, width + 2 * PAD, width)
     ends = (FIELDS, 2 * groups, width)
-    sends = [ends, ends, slab] + [slab] * (1 if count_x == 2 else 2)
+    sends = [(FIELDS, 6 * groups, width), ends, ends, (FIELDS, 6, high, width)]
+    sends += [slab] * (2 if count_x == 2 else 3)
     start_state = call(
         prepare_kernel,
         "prepare",

time: 60.9 us -> 51.4 us (0.84)
  Pallas kernels: 39.3 us -> 29.9 us
  local copies, waits for them, and re-layouts: 4.17 us -> 0 us
  starting transfers between devices: 14.9 us -> 18.2 us
    pallas_call x5, Pallas kernels: 39.3 us -> 29.9 us  [call(): pl.pallas_call(kernel, name=name, out_shape=[jax.ShapeDtypeStruct(s, jnp....]
    ppermute x4, starting transfers between devices: 3.08 us -> 7.84 us  [crossing(): return lax.ppermute(shear, ('gx', 'gy'), pairs)]
    unnamed x8 -> x0, local copies, waits for them, and re-layouts: 4.17 us -> none
    ppermute x2, starting transfers between devices: 4.09 us -> 3.26 us  [exchange(): lax.ppermute(last, 'gy', [(i, (i + 1) % count_y) for i in range(count_y)])]
    ppermute x2, starting transfers between devices: 7.62 us -> 6.86 us  [exchange(): lax.ppermute(first, 'gy', [((i + 1) % count_y, i) for i in range(count_y)])]
  transfers between devices with their start and end apart: 10 -> 10, of which waited for: 0 -> 0; matrix products, arithmetic and copies ran while one was open for 0% -> 0% of each run, Pallas kernels for 39% -> 36%
where the time goes in v2:
time: 51.4 us; the launch traced here: 50.6 us
  Pallas kernels  29.9 us (58%)
  starting transfers between devices  18.2 us (35%)
  between operations  1.58 us (3%)
  loops' own time  0.69 us (1%)
    pallas_call x5, Pallas kernels, call(): pl.pallas_call(kernel, name=name, out_shape=[jax.ShapeDtypeStruct(s, jnp....  29.9 us
    ppermute x4, starting transfers between devices, crossing(): return lax.ppermute(shear, ('gx', 'gy'), pairs)  7.84 us
    ppermute x2, starting transfers between devices, exchange(): lax.ppermute(first, 'gy', [((i + 1) % count_y, i) for i in range(count_y)])  6.86 us
    ppermute x2, starting transfers between devices, exchange(): lax.ppermute(last, 'gy', [(i, (i + 1) % count_y) for i in range(count_y)])  3.26 us
  transfers between devices with their start and end apart: 10, of which 0 were waited for; matrix products, arithmetic and copies ran while one was open for 0% of the time, Pallas kernels for 36%

profile of v2, /device:TPU:1, one launch (start us, length us, event | category | flops | bytes accessed | tf_op | source)
XLA Modules:
  0.0 50.6 jit_solution(16157051769560295621)
XLA Ops:
  1.3 0.1 pad_add_fusion.flags
  1.4 0.1 pad_maximum_fusion.weights
  1.5 0.1 pad_maximum_fusion.1.radial0
  1.6 3.1 %prepare.1 = (f32[8,32,16,128]{3,2,1,0:T(8,128)S(1)}, f32[8,4,144,128]{3,2,1,0:T(8,128)S(1)}, f32[8,24,128]{2,1,0:T(8,128)S(1)}, f32[8,8,128]{2,1,0:T(8,128)S(1)...) custom-call(s32[3]{0:T(128)S(1)} %pad_add_fusion.flags, ...), custom_call_target="tpu_custom_call" | custom-call | tf_op jit(solution)/shard_map/prepare/pallas_call | solution.py:454
  4.7 41.6 %conditional.1 = (f32[8,32,16,128]{3,2,1,0:T(8,128)S(1)}, f32[8,4,144,128]{3,2,1,0:T(8,128)S(1)}, f32[8,6,16,128]{3,2,1,0:T(8,128)S(1)}, f32[8,24,128]{2,1,0:T(8...) conditional(s32[]{:T(128)} %clamp.3, (f32[2]{0:T(128)S(1)}, ...), branch_computations={%region_0.1_spmd, %region_1.2_spmd, %region_2.3_spmd, %region_3.4_... | conditional | bytes 3670488 | solution.py:533
  4.9 0.1 collective-permute-start.84
  5.0 4.6 %collective-permute-start.83 = (f32[8,2,16,128]{3,2,1,0:T(8,128)S(1)}, f32[8,2,16,128]{3,2,1,0:T(8,128)S(1)}, u32[]{:S(2)}, u32[]{:S(2)}) collective-permute-start(f32[8,2,16,128]{3,2,1,0:T(8,128)S(1)} %get-tuple-element.560), channel_id=1, source_target_pairs={{16,9},{0,23},{17,10},{1,24},{18,11},{2,25},{19,12},{3,26},{20,13}... | collective-permute-start | bytes 393224 | tf_op jit(solution)/shard_map/cond/branch_8_fun/ppermute | solution.py:483
  9.7 2.6 %collective-permute-start.82 = (f32[8,2,16,128]{3,2,1,0:T(8,128)S(1)}, f32[8,2,16,128]{3,2,1,0:T(8,128)S(1)}, u32[]{:S(2)}, u32[]{:S(2)}) collective-permute-start(f32[8,2,16,128]{3,2,1,0:T(8,128)S(1)} %get-tuple-element.560), channel_id=1, source_target_pairs={{16,8},{0,24},{17,9},{1,25},{18,10},{2,26},{19,11},{3,27},{20,12},... | collective-permute-start | bytes 393224 | tf_op jit(solution)/shard_map/cond/branch_8_fun/ppermute | solution.py:483
  12.3 0.0 collective-permute-start.80
  12.3 5.1 %collective-permute-start.81 = (f32[8,8,128]{2,1,0:T(8,128)S(1)}, f32[8,8,128]{2,1,0:T(8,128)S(1)}, u32[]{:S(2)}, u32[]{:S(2)}) collective-permute-start(f32[8,8,128]{2,1,0:T(8,128)S(1)} %get-tuple-element.559), channel_id=1, source_target_pairs={{1,0},{2,1},{3,2},{4,3},{5,4},{6,5},{7,6},{8,7},{9,8},{10,9},{11,1... | collective-permute-start | bytes 98312 | tf_op jit(solution)/shard_map/cond/branch_8_fun/ppermute | solution.py:468
  17.3 9.2 %inner_1.24 = (f32[8,32,16,128]{3,2,1,0:T(8,128)S(1)}, f32[8,4,144,128]{3,2,1,0:T(8,128)S(1)}) custom-call(f32[2]{0:T(128)S(1)} %get-tuple-element.549.radial0, f32[8,32,16,128]{3,2,1,0:T(8,128)S(1)} %get-tuple-element.552.w_ref.refs_0_, f32[8,4,144,128]{3,2,1,0:T(8,128)S(1)} %get-tuple-element.553.wt_ref), custom_call_target="tpu_custom_call" | custom-call | tf_op jit(solution)/shard_map/cond/branch_8_fun/inner_1/pallas_call | solution.py:454
  26.5 0.0 collective-permute-done.80.low_ref
  26.5 0.0 collective-permute-done.81.high_ref
  26.5 0.0 collective-permute-done.84.refs_0_
  26.5 0.0 collective-permute-done.83.next_ref
  26.5 0.0 collective-permute-done.82.near_ref
  26.6 4.4 %edge_1.24 = (f32[8,32,16,128]{3,2,1,0:T(8,128)S(1)}, f32[8,4,144,128]{3,2,1,0:T(8,128)S(1)}, f32[8,32,16,128]{3,2,1,0:T(8,128)S(1)}, f32[8,24,128]{2,1,0:T(8,12...) custom-call(s32[3]{0:T(128)S(1)} %get-tuple-element.550.flags, ...), custom_call_target="tpu_custom_call" | custom-call | tf_op jit(solution)/shard_map/cond/branch_8_fun/edge_1/pallas_call | solution.py:454
  30.9 0.1 collective-permute-start.89
  31.0 0.1 collective-permute-start.88
  31.1 0.6 %collective-permute-start.87 = (f32[8,2,16,128]{3,2,1,0:T(8,128)S(1)}, f32[8,2,16,128]{3,2,1,0:T(8,128)}, u32[]{:S(2)}, u32[]{:S(2)}) collective-permute-start(f32[8,2,16,128]{3,2,1,0:T(8,128)S(1)} %get-tuple-element.571), channel_id=1, source_target_pairs={{16,8},{0,24},{17,9},{1,25},{18,10},{2,26},{19,11},{3,27},{20,12},... | collective-permute-start | bytes 393224 | tf_op jit(solution)/shard_map/cond/branch_8_fun/ppermute | solution.py:483
  31.6 3.3 %collective-permute-start.85 = (f32[8,8,128]{2,1,0:T(8,128)S(1)}, f32[8,8,128]{2,1,0:T(8,128)}, u32[]{:S(2)}, u32[]{:S(2)}) collective-permute-start(f32[8,8,128]{2,1,0:T(8,128)S(1)} %get-tuple-element.569), channel_id=1, source_target_pairs={{0,1},{1,2},{2,3},{3,4},{4,5},{5,6},{6,7},{7,8},{8,9},{9,10},{10,1... | collective-permute-start | bytes 98312 | tf_op jit(solution)/shard_map/cond/branch_8_fun/ppermute | solution.py:467
  34.9 1.8 %collective-permute-start.86 = (f32[8,8,128]{2,1,0:T(8,128)S(1)}, f32[8,8,128]{2,1,0:T(8,128)}, u32[]{:S(2)}, u32[]{:S(2)}) collective-permute-start(f32[8,8,128]{2,1,0:T(8,128)S(1)} %get-tuple-element.570), channel_id=1, source_target_pairs={{1,0},{2,1},{3,2},{4,3},{5,4},{6,5},{7,6},{8,7},{9,8},{10,9},{11,1... | collective-permute-start | bytes 98312 | tf_op jit(solution)/shard_map/cond/branch_8_fun/ppermute | solution.py:468
  36.7 9.2 %inner_2.24 = (f32[8,32,16,128]{3,2,1,0:T(8,128)S(1)}, f32[8,4,144,128]{3,2,1,0:T(8,128)S(1)}) custom-call(f32[2]{0:T(128)S(1)} %get-tuple-element.549.radial0, f32[8,32,16,128]{3,2,1,0:T(8,128)S(1)} %get-tuple-element.562.w_ref, f32[8,4,144,128]{3,2,1,0:T(8,128)S(1)} %get-tuple-element.563.wt_ref, f32[8,32,16,128]{3,2,1,0:T(8,128)S(1)} %get-tuple-element.552.w_ref.refs_0_, ...), custom_call_target="tpu_custom_call" | custom-call | tf_op jit(solution)/shard_map/cond/branch_8_fun/inner_2/pallas_call | solution.py:454
  45.9 0.0 collective-permute-done.85
  45.9 0.0 collective-permute-done.86
  45.9 0.0 collective-permute-done.89
  45.9 0.0 collective-permute-done.88
  45.9 0.0 collective-permute-done.87
  46.3 4.1 %edge_2.1 = f32[8,32,16,128]{3,2,1,0:T(8,128)} custom-call(s32[3]{0:T(128)S(1)} %pad_add_fusion.flags, f32[3]{0:T(128)S(1)} %pad_maximum_fusion.weights, f32[8,32,16,128]{3,2,1,0:T(8,128)S(1)} %get-tuple-element.766.v_ref, f32[8,4,144,128]{3,2,1,0:T(8,128)S(1)} %get-tuple-element.767.dy_ref, f32[8,6,16,128]{3,2,1,0:T(8,128)S(1)} %get-tuple-element.768.rows_ref, ...), custom_call_target="tpu_custom_call" | custom-call | tf_op jit(solution)/shard_map/edge_2/pallas_call | solution.py:454
Async XLA Ops:
  4.9 21.6 %collective-permute-start.84 = (f32[8,2,16,128]{3,2,1,0:T(8,128)S(1)}, f32[8,2,16,128]{3,2,1,0:T(8,128)S(1)}, u32[]{:S(2)}, u32[]{:S(2)}) collective-permute-start(f32[8,2,16,128]{3,2,1,0:T(8,128)S(1)} %get-tuple-element.561), channel_id=1, source_target_pairs={{0,16},{16,0},{1,17},{17,1},{2,18},{18,2},{3,19},{19,3},{4,20},{20... | collective-permute-start | bytes 393224 | tf_op jit(solution)/shard_map/cond/branch_8_fun/ppermute | solution.py:470
  5.0 21.5 %collective-permute-start.83 = (f32[8,2,16,128]{3,2,1,0:T(8,128)S(1)}, f32[8,2,16,128]{3,2,1,0:T(8,128)S(1)}, u32[]{:S(2)}, u32[]{:S(2)}) collective-permute-start(f32[8,2,16,128]{3,2,1,0:T(8,128)S(1)} %get-tuple-element.560), channel_id=1, source_target_pairs={{16,9},{0,23},{17,10},{1,24},{18,11},{2,25},{19,12},{3,26},{20,13}... | collective-permute-start | bytes 393224 | tf_op jit(solution)/shard_map/cond/branch_8_fun/ppermute | solution.py:483
  9.7 16.9 %collective-permute-start.82 = (f32[8,2,16,128]{3,2,1,0:T(8,128)S(1)}, f32[8,2,16,128]{3,2,1,0:T(8,128)S(1)}, u32[]{:S(2)}, u32[]{:S(2)}) collective-permute-start(f32[8,2,16,128]{3,2,1,0:T(8,128)S(1)} %get-tuple-element.560), channel_id=1, source_target_pairs={{16,8},{0,24},{17,9},{1,25},{18,10},{2,26},{19,11},{3,27},{20,12},... | collective-permute-start | bytes 393224 | tf_op jit(solution)/shard_map/cond/branch_8_fun/ppermute | solution.py:483
  12.3 14.3 %collective-permute-start.80 = (f32[8,8,128]{2,1,0:T(8,128)S(1)}, f32[8,8,128]{2,1,0:T(8,128)S(1)}, u32[]{:S(2)}, u32[]{:S(2)}) collective-permute-start(f32[8,8,128]{2,1,0:T(8,128)S(1)} %get-tuple-element.558), channel_id=1, source_target_pairs={{0,1},{1,2},{2,3},{3,4},{4,5},{5,6},{6,7},{7,8},{8,9},{9,10},{10,1... | collective-permute-start | bytes 98312 | tf_op jit(solution)/shard_map/cond/branch_8_fun/ppermute | solution.py:467
  12.3 14.3 %collective-permute-start.81 = (f32[8,8,128]{2,1,0:T(8,128)S(1)}, f32[8,8,128]{2,1,0:T(8,128)S(1)}, u32[]{:S(2)}, u32[]{:S(2)}) collective-permute-start(f32[8,8,128]{2,1,0:T(8,128)S(1)} %get-tuple-element.559), channel_id=1, source_target_pairs={{1,0},{2,1},{3,2},{4,3},{5,4},{6,5},{7,6},{8,7},{9,8},{10,9},{11,1... | collective-permute-start | bytes 98312 | tf_op jit(solution)/shard_map/cond/branch_8_fun/ppermute | solution.py:468
  30.9 15.0 %collective-permute-start.89 = (f32[8,2,16,128]{3,2,1,0:T(8,128)S(1)}, f32[8,2,16,128]{3,2,1,0:T(8,128)}, u32[]{:S(2)}, u32[]{:S(2)}) collective-permute-start(f32[8,2,16,128]{3,2,1,0:T(8,128)S(1)} %get-tuple-element.572), channel_id=1, source_target_pairs={{0,16},{16,0},{1,17},{17,1},{2,18},{18,2},{3,19},{19,3},{4,20},{20... | collective-permute-start | bytes 393224 | tf_op jit(solution)/shard_map/cond/branch_8_fun/ppermute | solution.py:470
  31.0 14.9 %collective-permute-start.88 = (f32[8,2,16,128]{3,2,1,0:T(8,128)S(1)}, f32[8,2,16,128]{3,2,1,0:T(8,128)}, u32[]{:S(2)}, u32[]{:S(2)}) collective-permute-start(f32[8,2,16,128]{3,2,1,0:T(8,128)S(1)} %get-tuple-element.571), channel_id=1, source_target_pairs={{16,9},{0,23},{17,10},{1,24},{18,11},{2,25},{19,12},{3,26},{20,13}... | collective-permute-start | bytes 393224 | tf_op jit(solution)/shard_map/cond/branch_8_fun/ppermute | solution.py:483
  31.1 14.9 %collective-permute-start.87 = (f32[8,2,16,128]{3,2,1,0:T(8,128)S(1)}, f32[8,2,16,128]{3,2,1,0:T(8,128)}, u32[]{:S(2)}, u32[]{:S(2)}) collective-permute-start(f32[8,2,16,128]{3,2,1,0:T(8,128)S(1)} %get-tuple-element.571), channel_id=1, source_target_pairs={{16,8},{0,24},{17,9},{1,25},{18,10},{2,26},{19,11},{3,27},{20,12},... | collective-permute-start | bytes 393224 | tf_op jit(solution)/shard_map/cond/branch_8_fun/ppermute | solution.py:483
  31.6 14.3 %collective-permute-start.85 = (f32[8,8,128]{2,1,0:T(8,128)S(1)}, f32[8,8,128]{2,1,0:T(8,128)}, u32[]{:S(2)}, u32[]{:S(2)}) collective-permute-start(f32[8,8,128]{2,1,0:T(8,128)S(1)} %get-tuple-element.569), channel_id=1, source_target_pairs={{0,1},{1,2},{2,3},{3,4},{4,5},{5,6},{6,7},{7,8},{8,9},{9,10},{10,1... | collective-permute-start | bytes 98312 | tf_op jit(solution)/shard_map/cond/branch_8_fun/ppermute | solution.py:467
  34.9 11.0 %collective-permute-start.86 = (f32[8,8,128]{2,1,0:T(8,128)S(1)}, f32[8,8,128]{2,1,0:T(8,128)}, u32[]{:S(2)}, u32[]{:S(2)}) collective-permute-start(f32[8,8,128]{2,1,0:T(8,128)S(1)} %get-tuple-element.570), channel_id=1, source_target_pairs={{1,0},{2,1},{3,2},{4,3},{5,4},{6,5},{7,6},{8,7},{9,8},{10,9},{11,1... | collective-permute-start | bytes 98312 | tf_op jit(solution)/shard_map/cond/branch_8_fun/ppermute | solution.py:468

commit v3 on v2

--- a/solution.py
+++ b/solution.py
@@ -59,8 +59,10 @@
     speed = jnp.maximum(sl, sr)
     out = []
     for f in range(FIELDS):
-        jump = speed * (ur[f] - ul[f])
-        out.append(-jump if fl[f] is None else (fl[f] + fr[f]) - jump)
+        if fl[f] is None:
+            out.append(speed * (ul[f] - ur[f]))
+        else:
+            out.append((fl[f] + fr[f]) - speed * (ur[f] - ul[f]))
     return out
 
 
@@ -99,34 +101,35 @@
     wt_ref[f, g, PAD : PAD + width] = tile.T
 
 
-def send_columns(wt_ref, cols_ref, last_ref, first_ref):
-    groups, rows = wt_ref.shape[1:3]
+def pad_ends(wt_ref, f, g):
+    rows = wt_ref.shape[2]
+    wt_ref[f, g, 0:PAD] = wt_ref[f, g, PAD : 2 * PAD]
+    wt_ref[f, g, rows - PAD : rows] = wt_ref[f, g, rows - 2 * PAD : rows - PAD]
+
+
+def send_columns(flags, groups, wt_ref, cols_ref, even_ref, odd_ref):
+    rows = wt_ref.shape[2]
+    even = flags[3] == 1
     cells = [PAD, PAD + 1, PAD + 2, rows - PAD - 3, rows - PAD - 2, rows - PAD - 1]
 
     def body(f, carry):
-        for k, cell in enumerate(cells):
-            for g in range(groups):
+        for g in range(groups):
+            for k, cell in enumerate(cells):
                 cols_ref[f, k * groups + g : k * groups + g + 1] = wt_ref[f, g, cell : cell + 1]
-        first_ref[f] = cols_ref[f, 0 : 2 * groups]
-        last_ref[f] = cols_ref[f, 4 * groups : 6 * groups]
+            pad_ends(wt_ref, f, g)
+        first, last = cols_ref[f, 0 : 2 * groups], cols_ref[f, 4 * groups : 6 * groups]
+        even_ref[f] = jnp.where(even, last, first)
+        odd_ref[f] = jnp.where(even, first, last)
         return carry
 
     lax.fori_loop(0, FIELDS, body, 0)
 
 
-def send_rows(flags, w_ref, rows_ref, shear_ref, *swap_refs):
-    rows = w_ref.shape[1]
+def send_rows(flags, rows_ref, shear_ref, *swap_refs):
     first = flags[0] == 1
 
-    def copy(f, carry):
-        rows_ref[f, 0:3] = w_ref[f, 0:3]
-        rows_ref[f, 3:6] = w_ref[f, rows - 3 : rows]
-        return carry
-
-    lax.fori_loop(0, FIELDS, copy, 0)
-
     def body(k, carry):
-        low, high = load_row(w_ref, k), load_row(w_ref, rows - 2 + k)
+        low, high = load_row(rows_ref, k), load_row(rows_ref, 4 + k)
         if len(swap_refs) == 1:
             for f in range(FIELDS):
                 swap_refs[0][f, k] = jnp.where(first, high[f], low[f])
@@ -142,7 +145,7 @@
     lax.fori_loop(0, 2, body, 0)
 
 
-def prepare_kernel(flags, radial0, rho_hbm, vel_hbm, mag_hbm, pres_hbm, w_ref, wt_ref, cols_ref, last_ref, first_ref, *rest):
+def prepare_kernel(flags, radial0, rho_hbm, vel_hbm, mag_hbm, pres_hbm, w_ref, wt_ref, cols_ref, even_ref, odd_ref, rows_ref, *rest):
     *sends, sems = rest
     rows = w_ref.shape[1]
     parts = sems.shape[1]
@@ -172,8 +175,15 @@
             return carry
 
         lax.fori_loop(0, FIELDS // 4, turn_fields, 0)
-    send_columns(wt_ref, cols_ref, last_ref, first_ref)
-    send_rows(flags, w_ref, *sends)
+    send_columns(flags, parts, wt_ref, cols_ref, even_ref, odd_ref)
+
+    def copy(f, carry):
+        rows_ref[f, 0:3] = w_ref[f, 0:3]
+        rows_ref[f, 3:6] = w_ref[f, rows - 3 : rows]
+        return carry
+
+    lax.fori_loop(0, FIELDS, copy, 0)
+    send_rows(flags, rows_ref, *sends)
 
 
 def three_states(cells):
@@ -203,24 +213,36 @@
     return result
 
 
-def interior_kernel(second, radial0, w_ref, wt_ref, *refs):
+def interior_kernel(second, radial0, *refs):
     if second:
-        w0_ref, u1_ref = refs[:2]
-        refs = refs[2:]
-    v_ref, dy_ref, hz_ref, rz_ref, fz_ref, wl_ref, dx_ref, fx_ref = refs
+        wt_ref, w0_ref, v_ref, dy_ref, w_ref, *refs = refs
+    else:
+        w_ref, wt_ref, vt_ref, v_ref, *refs = refs
+        dy_ref = vt_ref
+    hz_ref, rz_ref, fz_ref, wl_ref, dx_ref, fx_ref = refs
     rows, high, width = w_ref.shape[1:]
-    groups = wt_ref.shape[1]
+    per_group = width // high
+    groups = rows // per_group
     step = 0.5 * TIME_STEP if second else TIME_STEP
     coef = 0.5 * step
     omega_q = radial0[1]
     omega = omega_q / SHEAR_Q
     next_row, last_row = slice(9, 9 + high), slice(7, 7 + high)
-
-    for f in range(FIELDS):
-        blank = jnp.zeros((high, width), jnp.float32)
-        dx_ref[f], fx_ref[f], wl_ref[f] = blank, blank, w_ref[f, 0]
+    early = per_group + 1
+
+    def turn_result(m):
+        g, f = lax.div(m, FIELDS), lax.rem(m, FIELDS)
+        tile = v_ref[f, pl.ds(jnp.minimum(g, groups - 1) * per_group, per_group)].reshape(width, width)
+        vt_ref[f, jnp.minimum(g, groups), PAD : PAD + width] = tile.T
+
+    def turn_state(m):
+        g, f = lax.div(m, FIELDS), lax.rem(m, FIELDS)
+        tile = wt_ref[f, g, PAD : PAD + width].T
+        w_ref[f, pl.ds(g * per_group, per_group)] = tile.reshape(per_group, high, width)
 
     def body(i, carry):
+        if not second:
+            turn_result(jnp.maximum(i - early, 0))
         w = load_row(w_ref, i)
         half = [0.5 * x for x in w]
 
@@ -245,16 +267,16 @@
             wl_ref[f] = w[f] + slope
             right.append(w[f] - slope)
         fx = face(wl, right, 0)
-        valid = jnp.logical_and(i >= 2, i <= rows - 2)
-        for f in range(FIELDS):
-            here = jnp.where(valid, fx[f], 0.0)
-            v_ref[f, before] = v_ref[f, before] - coef * (here - fx_ref[f])
+        scale = jnp.where(jnp.logical_and(i >= 2, i <= rows - 2), coef, 0.0)
+        for f in range(FIELDS):
+            here = scale * fx[f]
+            v_ref[f, before] = v_ref[f, before] - (here - fx_ref[f])
             fx_ref[f] = here
 
         x = radial0[0] + i.astype(jnp.float32)
         cons = to_conserved(w)
         if second:
-            base = [0.5 * (a + u1_ref[f, i]) for f, a in enumerate(to_conserved(load_row(w0_ref, i)))]
+            base = [0.5 * (a + b) for a, b in zip(to_conserved(load_row(w0_ref, i)), cons)]
         else:
             base = cons
         tidal = 2.0 * omega * omega_q * x
@@ -266,13 +288,15 @@
             v_ref[f, i] = value[f]
         return carry
 
-    lax.fori_loop(0, rows, body, 0)
-
-    size = 16
+    size = groups * width // rows
     strips = width // size
     row = lax.broadcasted_iota(jnp.int32, (size, width), 0)
 
     def body_y(n, carry):
+        if second:
+            turn_state(n)
+        else:
+            turn_result(rows - early + n)
         g, start = lax.div(n, strips), size * lax.rem(n, strips)
         at = pl.multiple_of(start + PAD, 8)
         left, right = [], []
@@ -284,16 +308,38 @@
             right.append(w - slope)
         fy = face(left, right, 1)
         cell = row + start
-        valid = jnp.logical_and(cell >= 2, cell <= width - 2)
-        for f in range(FIELDS):
-            here = jnp.where(valid, fy[f], 0.0)
-            dy_ref[f, g, pl.ds(at - 1, size)] = coef * (here - behind(fz_ref, f, here))
-        return carry
-
-    lax.fori_loop(0, groups * strips, body_y, 0)
-    for f in range(FIELDS):
-        for g in range(groups):
-            dy_ref[f, g, PAD + width - 1 : PAD + width] = jnp.zeros((1, width), jnp.float32)
+        scale = jnp.where(jnp.logical_and(cell >= 2, cell <= width - 2), coef, 0.0)
+        for f in range(FIELDS):
+            here = scale * fy[f]
+            change = here - behind(fz_ref, f, here)
+            if second:
+                dy_ref[f, g, pl.ds(at - 1, size)] = change
+            else:
+                vt_ref[f, g, pl.ds(at - 1, size)] = vt_ref[f, g, pl.ds(at - 1, size)] - change
+        return carry
+
+    def azimuthal():
+        for f in range(FIELDS):
+            hz_ref[f, 0:8] = jnp.zeros((8, width), jnp.float32)
+            rz_ref[f, 0:8] = wt_ref[f, 0, PAD : 2 * PAD]
+            fz_ref[f, 0:8] = jnp.zeros((8, width), jnp.float32)
+        lax.fori_loop(0, rows, body_y, 0)
+
+    def others():
+        for f in range(FIELDS):
+            blank = jnp.zeros((high, width), jnp.float32)
+            dx_ref[f], fx_ref[f], wl_ref[f] = blank, blank, w_ref[f, 0]
+        lax.fori_loop(0, rows, body, 0)
+
+    if second:
+        azimuthal()
+        others()
+        for f in range(FIELDS):
+            for g in range(groups):
+                dy_ref[f, g, PAD + width - 1 : PAD + width] = jnp.zeros((1, width), jnp.float32)
+    else:
+        others()
+        azimuthal()
 
 
 def sheared_rows(flags, weights, near_ref, next_ref, ghost_ref):
@@ -325,26 +371,33 @@
     lax.fori_loop(0, 2, body, 0)
 
 
-def edge_kernel(second, beside, flags, weights, v_ref, dy_ref, rows_ref, cols_ref, low_ref, high_ref, near_ref, next_ref, *refs):
-    beside, refs = refs[:beside], refs[beside:]
-    xl_ref, xr_ref = beside[0], beside[-1]
-    rows, high, width = v_ref.shape[1:]
-    groups = dy_ref.shape[1]
-    size = rows // groups
+def edge_kernel(second, beside, flags, weights, *refs):
+    if second:
+        v_ref, dy_ref, *refs = refs
+    else:
+        vt_ref, *refs = refs
+    rows_ref, cols_ref, even_ref, odd_ref, near_ref, next_ref, *refs = refs
+    xl_ref, xr_ref = refs[0], refs[beside - 1]
+    if second:
+        out_hbm, e_ref, a_ref, c_ref, x_ref, ghost_ref, out_ref, sems = refs[beside:]
+    else:
+        w1_ref, cols1_ref, even1_ref, odd1_ref, rows1_ref, *sends, e_ref, a_ref, c_ref, x_ref, ghost_ref = refs[beside:]
+    high, width = rows_ref.shape[2:]
+    groups = cols_ref.shape[1] // 6
+    size = width // high
+    rows = groups * size
     step = 0.5 * TIME_STEP if second else TIME_STEP
     coef = 0.5 * step
-    if second:
-        out_hbm, e_ref, a_ref, c_ref, x_ref, ghost_ref, out_ref, sems = refs
-    else:
-        w1_ref, wt1_ref, out_ref, cols1_ref, last_ref, first_ref, *sends, e_ref, a_ref, c_ref, x_ref, ghost_ref = refs
-    first, last = flags[0] == 1, flags[1] == 1
+    first, last, even = flags[0] == 1, flags[1] == 1, flags[3] == 1
 
     def gather(f, carry):
-        for k in range(5):
-            at = slice(k % 2 * groups, k % 2 * groups + groups) if k < 2 else slice((k - 2) * groups, (k - 1) * groups)
-            e_ref[f, k, 0:groups] = low_ref[f, at] if k < 2 else cols_ref[f, at]
-            at = slice((k + 3) * groups, (k + 4) * groups) if k < 3 else slice((k - 3) * groups, (k - 2) * groups)
-            e_ref[f, k, groups : 2 * groups] = cols_ref[f, at] if k < 3 else high_ref[f, at]
+        for k in range(2):
+            at = slice(k * groups, (k + 1) * groups)
+            e_ref[f, k, 0:groups] = jnp.where(even, odd_ref[f, at], even_ref[f, at])
+            e_ref[f, 3 + k, groups : 2 * groups] = jnp.where(even, even_ref[f, at], odd_ref[f, at])
+        for k in range(3):
+            e_ref[f, 2 + k, 0:groups] = cols_ref[f, k * groups : (k + 1) * groups]
+            e_ref[f, k, groups : 2 * groups] = cols_ref[f, (3 + k) * groups : (4 + k) * groups]
         return carry
 
     lax.fori_loop(0, FIELDS, gather, 0)
@@ -357,16 +410,18 @@
         a_ref[f, 0] = coef * (two[f] - one[f])
         a_ref[f, 1] = coef * jnp.where(low_end, -two[f], one[f])
 
-    def scatter(f, carry):
-        for g in range(groups):
-            c_ref[f, g] = jnp.zeros((2 * PAD, width), jnp.float32)
-            c_ref[f, g, 0:1] = a_ref[f, 0, g : g + 1]
-            c_ref[f, g, 1:2] = a_ref[f, 1, g : g + 1]
-            c_ref[f, g, 2 * PAD - 2 : 2 * PAD - 1] = a_ref[f, 1, groups + g : groups + g + 1]
-            c_ref[f, g, 2 * PAD - 1 : 2 * PAD] = a_ref[f, 0, groups + g : groups + g + 1]
-        return carry
-
-    lax.fori_loop(0, FIELDS, scatter, 0)
+    if second:
+
+        def scatter(f, carry):
+            for g in range(groups):
+                c_ref[f, g] = jnp.zeros((2 * PAD, width), jnp.float32)
+                c_ref[f, g, 0:1] = a_ref[f, 0, g : g + 1]
+                c_ref[f, g, 1:2] = a_ref[f, 1, g : g + 1]
+                c_ref[f, g, 2 * PAD - 2 : 2 * PAD - 1] = a_ref[f, 1, groups + g : groups + g + 1]
+                c_ref[f, g, 2 * PAD - 1 : 2 * PAD] = a_ref[f, 0, groups + g : groups + g + 1]
+            return carry
+
+        lax.fori_loop(0, FIELDS, scatter, 0)
 
     sheared_rows(flags, weights, near_ref, next_ref, ghost_ref)
     def place(f, carry):
@@ -392,6 +447,55 @@
 
     lax.fori_loop(0, 4, radial, 0)
     batch = FIELDS // 2
+
+    if not second:
+        lane = lanes_of((width, width))
+
+        def correct(n, carry):
+            for k in range(batch):
+                f = n * batch + k
+                strip = [x_ref[0, f, 0], x_ref[0, f, 1], jnp.zeros((width - 4 * high, width), jnp.float32)]
+                strip = jnp.concatenate(strip + [x_ref[1, f, 1], x_ref[1, f, 0]], axis=0).T
+                at = slice(PAD, PAD + width)
+                w1_ref[f, 0, at] = vt_ref[f, 0, at] - jnp.where(lane < width // 2, strip, 0.0)
+                w1_ref[f, groups - 1, at] = vt_ref[f, groups - 1, at] - jnp.where(lane < width // 2, 0.0, strip)
+            return carry
+
+        lax.fori_loop(0, FIELDS // batch, correct, 0)
+
+        def correct_rows(f, carry):
+            for g in range(groups):
+                places = [(0, 0, g), (1, 1, g), (width - 2, 1, groups + g), (width - 1, 0, groups + g)]
+                for to, kind, at in places:
+                    to = slice(PAD + to, PAD + to + 1)
+                    w1_ref[f, g, to] = w1_ref[f, g, to] - a_ref[f, kind, at : at + 1]
+            return carry
+
+        lax.fori_loop(0, FIELDS, correct_rows, 0)
+        strips = width // 16
+
+        def primitives(n, carry):
+            g, at = lax.div(n, strips), pl.ds(pl.multiple_of(PAD + 16 * lax.rem(n, strips), 8), 16)
+            prim = to_primitive([w1_ref[f, g, at] for f in range(FIELDS)])
+            for f in range(FIELDS):
+                w1_ref[f, g, at] = prim[f]
+            return carry
+
+        lax.fori_loop(0, groups * strips, primitives, 0, unroll=4)
+
+        def turn_rows(n, carry):
+            for k in range(batch):
+                f = n * batch + k
+                at = slice(PAD, PAD + width)
+                strip = jnp.where(lane < width // 2, w1_ref[f, 0, at], w1_ref[f, groups - 1, at]).T
+                rows1_ref[f, 0:3] = strip[0 : 3 * high].reshape(3, high, width)
+                rows1_ref[f, 3:6] = strip[width - 3 * high : width].reshape(3, high, width)
+            return carry
+
+        lax.fori_loop(0, FIELDS // batch, turn_rows, 0)
+        send_columns(flags, groups, w1_ref, cols1_ref, even1_ref, odd1_ref)
+        send_rows(flags, rows1_ref, *sends)
+        return
 
     def finish(n, carry):
         g = lax.div(n, 2)
@@ -415,37 +519,17 @@
                 out_ref[f, rows - 1] = out_ref[f, rows - 1] - x_ref[1, f, 0]
                 out_ref[f, rows - 2] = out_ref[f, rows - 2] - x_ref[1, f, 1]
 
-        if second:
-            part = pl.ds(fields[0], batch)
-            pltpu.make_async_copy(out_ref.at[part, at], out_hbm.at[part, at], sems.at[n]).start()
+        part = pl.ds(fields[0], batch)
+        pltpu.make_async_copy(out_ref.at[part, at], out_hbm.at[part, at], sems.at[n]).start()
         return carry
 
     lax.fori_loop(0, 2 * groups, finish, 0)
-    if second:
-        for n in range(2 * groups):
-            at, part = pl.ds(n // 2 * size, size), pl.ds(n % 2 * batch, batch)
-            pltpu.make_async_copy(out_ref.at[part, at], out_hbm.at[part, at], sems.at[n]).wait()
-        return
-
-    def primitives(i, carry):
-        prim = to_primitive(load_row(out_ref, i))
-        for f in range(FIELDS):
-            w1_ref[f, i] = prim[f]
-        return carry
-
-    lax.fori_loop(0, rows, primitives, 0, unroll=4)
-
-    def turn_group(n, carry):
-        for f in range(batch):
-            turn(w1_ref, lax.rem(n, 2) * batch + f, lax.div(n, 2), wt1_ref)
-        return carry
-
-    lax.fori_loop(0, 2 * groups, turn_group, 0)
-    send_columns(wt1_ref, cols1_ref, last_ref, first_ref)
-    send_rows(flags, w1_ref, *sends)
-
-
-def call(kernel, name, scalars, arrays, shapes, scratch=(), in_hbm=False, out_hbm=False):
+    for n in range(2 * groups):
+        at, part = pl.ds(n // 2 * size, size), pl.ds(n % 2 * batch, batch)
+        pltpu.make_async_copy(out_ref.at[part, at], out_hbm.at[part, at], sems.at[n]).wait()
+
+
+def call(kernel, name, scalars, arrays, shapes, scratch=(), in_hbm=False, out_hbm=False, aliases=None):
     smem = pl.BlockSpec(memory_space=pltpu.SMEM)
     vmem = pl.BlockSpec(memory_space=pltpu.VMEM)
     hbm = pl.BlockSpec(memory_space=pltpu.HBM)
@@ -458,19 +542,24 @@
         in_specs=[smem] * len(scalars) + [hbm if in_hbm else vmem] * len(arrays),
         out_specs=[hbm if out_hbm else vmem] * len(shapes),
         scratch_shapes=[pltpu.VMEM(s, jnp.float32) if isinstance(s, tuple) else s for s in scratch],
+        input_output_aliases=aliases or {},
         compiler_params=pltpu.CompilerParams(vmem_limit_bytes=20 * 1024 * 1024),
     )(*scalars, *arrays)
 
 
-def exchange(last, first, swap):
+def exchange(even, odd, swap):
     count_x, count_y = lax.axis_size("gx"), lax.axis_size("gy")
-    low = lax.ppermute(last, "gy", [(i, (i + 1) % count_y) for i in range(count_y)])
-    high = lax.ppermute(first, "gy", [((i + 1) % count_y, i) for i in range(count_y)])
+
+    def pairs(start):
+        ends = [(i, (i + 1) % count_y) for i in range(start, count_y, 2)]
+        return ends + [(j, i) for i, j in ends]
+
+    even, odd = lax.ppermute(even, "gy", pairs(0)), lax.ppermute(odd, "gy", pairs(1))
     if len(swap) == 1:
-        return low, high, lax.ppermute(swap[0], "gx", [(0, 1), (1, 0)])
+        return even, odd, lax.ppermute(swap[0], "gx", [(0, 1), (1, 0)])
     x_low = lax.ppermute(swap[1], "gx", [(i, i + 1) for i in range(count_x - 1)])
     x_high = lax.ppermute(swap[0], "gx", [(i + 1, i) for i in range(count_x - 1)])
-    return low, high, x_low, x_high
+    return even, odd, x_low, x_high
 
 
 def crossing(by, shear):
@@ -501,37 +590,38 @@
     ]
 
 
-def sections(block, flags, weights, radial0, w0, wt0, cols, last, first, rows, shear, *swap):
+def sections(block, flags, weights, radial0, w0, wt0, cols, even, odd, rows, shear, *swap):
     full, turned = w0.shape, wt0.shape
-    groups = turned[1]
-    sends = [x.shape for x in (cols, last, first, rows, shear, *swap)]
+    groups = cols.shape[1] // 6
+    sends = [x.shape for x in (cols, even, odd, rows, shear, *swap)]
     scratch = edge_scratch(full, groups)
 
     def branch(by):
-        def run(flags, weights, radial0, w0, wt0, cols, last, first, rows, shear, *swap):
-            low, high, *beside = exchange(last, first, swap)
+        def run(flags, weights, radial0, w0, wt0, cols, even, odd, rows, shear, *swap):
+            even, odd, *beside = exchange(even, odd, swap)
             sheared = crossing(by, shear), crossing(by + 1, shear)
             kernel = functools.partial(interior_kernel, False)
-            v, dy = call(kernel, "inner_1", [radial0], [w0, wt0], [full, turned], inner_scratch(full))
-            w1, wt1, u1, cols, last, first, rows, shear, *swap = call(
+            (vt,) = call(kernel, "inner_1", [radial0], [w0, wt0], [turned], [full] + inner_scratch(full))
+            wt1, cols, even, odd, rows, shear, *swap = call(
                 functools.partial(edge_kernel, False, len(beside)),
                 "edge_1",
                 [flags, weights],
-                [v, dy, rows, cols, low, high, *sheared, *beside],
-                [full, turned, full] + sends,
+                [vt, rows, cols, even, odd, *sheared, *beside],
+                [turned] + sends,
                 scratch,
+                aliases={2: 0},
             )
-            low, high, *beside = exchange(last, first, swap)
+            even, odd, *beside = exchange(even, odd, swap)
             sheared = crossing(by, shear), crossing(by + 1, shear)
             kernel = functools.partial(interior_kernel, True)
-            v, dy = call(kernel, "inner_2", [radial0], [w1, wt1, w0, u1], [full, turned], inner_scratch(full))
-            return v, dy, rows, cols, low, high, *sheared, *beside
+            v, dy = call(kernel, "inner_2", [radial0], [wt1, w0], [full, turned], [full] + inner_scratch(full))
+            return v, dy, rows, cols, even, odd, *sheared, *beside
 
         return run
 
     branches = [branch(by) for by in range(lax.axis_size("gy"))]
     arrays = lax.switch(
-        block, branches, flags, weights, radial0, w0, wt0, cols, last, first, rows, shear, *swap
+        block, branches, flags, weights, radial0, w0, wt0, cols, even, odd, rows, shear, *swap
     )
     (out,) = call(
         functools.partial(edge_kernel, True, 1 if lax.axis_size("gx") == 2 else 2),
@@ -557,7 +647,8 @@
     weight = remap_weight.astype(jnp.float32) * WEIGHT_SCALE
     block, rest = shear_shift // width, shear_shift % width
     start = jnp.where(is_first, width - 1 - rest, rest)
-    flags = jnp.stack([is_first.astype(jnp.int32), is_last.astype(jnp.int32), start.astype(jnp.int32)])
+    even = 1 - lax.axis_index("gy") % 2
+    flags = jnp.stack([x.astype(jnp.int32) for x in (is_first, is_last, start, even)])
     other = 1.0 - weight
     weights = jnp.stack(
         [
@@ -569,7 +660,7 @@
     full = (FIELDS, rows, high, width)
     slab = (FIELDS, 2, high, width)
     groups = rows * high // width
-    turned = (FIELDS, groups, width + 2 * PAD, width)
+    turned = (FIELDS, groups + 1, width + 2 * PAD, width)
     ends = (FIELDS, 2 * groups, width)
     sends = [(FIELDS, 6 * groups, width), ends, ends, (FIELDS, 6, high, width)]
     sends += [slab] * (2 if count_x == 2 else 3)

time: 51.4 us -> 50.7 us (0.986)
  starting transfers between devices: 18.2 us -> 17.5 us
    ppermute x6, starting transfers between devices: 10.3 us -> 8.24 us  [the longest x2 7.11 us: exchange(): lax.ppermute(odd, 'gy', pairs(1))]
    ppermute x4, starting transfers between devices: 7.84 us -> 9.27 us  [crossing(): return lax.ppermute(shear, ('gx', 'gy'), pairs)]
  transfers between devices with their start and end apart: 10 -> 10, of which waited for: 0 -> 0; matrix products, arithmetic and copies ran while one was open for 0% -> 0% of each run, Pallas kernels for 36% -> 40%
where the time goes in v3:
time: 50.7 us; the launch traced here: 50.1 us
  Pallas kernels  29.9 us (59%)
  starting transfers between devices  17.5 us (35%)
  between operations  1.58 us (3%)
  loops' own time  0.87 us (2%)
    pallas_call x5, Pallas kernels, call(): pl.pallas_call(kernel, name=name, out_shape=[jax.ShapeDtypeStruct(s, jnp....  29.9 us
    ppermute x4, starting transfers between devices, crossing(): return lax.ppermute(shear, ('gx', 'gy'), pairs)  9.27 us
    ppermute x2, starting transfers between devices, exchange(): lax.ppermute(odd, 'gy', pairs(1))  7.11 us
  transfers between devices with their start and end apart: 10, of which 0 were waited for; matrix products, arithmetic and copies ran while one was open for 0% of the time, Pallas kernels for 40%

profile of v3, /device:TPU:1, one launch (start us, length us, event | category | flops | bytes accessed | tf_op | source)
XLA Modules:
  0.0 50.1 jit_solution(705745408326648790)
XLA Ops:
  1.3 0.1 pad_add_fusion.flags
  1.4 0.1 pad_maximum_fusion.weights
  1.5 0.1 pad_maximum_fusion.1.radial0
  1.6 3.1 %prepare.1 = (f32[8,32,16,128]{3,2,1,0:T(8,128)S(1)}, f32[8,5,144,128]{3,2,1,0:T(8,128)S(1)}, f32[8,24,128]{2,1,0:T(8,128)S(1)}, f32[8,8,128]{2,1,0:T(8,128)S(1)...) custom-call(s32[4]{0:T(128)S(1)} %pad_add_fusion.flags, ...), custom_call_target="tpu_custom_call" | custom-call | tf_op jit(solution)/shard_map/prepare/pallas_call | solution.py:538
  4.7 41.1 %conditional.1 = (f32[8,32,16,128]{3,2,1,0:T(8,128)S(1)}, f32[8,5,144,128]{3,2,1,0:T(8,128)S(1)}, f32[8,6,16,128]{3,2,1,0:T(8,128)S(1)}, f32[8,24,128]{2,1,0:T(8...) conditional(s32[]{:T(128)} %clamp.3, (f32[2]{0:T(128)S(1)}, ...), branch_computations={%region_0.1_spmd, %region_1.2_spmd, %region_2.3_spmd, %region_3.4_... | conditional | bytes 3670488 | solution.py:623
  4.7 0.1 collective-permute-start.44
  4.8 3.6 %collective-permute-start.43 = (f32[8,2,16,128]{3,2,1,0:T(8,128)S(1)}, f32[8,2,16,128]{3,2,1,0:T(8,128)S(1)}, u32[]{:S(2)}, u32[]{:S(2)}) collective-permute-start(f32[8,2,16,128]{3,2,1,0:T(8,128)S(1)} %get-tuple-element.446), channel_id=1, source_target_pairs={{16,5},{0,27},{17,6},{1,28},{18,7},{2,29},{19,8},{3,30},{20,9},{4,... | collective-permute-start | bytes 393224 | tf_op jit(solution)/shard_map/cond/branch_4_fun/ppermute | solution.py:572
  8.5 3.6 %collective-permute-start.42 = (f32[8,2,16,128]{3,2,1,0:T(8,128)S(1)}, f32[8,2,16,128]{3,2,1,0:T(8,128)S(1)}, u32[]{:S(2)}, u32[]{:S(2)}) collective-permute-start(f32[8,2,16,128]{3,2,1,0:T(8,128)S(1)} %get-tuple-element.446), channel_id=1, source_target_pairs={{16,4},{0,28},{17,5},{1,29},{18,6},{2,30},{19,7},{3,31},{20,8},{4,... | collective-permute-start | bytes 393224 | tf_op jit(solution)/shard_map/cond/branch_4_fun/ppermute | solution.py:572
  12.0 0.0 collective-permute-start.40
  12.0 4.1 %collective-permute-start.41 = (f32[8,8,128]{2,1,0:T(8,128)S(1)}, f32[8,8,128]{2,1,0:T(8,128)S(1)}, u32[]{:S(2)}, u32[]{:S(2)}) collective-permute-start(f32[8,8,128]{2,1,0:T(8,128)S(1)} %get-tuple-element.445), channel_id=1, source_target_pairs={{1,2},{3,4},{5,6},{7,8},{9,10},{11,12},{13,14},{15,0},{2,1},{4,3},... | collective-permute-start | bytes 98312 | tf_op jit(solution)/shard_map/cond/branch_4_fun/ppermute | solution.py:557
  16.2 9.8 %inner_1.20.refs_0_ = f32[8,5,144,128]{3,2,1,0:T(8,128)S(1)} custom-call(f32[2]{0:T(128)S(1)} %get-tuple-element.437.radial0, f32[8,32,16,128]{3,2,1,0:T(8,128)S(1)} %get-tuple-element.440.refs_0_.refs_1_, f32[8,5,144,128]{3,2,1,0:T(8,128)S(1)} %get-tuple-element.441.refs_1_), custom_call_target="tpu_custom_call" | custom-call | tf_op jit(solution)/shard_map/cond/branch_4_fun/inner_1/pallas_call | solution.py:538
  26.0 0.0 collective-permute-done.40.refs_3_
  26.0 0.0 collective-permute-done.41.refs_4_
  26.0 0.0 collective-permute-done.44.refs_7_
  26.0 0.0 collective-permute-done.43.refs_6_
  26.0 0.0 collective-permute-done.42.refs_5_
  26.0 2.9 %edge_1.20 = (f32[8,5,144,128]{3,2,1,0:T(8,128)S(1)}, f32[8,24,128]{2,1,0:T(8,128)S(1)}, f32[8,8,128]{2,1,0:T(8,128)S(1)}, f32[8,8,128]{2,1,0:T(8,128)S(1)}, f32...) custom-call(s32[4]{0:T(128)S(1)} %get-tuple-element.438.flags, ...), custom_call_target="tpu_custom_call", output_to_operand_aliasing={{0}: (2, {})} | custom-call | tf_op jit(solution)/shard_map/cond/branch_4_fun/edge_1/pallas_call | solution.py:538
  28.9 0.1 collective-permute-start.49
  29.0 0.1 collective-permute-start.48
  29.1 2.0 %collective-permute-start.47 = (f32[8,2,16,128]{3,2,1,0:T(8,128)S(1)}, f32[8,2,16,128]{3,2,1,0:T(8,128)}, u32[]{:S(2)}, u32[]{:S(2)}) collective-permute-start(f32[8,2,16,128]{3,2,1,0:T(8,128)S(1)} %get-tuple-element.455), channel_id=1, source_target_pairs={{16,4},{0,28},{17,5},{1,29},{18,6},{2,30},{19,7},{3,31},{20,8},{4,... | collective-permute-start | bytes 393224 | tf_op jit(solution)/shard_map/cond/branch_4_fun/ppermute | solution.py:572
  31.0 0.9 %collective-permute-start.45 = (f32[8,8,128]{2,1,0:T(8,128)S(1)}, f32[8,8,128]{2,1,0:T(8,128)}, u32[]{:S(2)}, u32[]{:S(2)}) collective-permute-start(f32[8,8,128]{2,1,0:T(8,128)S(1)} %get-tuple-element.453), channel_id=1, source_target_pairs={{0,1},{2,3},{4,5},{6,7},{8,9},{10,11},{12,13},{14,15},{1,0},{3,2},... | collective-permute-start | bytes 98312 | tf_op jit(solution)/shard_map/cond/branch_4_fun/ppermute | solution.py:557
  32.0 3.0 %collective-permute-start.46 = (f32[8,8,128]{2,1,0:T(8,128)S(1)}, f32[8,8,128]{2,1,0:T(8,128)}, u32[]{:S(2)}, u32[]{:S(2)}) collective-permute-start(f32[8,8,128]{2,1,0:T(8,128)S(1)} %get-tuple-element.454), channel_id=1, source_target_pairs={{1,2},{3,4},{5,6},{7,8},{9,10},{11,12},{13,14},{15,0},{2,1},{4,3},... | collective-permute-start | bytes 98312 | tf_op jit(solution)/shard_map/cond/branch_4_fun/ppermute | solution.py:557
  35.0 10.0 %inner_2.20 = (f32[8,32,16,128]{3,2,1,0:T(8,128)S(1)}, f32[8,5,144,128]{3,2,1,0:T(8,128)S(1)}) custom-call(f32[2]{0:T(128)S(1)} %get-tuple-element.437.radial0, f32[8,5,144,128]{3,2,1,0:T(8,128)S(1)} %get-tuple-element.448.refs_0_, f32[8,32,16,128]{3,2,1,0:T(8,128)S(1)} %get-tuple-element.440.refs_0_.refs_1_), custom_call_target="tpu_custom_call" | custom-call | tf_op jit(solution)/shard_map/cond/branch_4_fun/inner_2/pallas_call | solution.py:538
  45.0 0.0 collective-permute-done.45
  45.0 0.0 collective-permute-done.46
  45.0 0.0 collective-permute-done.49
  45.0 0.0 collective-permute-done.48
  45.0 0.0 collective-permute-done.47
  45.8 4.1 %edge_2.1 = f32[8,32,16,128]{3,2,1,0:T(8,128)} custom-call(s32[4]{0:T(128)S(1)} %pad_add_fusion.flags, f32[3]{0:T(128)S(1)} %pad_maximum_fusion.weights, f32[8,32,16,128]{3,2,1,0:T(8,128)S(1)} %get-tuple-element.702.refs_0_, f32[8,5,144,128]{3,2,1,0:T(8,128)S(1)} %get-tuple-element.703.refs_1_, f32[8,6,16,128]{3,2,1,0:T(8,128)S(1)} %get-tuple-element.704.refs_2_, ...), custom_call_target="tpu_custom_call" | custom-call | tf_op jit(solution)/shard_map/edge_2/pallas_call | solution.py:538
Async XLA Ops:
  4.7 21.3 %collective-permute-start.44 = (f32[8,2,16,128]{3,2,1,0:T(8,128)S(1)}, f32[8,2,16,128]{3,2,1,0:T(8,128)S(1)}, u32[]{:S(2)}, u32[]{:S(2)}) collective-permute-start(f32[8,2,16,128]{3,2,1,0:T(8,128)S(1)} %get-tuple-element.447), channel_id=1, source_target_pairs={{0,16},{16,0},{1,17},{17,1},{2,18},{18,2},{3,19},{19,3},{4,20},{20... | collective-permute-start | bytes 393224 | tf_op jit(solution)/shard_map/cond/branch_4_fun/ppermute | solution.py:559
  4.8 21.2 %collective-permute-start.43 = (f32[8,2,16,128]{3,2,1,0:T(8,128)S(1)}, f32[8,2,16,128]{3,2,1,0:T(8,128)S(1)}, u32[]{:S(2)}, u32[]{:S(2)}) collective-permute-start(f32[8,2,16,128]{3,2,1,0:T(8,128)S(1)} %get-tuple-element.446), channel_id=1, source_target_pairs={{16,5},{0,27},{17,6},{1,28},{18,7},{2,29},{19,8},{3,30},{20,9},{4,... | collective-permute-start | bytes 393224 | tf_op jit(solution)/shard_map/cond/branch_4_fun/ppermute | solution.py:572
  8.5 17.5 %collective-permute-start.42 = (f32[8,2,16,128]{3,2,1,0:T(8,128)S(1)}, f32[8,2,16,128]{3,2,1,0:T(8,128)S(1)}, u32[]{:S(2)}, u32[]{:S(2)}) collective-permute-start(f32[8,2,16,128]{3,2,1,0:T(8,128)S(1)} %get-tuple-element.446), channel_id=1, source_target_pairs={{16,4},{0,28},{17,5},{1,29},{18,6},{2,30},{19,7},{3,31},{20,8},{4,... | collective-permute-start | bytes 393224 | tf_op jit(solution)/shard_map/cond/branch_4_fun/ppermute | solution.py:572
  12.0 13.9 %collective-permute-start.40 = (f32[8,8,128]{2,1,0:T(8,128)S(1)}, f32[8,8,128]{2,1,0:T(8,128)S(1)}, u32[]{:S(2)}, u32[]{:S(2)}) collective-permute-start(f32[8,8,128]{2,1,0:T(8,128)S(1)} %get-tuple-element.444), channel_id=1, source_target_pairs={{0,1},{2,3},{4,5},{6,7},{8,9},{10,11},{12,13},{14,15},{1,0},{3,2},... | collective-permute-start | bytes 98312 | tf_op jit(solution)/shard_map/cond/branch_4_fun/ppermute | solution.py:557
  12.0 13.9 %collective-permute-start.41 = (f32[8,8,128]{2,1,0:T(8,128)S(1)}, f32[8,8,128]{2,1,0:T(8,128)S(1)}, u32[]{:S(2)}, u32[]{:S(2)}) collective-permute-start(f32[8,8,128]{2,1,0:T(8,128)S(1)} %get-tuple-element.445), channel_id=1, source_target_pairs={{1,2},{3,4},{5,6},{7,8},{9,10},{11,12},{13,14},{15,0},{2,1},{4,3},... | collective-permute-start | bytes 98312 | tf_op jit(solution)/shard_map/cond/branch_4_fun/ppermute | solution.py:557
  28.9 16.1 %collective-permute-start.49 = (f32[8,2,16,128]{3,2,1,0:T(8,128)S(1)}, f32[8,2,16,128]{3,2,1,0:T(8,128)}, u32[]{:S(2)}, u32[]{:S(2)}) collective-permute-start(f32[8,2,16,128]{3,2,1,0:T(8,128)S(1)} %get-tuple-element.456), channel_id=1, source_target_pairs={{0,16},{16,0},{1,17},{17,1},{2,18},{18,2},{3,19},{19,3},{4,20},{20... | collective-permute-start | bytes 393224 | tf_op jit(solution)/shard_map/cond/branch_4_fun/ppermute | solution.py:559
  29.0 16.1 %collective-permute-start.48 = (f32[8,2,16,128]{3,2,1,0:T(8,128)S(1)}, f32[8,2,16,128]{3,2,1,0:T(8,128)}, u32[]{:S(2)}, u32[]{:S(2)}) collective-permute-start(f32[8,2,16,128]{3,2,1,0:T(8,128)S(1)} %get-tuple-element.455), channel_id=1, source_target_pairs={{16,5},{0,27},{17,6},{1,28},{18,7},{2,29},{19,8},{3,30},{20,9},{4,... | collective-permute-start | bytes 393224 | tf_op jit(solution)/shard_map/cond/branch_4_fun/ppermute | solution.py:572
  29.1 16.0 %collective-permute-start.47 = (f32[8,2,16,128]{3,2,1,0:T(8,128)S(1)}, f32[8,2,16,128]{3,2,1,0:T(8,128)}, u32[]{:S(2)}, u32[]{:S(2)}) collective-permute-start(f32[8,2,16,128]{3,2,1,0:T(8,128)S(1)} %get-tuple-element.455), channel_id=1, source_target_pairs={{16,4},{0,28},{17,5},{1,29},{18,6},{2,30},{19,7},{3,31},{20,8},{4,... | collective-permute-start | bytes 393224 | tf_op jit(solution)/shard_map/cond/branch_4_fun/ppermute | solution.py:572
  31.0 14.0 %collective-permute-start.45 = (f32[8,8,128]{2,1,0:T(8,128)S(1)}, f32[8,8,128]{2,1,0:T(8,128)}, u32[]{:S(2)}, u32[]{:S(2)}) collective-permute-start(f32[8,8,128]{2,1,0:T(8,128)S(1)} %get-tuple-element.453), channel_id=1, source_target_pairs={{0,1},{2,3},{4,5},{6,7},{8,9},{10,11},{12,13},{14,15},{1,0},{3,2},... | collective-permute-start | bytes 98312 | tf_op jit(solution)/shard_map/cond/branch_4_fun/ppermute | solution.py:557
  32.0 13.0 %collective-permute-start.46 = (f32[8,8,128]{2,1,0:T(8,128)S(1)}, f32[8,8,128]{2,1,0:T(8,128)}, u32[]{:S(2)}, u32[]{:S(2)}) collective-permute-start(f32[8,8,128]{2,1,0:T(8,128)S(1)} %get-tuple-element.454), channel_id=1, source_target_pairs={{1,2},{3,4},{5,6},{7,8},{9,10},{11,12},{13,14},{15,0},{2,1},{4,3},... | collective-permute-start | bytes 98312 | tf_op jit(solution)/shard_map/cond/branch_4_fun/ppermute | solution.py:557

commit v4 on v3

--- a/solution.py
+++ b/solution.py
@@ -20,50 +20,47 @@
     return x * lax.rsqrt(jnp.maximum(x, TINY))
 
 
-def side(state, normal):
-    rho, pressure = state[0], state[7]
-    vel, mag = state[1:4], state[4:7]
-    one, two = [c for c in range(3) if c != normal]
-    mom = [rho * v for v in vel]
-    vn, bn = vel[normal], mag[normal]
-    mn = mom[normal]
-    mnvn = mn * vn
-    kinetic = 0.5 * ((mnvn + mom[one] * vel[one]) + mom[two] * vel[two])
-    bn2 = bn * bn
-    bt2 = mag[one] * mag[one] + mag[two] * mag[two]
+def signal(state, normal):
+    rho, pressure, vn = state[0], state[7], state[1 + normal]
+    one, two = [4 + c for c in range(3) if c != normal]
+    bn2 = state[4 + normal] * state[4 + normal]
+    bt2 = state[one] * state[one] + state[two] * state[two]
     half_b2 = 0.5 * (bt2 + bn2)
-    inner = kinetic + 1.5 * pressure
-    energy = inner + half_b2
-    ind_one = vn * mag[one] - bn * vel[one]
-    ind_two = vn * mag[two] - bn * vel[two]
-    flux = [None] * FIELDS
-    flux[0] = mn
-    flux[1 + normal] = mnvn + (pressure + half_b2) - bn2
-    flux[1 + one] = mn * vel[one] - bn * mag[one]
-    flux[1 + two] = mn * vel[two] - bn * mag[two]
-    flux[4 + one] = ind_one
-    flux[4 + two] = ind_two
-    flux[7] = vn * (inner + pressure) + (mag[one] * ind_one + mag[two] * ind_two)
-    cons = [rho] + mom + list(mag) + [energy]
     half_gp = (0.5 * GAMMA) * pressure
     spread = half_gp - half_b2
     disc = spread * spread + (GAMMA * pressure) * bt2
     fast = (half_gp + half_b2) + root(disc)
-    speed = jnp.abs(vn) + fast * lax.rsqrt(jnp.maximum(rho * fast, TINY))
-    return flux, cons, speed
+    return jnp.abs(vn) + fast * lax.rsqrt(jnp.maximum(rho * fast, TINY)), bn2 - half_b2
+
+
+def carried(state, normal, speed, excess):
+    rho, pressure = state[0], state[7]
+    vel, mag = state[1:4], state[4:7]
+    one, two = [c for c in range(3) if c != normal]
+    vn, bn = vel[normal], mag[normal]
+    pace = vn + speed
+    mass = rho * pace
+    inner = (0.5 * rho) * (vn * vn + vel[one] * vel[one] + vel[two] * vel[two]) + 1.5 * pressure
+    out = [None] * FIELDS
+    out[0] = mass
+    out[1 + normal] = mass * vn + (pressure - excess)
+    out[1 + one] = mass * vel[one] - bn * mag[one]
+    out[1 + two] = mass * vel[two] - bn * mag[two]
+    out[4 + one] = pace * mag[one] - bn * vel[one]
+    out[4 + two] = pace * mag[two] - bn * vel[two]
+    work = (pace * inner + vn * pressure) + speed * excess
+    out[7] = work + (mag[one] * out[4 + one] + mag[two] * out[4 + two])
+    return out
 
 
 def face(left, right, normal):
-    fl, ul, sl = side(left, normal)
-    fr, ur, sr = side(right, normal)
-    speed = jnp.maximum(sl, sr)
-    out = []
-    for f in range(FIELDS):
-        if fl[f] is None:
-            out.append(speed * (ul[f] - ur[f]))
-        else:
-            out.append((fl[f] + fr[f]) - speed * (ur[f] - ul[f]))
-    return out
+    speed_left, excess_left = signal(left, normal)
+    speed_right, excess_right = signal(right, normal)
+    speed = jnp.maximum(speed_left, speed_right)
+    one = carried(left, normal, speed, excess_left)
+    two = carried(right, normal, -speed, excess_right)
+    field = 4 + normal
+    return [speed * (left[f] - right[f]) if f == field else one[f] + two[f] for f in range(FIELDS)]
 
 
 def limited(up, down):
@@ -86,6 +83,18 @@
     return [u[0]] + vel + list(u[4:7]) + [(GAMMA - 1.0) * (u[7] - kinetic - magnetic)]
 
 
+def whereabouts(rows):
+    count_x = lax.axis_size("gx")
+    row = lax.axis_index("gx")
+    total = rows * count_x
+    radial = (row * rows).astype(jnp.float32) + (0.5 - 0.5 * total)
+    return radial, 1.0 / (SHEAR_Q * total), row == 0, row == count_x - 1
+
+
+def at_even_block():
+    return lax.rem(lax.axis_index("gy"), 2) == 0
+
+
 def lanes_of(shape):
     return lax.broadcasted_iota(jnp.int32, shape, 1)
 
@@ -107,9 +116,9 @@
     wt_ref[f, g, rows - PAD : rows] = wt_ref[f, g, rows - 2 * PAD : rows - PAD]
 
 
-def send_columns(flags, groups, wt_ref, cols_ref, even_ref, odd_ref):
+def send_columns(groups, wt_ref, cols_ref, even_ref, odd_ref):
     rows = wt_ref.shape[2]
-    even = flags[3] == 1
+    even = at_even_block()
     cells = [PAD, PAD + 1, PAD + 2, rows - PAD - 3, rows - PAD - 2, rows - PAD - 1]
 
     def body(f, carry):
@@ -125,8 +134,8 @@
     lax.fori_loop(0, FIELDS, body, 0)
 
 
-def send_rows(flags, rows_ref, shear_ref, *swap_refs):
-    first = flags[0] == 1
+def send_rows(rows, rows_ref, shear_ref, *swap_refs):
+    _, _, first, _ = whereabouts(rows)
 
     def body(k, carry):
         low, high = load_row(rows_ref, k), load_row(rows_ref, 4 + k)
@@ -145,9 +154,10 @@
     lax.fori_loop(0, 2, body, 0)
 
 
-def prepare_kernel(flags, radial0, rho_hbm, vel_hbm, mag_hbm, pres_hbm, w_ref, wt_ref, cols_ref, even_ref, odd_ref, rows_ref, *rest):
+def prepare_kernel(rho_hbm, vel_hbm, mag_hbm, pres_hbm, w_ref, wt_ref, cols_ref, even_ref, odd_ref, rows_ref, *rest):
     *sends, sems = rest
     rows = w_ref.shape[1]
+    radial, omega, _, _ = whereabouts(rows)
     parts = sems.shape[1]
     size = rows // parts
     copies = []
@@ -167,7 +177,7 @@
         for copy in copies[part]:
             copy.wait()
         for i in range(part * size, (part + 1) * size):
-            w_ref[2, i] = w_ref[2, i] - radial0[1] * (radial0[0] + float(i))
+            w_ref[2, i] = w_ref[2, i] - (SHEAR_Q * omega) * (radial + float(i))
 
         def turn_fields(n, carry, part=part):
             for f in range(4):
@@ -175,7 +185,7 @@
             return carry
 
         lax.fori_loop(0, FIELDS // 4, turn_fields, 0)
-    send_columns(flags, parts, wt_ref, cols_ref, even_ref, odd_ref)
+    send_columns(parts, wt_ref, cols_ref, even_ref, odd_ref)
 
     def copy(f, carry):
         rows_ref[f, 0:3] = w_ref[f, 0:3]
@@ -183,7 +193,7 @@
         return carry
 
     lax.fori_loop(0, FIELDS, copy, 0)
-    send_rows(flags, rows_ref, *sends)
+    send_rows(rows, rows_ref, *sends)
 
 
 def three_states(cells):
@@ -205,28 +215,24 @@
         ref[f, 8 + high : 16 + high] = value[0:8]
 
 
-def behind(ref, f, value):
-    high = value.shape[0]
-    ref[f, 8 : 8 + high] = value
-    result = ref[f, 7 : 7 + high]
-    ref[f, 0:8] = value[high - 8 : high]
-    return result
-
-
-def interior_kernel(second, radial0, *refs):
+def behind(ref, f, at, value):
+    ref[f, pl.ds(at, value.shape[0])] = value
+    return ref[f, pl.ds(at - 1, value.shape[0])]
+
+
+def interior_kernel(second, *refs):
     if second:
         wt_ref, w0_ref, v_ref, dy_ref, w_ref, *refs = refs
     else:
         w_ref, wt_ref, vt_ref, v_ref, *refs = refs
         dy_ref = vt_ref
-    hz_ref, rz_ref, fz_ref, wl_ref, dx_ref, fx_ref = refs
+    hz_ref, rz_ref, fz_ref, wl_ref, dx_ref, fx_ref, uy_ref, ly_ref, fy_ref = refs
     rows, high, width = w_ref.shape[1:]
     per_group = width // high
     groups = rows // per_group
     step = 0.5 * TIME_STEP if second else TIME_STEP
     coef = 0.5 * step
-    omega_q = radial0[1]
-    omega = omega_q / SHEAR_Q
+    radial, omega, _, _ = whereabouts(rows)
     next_row, last_row = slice(9, 9 + high), slice(7, 7 + high)
     early = per_group + 1
 
@@ -273,13 +279,13 @@
             v_ref[f, before] = v_ref[f, before] - (here - fx_ref[f])
             fx_ref[f] = here
 
-        x = radial0[0] + i.astype(jnp.float32)
+        x = radial + i.astype(jnp.float32)
         cons = to_conserved(w)
         if second:
             base = [0.5 * (a + b) for a, b in zip(to_conserved(load_row(w0_ref, i)), cons)]
         else:
             base = cons
-        tidal = 2.0 * omega * omega_q * x
+        tidal = (2.0 * SHEAR_Q * omega * omega) * x
         value = [base[f] - coef * total[f] for f in range(FIELDS)]
         value[1] = value[1] + ((step * 2.0) * omega * cons[2] + (step * tidal) * cons[0])
         value[2] = value[2] - ((step * 2.0) * omega) * cons[1]
@@ -288,30 +294,31 @@
             v_ref[f, i] = value[f]
         return carry
 
-    size = groups * width // rows
+    size = 2 * groups * width // rows
     strips = width // size
     row = lax.broadcasted_iota(jnp.int32, (size, width), 0)
 
     def body_y(n, carry):
-        if second:
-            turn_state(n)
-        else:
-            turn_result(rows - early + n)
+        for m in (2 * n, 2 * n + 1):
+            if second:
+                turn_state(m)
+            else:
+                turn_result(rows - early + m)
         g, start = lax.div(n, strips), size * lax.rem(n, strips)
         at = pl.multiple_of(start + PAD, 8)
         left, right = [], []
         for f in range(FIELDS):
             w = wt_ref[f, g, pl.ds(at, size)]
             up = 0.5 * (wt_ref[f, g, pl.ds(at + 1, size)] - w)
-            slope = limited(up, behind(hz_ref, f, up))
-            left.append(behind(rz_ref, f, w + slope))
+            slope = limited(up, behind(uy_ref, f, at, up))
+            left.append(behind(ly_ref, f, at, w + slope))
             right.append(w - slope)
         fy = face(left, right, 1)
         cell = row + start
         scale = jnp.where(jnp.logical_and(cell >= 2, cell <= width - 2), coef, 0.0)
         for f in range(FIELDS):
             here = scale * fy[f]
-            change = here - behind(fz_ref, f, here)
+            change = here - behind(fy_ref, f, at, here)
             if second:
                 dy_ref[f, g, pl.ds(at - 1, size)] = change
             else:
@@ -320,10 +327,10 @@
 
     def azimuthal():
         for f in range(FIELDS):
-            hz_ref[f, 0:8] = jnp.zeros((8, width), jnp.float32)
-            rz_ref[f, 0:8] = wt_ref[f, 0, PAD : 2 * PAD]
-            fz_ref[f, 0:8] = jnp.zeros((8, width), jnp.float32)
-        lax.fori_loop(0, rows, body_y, 0)
+            uy_ref[f, 0:PAD] = jnp.zeros((PAD, width), jnp.float32)
+            ly_ref[f, 0:PAD] = wt_ref[f, 0, PAD : 2 * PAD]
+            fy_ref[f, 0:PAD] = jnp.zeros((PAD, width), jnp.float32)
+        lax.fori_loop(0, rows // 2, body_y, 0)
 
     def others():
         for f in range(FIELDS):
@@ -342,11 +349,16 @@
         azimuthal()
 
 
-def sheared_rows(flags, weights, near_ref, next_ref, ghost_ref):
-    first = flags[0] == 1
+def sheared_rows(first, shear_ref, near_ref, next_ref, ghost_ref):
     high, width = near_ref.shape[2:]
-    start = flags[2]
+    rest = lax.rem(shear_ref[0], width)
+    start = jnp.where(first, width - 1 - rest, rest)
     back = lax.rem(width - start, width)
+    weight = shear_ref[1].astype(jnp.float32) * WEIGHT_SCALE
+    other = 1.0 - weight
+    ahead = jnp.where(first, 1.0 - weight, 1.0 - other)
+    here = jnp.where(first, weight, other)
+    delta = jnp.where(first, 1.0, -1.0)
     lane = lanes_of((high, width))
 
     def body(k, carry):
@@ -356,10 +368,9 @@
             one = jnp.where(first, following, near)
             two = jnp.where(first, near, following)
             one_up, two_up = pltpu.roll(one, width - 1, 1), pltpu.roll(two, width - 1, 1)
-            one = weights[0] * jnp.where(lane < width - 1, one_up, two_up) + weights[1] * one
-            two = weights[0] * two_up + weights[1] * two
+            one = ahead * jnp.where(lane < width - 1, one_up, two_up) + here * one
+            two = ahead * two_up + here * two
             ghost.append(jnp.where(lane < width - start, pltpu.roll(one, back, 1), pltpu.roll(two, back, 1)))
-        delta = weights[2]
         boosted = list(ghost)
         boosted[2] = ghost[2] + ghost[0] * delta
         boosted[7] = ghost[7] + ghost[2] * delta + 0.5 * ghost[0] * delta * delta
@@ -371,16 +382,18 @@
     lax.fori_loop(0, 2, body, 0)
 
 
-def edge_kernel(second, beside, flags, weights, *refs):
+def edge_kernel(second, beside, shear_any, *refs):
+    *refs, shear_smem, shear_sem = refs
+    shear_copy = pltpu.make_async_copy(shear_any, shear_smem, shear_sem)
+    shear_copy.start()
     if second:
-        v_ref, dy_ref, *refs = refs
+        v_ref, dy_ref, rows_ref, cols_ref, ends_ref, slabs_ref, out_hbm, *refs = refs
+        e_ref, a_ref, c_ref, x_ref, ghost_ref, out_ref, sems = refs
+        even_ref, odd_ref = ends_ref.at[0], ends_ref.at[1]
+        near_ref, next_ref, xl_ref, xr_ref = (slabs_ref.at[k] for k in (0, 1, 2, 1 + beside))
     else:
-        vt_ref, *refs = refs
-    rows_ref, cols_ref, even_ref, odd_ref, near_ref, next_ref, *refs = refs
-    xl_ref, xr_ref = refs[0], refs[beside - 1]
-    if second:
-        out_hbm, e_ref, a_ref, c_ref, x_ref, ghost_ref, out_ref, sems = refs[beside:]
-    else:
+        vt_ref, rows_ref, cols_ref, even_ref, odd_ref, near_ref, next_ref, *refs = refs
+        xl_ref, xr_ref = refs[0], refs[beside - 1]
         w1_ref, cols1_ref, even1_ref, odd1_ref, rows1_ref, *sends, e_ref, a_ref, c_ref, x_ref, ghost_ref = refs[beside:]
     high, width = rows_ref.shape[2:]
     groups = cols_ref.shape[1] // 6
@@ -388,7 +401,8 @@
     rows = groups * size
     step = 0.5 * TIME_STEP if second else TIME_STEP
     coef = 0.5 * step
-    first, last, even = flags[0] == 1, flags[1] == 1, flags[3] == 1
+    _, _, first, last = whereabouts(rows)
+    even = at_even_block()
 
     def gather(f, carry):
         for k in range(2):
@@ -423,7 +437,8 @@
 
         lax.fori_loop(0, FIELDS, scatter, 0)
 
-    sheared_rows(flags, weights, near_ref, next_ref, ghost_ref)
+    shear_copy.wait()
+    sheared_rows(first, shear_smem, near_ref, next_ref, ghost_ref)
     def place(f, carry):
         x_ref[0, f, 0:2] = jnp.where(first, ghost_ref[f], xl_ref[f])
         x_ref[1, f, 3:5] = jnp.where(last, ghost_ref[f], xr_ref[f])
@@ -493,8 +508,8 @@
             return carry
 
         lax.fori_loop(0, FIELDS // batch, turn_rows, 0)
-        send_columns(flags, groups, w1_ref, cols1_ref, even1_ref, odd1_ref)
-        send_rows(flags, rows1_ref, *sends)
+        send_columns(groups, w1_ref, cols1_ref, even1_ref, odd1_ref)
+        send_rows(rows, rows1_ref, *sends)
         return
 
     def finish(n, carry):
@@ -529,8 +544,19 @@
         pltpu.make_async_copy(out_ref.at[part, at], out_hbm.at[part, at], sems.at[n]).wait()
 
 
-def call(kernel, name, scalars, arrays, shapes, scratch=(), in_hbm=False, out_hbm=False, aliases=None):
-    smem = pl.BlockSpec(memory_space=pltpu.SMEM)
+def gather_kernel(even_ref, odd_ref, *refs):
+    *slabs, ends_ref, slabs_ref = refs
+
+    def body(f, carry):
+        ends_ref[0, f], ends_ref[1, f] = even_ref[f], odd_ref[f]
+        for k, ref in enumerate(slabs):
+            slabs_ref[k, f] = ref[f]
+        return carry
+
+    lax.fori_loop(0, FIELDS, body, 0)
+
+
+def call(kernel, name, arrays, shapes, scratch=(), in_hbm=False, out_hbm=False, aliases=None, shear=()):
     vmem = pl.BlockSpec(memory_space=pltpu.VMEM)
     hbm = pl.BlockSpec(memory_space=pltpu.HBM)
     if in_hbm:
@@ -539,12 +565,12 @@
         kernel,
         name=name,
         out_shape=[jax.ShapeDtypeStruct(s, jnp.float32) for s in shapes],
-        in_specs=[smem] * len(scalars) + [hbm if in_hbm else vmem] * len(arrays),
+        in_specs=[pl.BlockSpec(memory_space=pl.ANY)] * len(shear) + [hbm if in_hbm else vmem] * len(arrays),
         out_specs=[hbm if out_hbm else vmem] * len(shapes),
         scratch_shapes=[pltpu.VMEM(s, jnp.float32) if isinstance(s, tuple) else s for s in scratch],
         input_output_aliases=aliases or {},
         compiler_params=pltpu.CompilerParams(vmem_limit_bytes=20 * 1024 * 1024),
-    )(*scalars, *arrays)
+    )(*shear, *arrays)
 
 
 def exchange(even, odd, swap):
@@ -576,7 +602,8 @@
     high, width = full[2:]
     tile = (FIELDS, high, width)
     padded = (FIELDS, high + 2 * PAD, width)
-    return [padded, padded, padded, tile, tile, tile]
+    column = (FIELDS, PAD + width, width)
+    return [padded] * 3 + [tile] * 3 + [column] * 3
 
 
 def edge_scratch(full, groups):
@@ -587,76 +614,60 @@
         (FIELDS, groups, 2 * PAD, width),
         (2, FIELDS, 5, high, width),
         (FIELDS, 2, high, width),
+        pltpu.SMEM((2,), jnp.int32),
+        pltpu.SemaphoreType.DMA,
     ]
 
 
-def sections(block, flags, weights, radial0, w0, wt0, cols, even, odd, rows, shear, *swap):
+def sections(block, drift, w0, wt0, cols, even, odd, rows, shear, *swap):
     full, turned = w0.shape, wt0.shape
     groups = cols.shape[1] // 6
     sends = [x.shape for x in (cols, even, odd, rows, shear, *swap)]
     scratch = edge_scratch(full, groups)
+    received = [(2,) + even.shape, (2 + (1 if len(swap) == 1 else 2),) + shear.shape]
 
     def branch(by):
-        def run(flags, weights, radial0, w0, wt0, cols, even, odd, rows, shear, *swap):
+        def run(drift, w0, wt0, cols, even, odd, rows, shear, *swap):
             even, odd, *beside = exchange(even, odd, swap)
             sheared = crossing(by, shear), crossing(by + 1, shear)
             kernel = functools.partial(interior_kernel, False)
-            (vt,) = call(kernel, "inner_1", [radial0], [w0, wt0], [turned], [full] + inner_scratch(full))
+            (vt,) = call(kernel, "inner_1", [w0, wt0], [turned], [full] + inner_scratch(full))
             wt1, cols, even, odd, rows, shear, *swap = call(
                 functools.partial(edge_kernel, False, len(beside)),
                 "edge_1",
-                [flags, weights],
                 [vt, rows, cols, even, odd, *sheared, *beside],
                 [turned] + sends,
                 scratch,
-                aliases={2: 0},
+                aliases={1: 0},
+                shear=[drift],
             )
             even, odd, *beside = exchange(even, odd, swap)
             sheared = crossing(by, shear), crossing(by + 1, shear)
             kernel = functools.partial(interior_kernel, True)
-            v, dy = call(kernel, "inner_2", [radial0], [wt1, w0], [full, turned], [full] + inner_scratch(full))
-            return v, dy, rows, cols, even, odd, *sheared, *beside
+            v, dy = call(kernel, "inner_2", [wt1, w0], [full, turned], [full] + inner_scratch(full))
+            ends, slabs = call(gather_kernel, "gather", [even, odd, *sheared, *beside], received)
+            return v, dy, rows, cols, ends, slabs
 
         return run
 
     branches = [branch(by) for by in range(lax.axis_size("gy"))]
-    arrays = lax.switch(
-        block, branches, flags, weights, radial0, w0, wt0, cols, even, odd, rows, shear, *swap
-    )
+    arrays = lax.switch(block, branches, drift, w0, wt0, cols, even, odd, rows, shear, *swap)
     (out,) = call(
-        functools.partial(edge_kernel, True, 1 if lax.axis_size("gx") == 2 else 2),
+        functools.partial(edge_kernel, True, received[1][0] - 2),
         "edge_2",
-        [flags, weights],
         arrays,
         [full],
-        scratch + [full, pltpu.SemaphoreType.DMA((2 * groups,))],
+        scratch[:-2] + [full, pltpu.SemaphoreType.DMA((2 * groups,))] + scratch[-2:],
         out_hbm=True,
+        shear=[drift],
     )
     return out
 
 
 def on_device(density, velocity, bfield, pressure, shear_shift, remap_weight):
     rows, high, width = density.shape
-    count_x, count_y = lax.axis_size("gx"), lax.axis_size("gy")
-    total_x = rows * count_x
-    omega = 1.0 / (SHEAR_Q * total_x)
-    row = lax.axis_index("gx")
-    is_first, is_last = row == 0, row == count_x - 1
-    radial0 = (row * rows).astype(jnp.float32) + 0.5 - 0.5 * total_x
-    radial0 = jnp.stack([radial0, jnp.float32(SHEAR_Q * omega)])
-    weight = remap_weight.astype(jnp.float32) * WEIGHT_SCALE
-    block, rest = shear_shift // width, shear_shift % width
-    start = jnp.where(is_first, width - 1 - rest, rest)
-    even = 1 - lax.axis_index("gy") % 2
-    flags = jnp.stack([x.astype(jnp.int32) for x in (is_first, is_last, start, even)])
-    other = 1.0 - weight
-    weights = jnp.stack(
-        [
-            jnp.where(is_first, 1.0 - weight, 1.0 - other),
-            jnp.where(is_first, weight, other),
-            jnp.where(is_first, 1.0, -1.0),
-        ]
-    )
+    count_x = lax.axis_size("gx")
+    drift = jnp.stack([shear_shift, remap_weight])
     full = (FIELDS, rows, high, width)
     slab = (FIELDS, 2, high, width)
     groups = rows * high // width
@@ -667,13 +678,12 @@
     start_state = call(
         prepare_kernel,
         "prepare",
-        [flags, radial0],
         [density, velocity, bfield, pressure],
         [full, turned] + sends,
         [pltpu.SemaphoreType.DMA((4, groups))],
         in_hbm=True,
     )
-    return sections(block, flags, weights, radial0, *start_state)
+    return sections(shear_shift // width, drift, *start_state)
 
 
 def solution(mesh):

time: 50.7 us -> 46.3 us (0.913)
  Pallas kernels: 29.9 us -> 24.8 us
  starting transfers between devices: 17.5 us -> 18.2 us
    pallas_call x5 -> x6, Pallas kernels: 29.9 us -> 24.8 us  [call(): pl.pallas_call(kernel, name=name, out_shape=[jax.ShapeDtypeStruct(s, jnp....]
    ppermute x2, starting transfers between devices: 0.94 us -> 1.91 us  [exchange(): lax.ppermute(even, 'gy', pairs(0))]
    ppermute x2, starting transfers between devices: 7.11 us -> 6.29 us  [exchange(): lax.ppermute(odd, 'gy', pairs(1))]
    ppermute x2, starting transfers between devices: 0.19 us -> 0.9 us  [exchange(): return (even, odd, lax.ppermute(swap[0], 'gx', [(0, 1), (1, 0)]))]
  transfers between devices with their start and end apart: 10 -> 10, of which waited for: 0 -> 0; matrix products, arithmetic and copies ran while one was open for 0% -> 0% of each run, Pallas kernels for 40% -> 36%
where the time goes in v4:
time: 46.3 us; the launch traced here: 45.4 us
  Pallas kernels  24.8 us (54%)
  starting transfers between devices  18.2 us (39%)
  between operations  1.56 us (3%)
  loops' own time  0.69 us (1%)
    pallas_call x6, Pallas kernels, call(): pl.pallas_call(kernel, name=name, out_shape=[jax.ShapeDtypeStruct(s, jnp....  24.8 us
    ppermute x4, starting transfers between devices, crossing(): return lax.ppermute(shear, ('gx', 'gy'), pairs)  9.13 us
    ppermute x2, starting transfers between devices, exchange(): lax.ppermute(odd, 'gy', pairs(1))  6.29 us
    ppermute x2, starting transfers between devices, exchange(): lax.ppermute(even, 'gy', pairs(0))  1.91 us
  transfers between devices with their start and end apart: 10, of which 0 were waited for; matrix products, arithmetic and copies ran while one was open for 0% of the time, Pallas kernels for 36%

profile of v4, /device:TPU:1, one launch (start us, length us, event | category | flops | bytes accessed | tf_op | source)
XLA Modules:
  0.0 45.4 jit_solution(9982110408484416972)
XLA Ops:
  1.3 0.1 pad_add_fusion.shear_any
  1.4 2.6 %prepare.1 = (f32[8,32,16,128]{3,2,1,0:T(8,128)S(1)}, f32[8,5,144,128]{3,2,1,0:T(8,128)S(1)}, f32[8,24,128]{2,1,0:T(8,128)S(1)}, f32[8,8,128]{2,1,0:T(8,128)S(1)...) custom-call(f32[32,16,128]{2,1,0:T(8,128)} %rho_hbm.1, ...), custom_call_target="tpu_custom_call" | custom-call | tf_op jit(solution)/shard_map/prepare/pallas_call | solution.py:564
  4.0 37.9 %conditional.1 = (f32[8,32,16,128]{3,2,1,0:T(8,128)S(1)}, f32[8,5,144,128]{3,2,1,0:T(8,128)S(1)}, f32[8,6,16,128]{3,2,1,0:T(8,128)S(1)}, f32[8,24,128]{2,1,0:T(8...) conditional(s32[]{:T(128)} %clamp.3, ...), branch_computations={%region_0.1_spmd, %region_1.2_spmd, %region_2.3_spmd, %region_3.4_... | conditional | bytes 3670464 | solution.py:654
  4.2 0.1 collective-permute-start.84
  4.3 4.6 %collective-permute-start.83 = (f32[8,2,16,128]{3,2,1,0:T(8,128)S(1)}, f32[8,2,16,128]{3,2,1,0:T(8,128)S(1)}, u32[]{:S(2)}, u32[]{:S(2)}) collective-permute-start(f32[8,2,16,128]{3,2,1,0:T(8,128)S(1)} %get-tuple-element.460), channel_id=1, source_target_pairs={{16,9},{0,23},{17,10},{1,24},{18,11},{2,25},{19,12},{3,26},{20,13}... | collective-permute-start | bytes 393224 | tf_op jit(solution)/shard_map/cond/branch_8_fun/ppermute | solution.py:598
  9.0 2.6 %collective-permute-start.82 = (f32[8,2,16,128]{3,2,1,0:T(8,128)S(1)}, f32[8,2,16,128]{3,2,1,0:T(8,128)S(1)}, u32[]{:S(2)}, u32[]{:S(2)}) collective-permute-start(f32[8,2,16,128]{3,2,1,0:T(8,128)S(1)} %get-tuple-element.460), channel_id=1, source_target_pairs={{16,8},{0,24},{17,9},{1,25},{18,10},{2,26},{19,11},{3,27},{20,12},... | collective-permute-start | bytes 393224 | tf_op jit(solution)/shard_map/cond/branch_8_fun/ppermute | solution.py:598
  11.6 0.0 collective-permute-start.80
  11.6 3.2 %collective-permute-start.81 = (f32[8,8,128]{2,1,0:T(8,128)S(1)}, f32[8,8,128]{2,1,0:T(8,128)S(1)}, u32[]{:S(2)}, u32[]{:S(2)}) collective-permute-start(f32[8,8,128]{2,1,0:T(8,128)S(1)} %get-tuple-element.459), channel_id=1, source_target_pairs={{1,2},{3,4},{5,6},{7,8},{9,10},{11,12},{13,14},{15,0},{2,1},{4,3},... | collective-permute-start | bytes 98312 | tf_op jit(solution)/shard_map/cond/branch_8_fun/ppermute | solution.py:583
  14.8 8.0 %inner_1.24.refs_0_ = f32[8,5,144,128]{3,2,1,0:T(8,128)S(1)} custom-call(f32[8,32,16,128]{3,2,1,0:T(8,128)S(1)} %get-tuple-element.454.refs_0_.refs_1_, f32[8,5,144,128]{3,2,1,0:T(8,128)S(1)} %get-tuple-element.455.refs_1_), custom_call_target="tpu_custom_call" | custom-call | tf_op jit(solution)/shard_map/cond/branch_8_fun/inner_1/pallas_call | solution.py:564
  22.7 0.0 collective-permute-done.80.refs_3_
  22.8 0.0 collective-permute-done.81.refs_4_
  22.8 0.0 collective-permute-done.84.refs_7_
  22.8 0.0 collective-permute-done.83.refs_6_
  22.8 0.0 collective-permute-done.82.refs_5_
  22.8 2.7 %edge_1.24 = (f32[8,5,144,128]{3,2,1,0:T(8,128)S(1)}, f32[8,24,128]{2,1,0:T(8,128)S(1)}, f32[8,8,128]{2,1,0:T(8,128)S(1)}, f32[8,8,128]{2,1,0:T(8,128)S(1)}, f32...) custom-call(s32[2]{0:T(128)S(1)} %get-tuple-element.453.shear_any, ...), custom_call_target="tpu_custom_call", output_to_operand_aliasing={{0}: (1, {})} | custom-call | tf_op jit(solution)/shard_map/cond/branch_8_fun/edge_1/pallas_call | solution.py:564
  25.5 0.8 %collective-permute-start.89 = (f32[8,2,16,128]{3,2,1,0:T(8,128)S(1)}, f32[8,2,16,128]{3,2,1,0:T(8,128)S(1)}, u32[]{:S(2)}, u32[]{:S(2)}) collective-permute-start(f32[8,2,16,128]{3,2,1,0:T(8,128)S(1)} %get-tuple-element.470), channel_id=1, source_target_pairs={{0,16},{16,0},{1,17},{17,1},{2,18},{18,2},{3,19},{19,3},{4,20},{20... | collective-permute-start | bytes 393224 | tf_op jit(solution)/shard_map/cond/branch_8_fun/ppermute | solution.py:585
  26.3 0.1 collective-permute-start.88
  26.5 1.8 %collective-permute-start.87 = (f32[8,2,16,128]{3,2,1,0:T(8,128)S(1)}, f32[8,2,16,128]{3,2,1,0:T(8,128)S(1)}, u32[]{:S(2)}, u32[]{:S(2)}) collective-permute-start(f32[8,2,16,128]{3,2,1,0:T(8,128)S(1)} %get-tuple-element.469), channel_id=1, source_target_pairs={{16,8},{0,24},{17,9},{1,25},{18,10},{2,26},{19,11},{3,27},{20,12},... | collective-permute-start | bytes 393224 | tf_op jit(solution)/shard_map/cond/branch_8_fun/ppermute | solution.py:598
  28.2 1.9 %collective-permute-start.85 = (f32[8,8,128]{2,1,0:T(8,128)S(1)}, f32[8,8,128]{2,1,0:T(8,128)S(1)}, u32[]{:S(2)}, u32[]{:S(2)}) collective-permute-start(f32[8,8,128]{2,1,0:T(8,128)S(1)} %get-tuple-element.467), channel_id=1, source_target_pairs={{0,1},{2,3},{4,5},{6,7},{8,9},{10,11},{12,13},{14,15},{1,0},{3,2},... | collective-permute-start | bytes 98312 | tf_op jit(solution)/shard_map/cond/branch_8_fun/ppermute | solution.py:583
  30.1 3.1 %collective-permute-start.86 = (f32[8,8,128]{2,1,0:T(8,128)S(1)}, f32[8,8,128]{2,1,0:T(8,128)S(1)}, u32[]{:S(2)}, u32[]{:S(2)}) collective-permute-start(f32[8,8,128]{2,1,0:T(8,128)S(1)} %get-tuple-element.468), channel_id=1, source_target_pairs={{1,2},{3,4},{5,6},{7,8},{9,10},{11,12},{13,14},{15,0},{2,1},{4,3},... | collective-permute-start | bytes 98312 | tf_op jit(solution)/shard_map/cond/branch_8_fun/ppermute | solution.py:583
  33.2 8.2 %inner_2.24 = (f32[8,32,16,128]{3,2,1,0:T(8,128)S(1)}, f32[8,5,144,128]{3,2,1,0:T(8,128)S(1)}) custom-call(f32[8,5,144,128]{3,2,1,0:T(8,128)S(1)} %get-tuple-element.462.refs_0_, f32[8,32,16,128]{3,2,1,0:T(8,128)S(1)} %get-tuple-element.454.refs_0_.refs_1_), custom_call_target="tpu_custom_call" | custom-call | tf_op jit(solution)/shard_map/cond/branch_8_fun/inner_2/pallas_call | solution.py:564
  41.4 0.0 collective-permute-done.85.even_ref
  41.4 0.0 collective-permute-done.86.odd_ref
  41.4 0.0 collective-permute-done.89.refs_2_
  41.5 0.0 collective-permute-done.88.refs_1_
  41.5 0.0 collective-permute-done.87.refs_0_
  41.5 0.1 gather.24
  41.9 3.3 %edge_2.1 = f32[8,32,16,128]{3,2,1,0:T(8,128)} custom-call(s32[2]{0:T(128)S(1)} %pad_add_fusion.shear_any, f32[8,32,16,128]{3,2,1,0:T(8,128)S(1)} %get-tuple-element.635.refs_0_, f32[8,5,144,128]{3,2,1,0:T(8,128)S(1)} %get-tuple-element.636.refs_1_, f32[8,6,16,128]{3,2,1,0:T(8,128)S(1)} %get-tuple-element.637.refs_2_, ...), custom_call_target="tpu_custom_call" | custom-call | tf_op jit(solution)/shard_map/edge_2/pallas_call | solution.py:564
Async XLA Ops:
  4.2 18.6 %collective-permute-start.84 = (f32[8,2,16,128]{3,2,1,0:T(8,128)S(1)}, f32[8,2,16,128]{3,2,1,0:T(8,128)S(1)}, u32[]{:S(2)}, u32[]{:S(2)}) collective-permute-start(f32[8,2,16,128]{3,2,1,0:T(8,128)S(1)} %get-tuple-element.461), channel_id=1, source_target_pairs={{0,16},{16,0},{1,17},{17,1},{2,18},{18,2},{3,19},{19,3},{4,20},{20... | collective-permute-start | bytes 393224 | tf_op jit(solution)/shard_map/cond/branch_8_fun/ppermute | solution.py:585
  4.3 18.4 %collective-permute-start.83 = (f32[8,2,16,128]{3,2,1,0:T(8,128)S(1)}, f32[8,2,16,128]{3,2,1,0:T(8,128)S(1)}, u32[]{:S(2)}, u32[]{:S(2)}) collective-permute-start(f32[8,2,16,128]{3,2,1,0:T(8,128)S(1)} %get-tuple-element.460), channel_id=1, source_target_pairs={{16,9},{0,23},{17,10},{1,24},{18,11},{2,25},{19,12},{3,26},{20,13}... | collective-permute-start | bytes 393224 | tf_op jit(solution)/shard_map/cond/branch_8_fun/ppermute | solution.py:598
  9.0 13.8 %collective-permute-start.82 = (f32[8,2,16,128]{3,2,1,0:T(8,128)S(1)}, f32[8,2,16,128]{3,2,1,0:T(8,128)S(1)}, u32[]{:S(2)}, u32[]{:S(2)}) collective-permute-start(f32[8,2,16,128]{3,2,1,0:T(8,128)S(1)} %get-tuple-element.460), channel_id=1, source_target_pairs={{16,8},{0,24},{17,9},{1,25},{18,10},{2,26},{19,11},{3,27},{20,12},... | collective-permute-start | bytes 393224 | tf_op jit(solution)/shard_map/cond/branch_8_fun/ppermute | solution.py:598
  11.6 11.2 %collective-permute-start.80 = (f32[8,8,128]{2,1,0:T(8,128)S(1)}, f32[8,8,128]{2,1,0:T(8,128)S(1)}, u32[]{:S(2)}, u32[]{:S(2)}) collective-permute-start(f32[8,8,128]{2,1,0:T(8,128)S(1)} %get-tuple-element.458), channel_id=1, source_target_pairs={{0,1},{2,3},{4,5},{6,7},{8,9},{10,11},{12,13},{14,15},{1,0},{3,2},... | collective-permute-start | bytes 98312 | tf_op jit(solution)/shard_map/cond/branch_8_fun/ppermute | solution.py:583
  11.6 11.2 %collective-permute-start.81 = (f32[8,8,128]{2,1,0:T(8,128)S(1)}, f32[8,8,128]{2,1,0:T(8,128)S(1)}, u32[]{:S(2)}, u32[]{:S(2)}) collective-permute-start(f32[8,8,128]{2,1,0:T(8,128)S(1)} %get-tuple-element.459), channel_id=1, source_target_pairs={{1,2},{3,4},{5,6},{7,8},{9,10},{11,12},{13,14},{15,0},{2,1},{4,3},... | collective-permute-start | bytes 98312 | tf_op jit(solution)/shard_map/cond/branch_8_fun/ppermute | solution.py:583
  25.5 15.9 %collective-permute-start.89 = (f32[8,2,16,128]{3,2,1,0:T(8,128)S(1)}, f32[8,2,16,128]{3,2,1,0:T(8,128)S(1)}, u32[]{:S(2)}, u32[]{:S(2)}) collective-permute-start(f32[8,2,16,128]{3,2,1,0:T(8,128)S(1)} %get-tuple-element.470), channel_id=1, source_target_pairs={{0,16},{16,0},{1,17},{17,1},{2,18},{18,2},{3,19},{19,3},{4,20},{20... | collective-permute-start | bytes 393224 | tf_op jit(solution)/shard_map/cond/branch_8_fun/ppermute | solution.py:585
  26.3 15.2 %collective-permute-start.88 = (f32[8,2,16,128]{3,2,1,0:T(8,128)S(1)}, f32[8,2,16,128]{3,2,1,0:T(8,128)S(1)}, u32[]{:S(2)}, u32[]{:S(2)}) collective-permute-start(f32[8,2,16,128]{3,2,1,0:T(8,128)S(1)} %get-tuple-element.469), channel_id=1, source_target_pairs={{16,9},{0,23},{17,10},{1,24},{18,11},{2,25},{19,12},{3,26},{20,13}... | collective-permute-start | bytes 393224 | tf_op jit(solution)/shard_map/cond/branch_8_fun/ppermute | solution.py:598
  26.5 15.0 %collective-permute-start.87 = (f32[8,2,16,128]{3,2,1,0:T(8,128)S(1)}, f32[8,2,16,128]{3,2,1,0:T(8,128)S(1)}, u32[]{:S(2)}, u32[]{:S(2)}) collective-permute-start(f32[8,2,16,128]{3,2,1,0:T(8,128)S(1)} %get-tuple-element.469), channel_id=1, source_target_pairs={{16,8},{0,24},{17,9},{1,25},{18,10},{2,26},{19,11},{3,27},{20,12},... | collective-permute-start | bytes 393224 | tf_op jit(solution)/shard_map/cond/branch_8_fun/ppermute | solution.py:598
  28.2 13.2 %collective-permute-start.85 = (f32[8,8,128]{2,1,0:T(8,128)S(1)}, f32[8,8,128]{2,1,0:T(8,128)S(1)}, u32[]{:S(2)}, u32[]{:S(2)}) collective-permute-start(f32[8,8,128]{2,1,0:T(8,128)S(1)} %get-tuple-element.467), channel_id=1, source_target_pairs={{0,1},{2,3},{4,5},{6,7},{8,9},{10,11},{12,13},{14,15},{1,0},{3,2},... | collective-permute-start | bytes 98312 | tf_op jit(solution)/shard_map/cond/branch_8_fun/ppermute | solution.py:583
  30.1 11.3 %collective-permute-start.86 = (f32[8,8,128]{2,1,0:T(8,128)S(1)}, f32[8,8,128]{2,1,0:T(8,128)S(1)}, u32[]{:S(2)}, u32[]{:S(2)}) collective-permute-start(f32[8,8,128]{2,1,0:T(8,128)S(1)} %get-tuple-element.468), channel_id=1, source_target_pairs={{1,2},{3,4},{5,6},{7,8},{9,10},{11,12},{13,14},{15,0},{2,1},{4,3},... | collective-permute-start | bytes 98312 | tf_op jit(solution)/shard_map/cond/branch_8_fun/ppermute | solution.py:583

commit v5 on v4

--- a/solution.py
+++ b/solution.py
@@ -178,13 +178,8 @@
             copy.wait()
         for i in range(part * size, (part + 1) * size):
             w_ref[2, i] = w_ref[2, i] - (SHEAR_Q * omega) * (radial + float(i))
-
-        def turn_fields(n, carry, part=part):
-            for f in range(4):
-                turn(w_ref, 4 * n + f, part, wt_ref)
-            return carry
-
-        lax.fori_loop(0, FIELDS // 4, turn_fields, 0)
+        for f in range(FIELDS):
+            turn(w_ref, f, part, wt_ref)
     send_columns(parts, wt_ref, cols_ref, even_ref, odd_ref)
 
     def copy(f, carry):
@@ -226,7 +221,7 @@
     else:
         w_ref, wt_ref, vt_ref, v_ref, *refs = refs
         dy_ref = vt_ref
-    hz_ref, rz_ref, fz_ref, wl_ref, dx_ref, fx_ref, uy_ref, ly_ref, fy_ref = refs
+    hz_ref, rz_ref, fz_ref, wl_ref, dx_ref, fx_ref, half_ref, uy_ref, ly_ref, fy_ref = refs
     rows, high, width = w_ref.shape[1:]
     per_group = width // high
     groups = rows // per_group
@@ -250,7 +245,24 @@
         if not second:
             turn_result(jnp.maximum(i - early, 0))
         w = load_row(w_ref, i)
-        half = [0.5 * x for x in w]
+        half = [half_ref[f] for f in range(FIELDS)]
+
+        after, before = jnp.minimum(i + 1, rows - 1), jnp.maximum(i - 1, 0)
+        right, wl = [], [wl_ref[f] for f in range(FIELDS)]
+        for f in range(FIELDS):
+            half_after = 0.5 * w_ref[f, after]
+            half_ref[f] = half_after
+            up = half_after - half[f]
+            slope = limited(up, dx_ref[f])
+            dx_ref[f] = up
+            wl_ref[f] = w[f] + slope
+            right.append(w[f] - slope)
+        fx = face(wl, right, 0)
+        scale = jnp.where(jnp.logical_and(i >= 2, i <= rows - 2), coef, 0.0)
+        for f in range(FIELDS):
+            here = scale * fx[f]
+            v_ref[f, before] = v_ref[f, before] - (here - fx_ref[f])
+            fx_ref[f] = here
 
         left = []
         for f in range(FIELDS):
@@ -263,21 +275,6 @@
         for f in range(FIELDS):
             wrapped(fz_ref, f, fz[f], True, False)
             total.append(fz[f] - fz_ref[f, last_row])
-
-        after, before = jnp.minimum(i + 1, rows - 1), jnp.maximum(i - 1, 0)
-        right, wl = [], [wl_ref[f] for f in range(FIELDS)]
-        for f in range(FIELDS):
-            up = 0.5 * w_ref[f, after] - half[f]
-            slope = limited(up, dx_ref[f])
-            dx_ref[f] = up
-            wl_ref[f] = w[f] + slope
-            right.append(w[f] - slope)
-        fx = face(wl, right, 0)
-        scale = jnp.where(jnp.logical_and(i >= 2, i <= rows - 2), coef, 0.0)
-        for f in range(FIELDS):
-            here = scale * fx[f]
-            v_ref[f, before] = v_ref[f, before] - (here - fx_ref[f])
-            fx_ref[f] = here
 
         x = radial + i.astype(jnp.float32)
         cons = to_conserved(w)
@@ -336,6 +333,7 @@
         for f in range(FIELDS):
             blank = jnp.zeros((high, width), jnp.float32)
             dx_ref[f], fx_ref[f], wl_ref[f] = blank, blank, w_ref[f, 0]
+            half_ref[f] = 0.5 * w_ref[f, 0]
         lax.fori_loop(0, rows, body, 0)
 
     if second:
@@ -349,7 +347,7 @@
         azimuthal()
 
 
-def sheared_rows(first, shear_ref, near_ref, next_ref, ghost_ref):
+def sheared_rows(loop, first, shear_ref, near_ref, next_ref, ghost_ref):
     high, width = near_ref.shape[2:]
     rest = lax.rem(shear_ref[0], width)
     start = jnp.where(first, width - 1 - rest, rest)
@@ -367,10 +365,10 @@
             near, following = near_ref[f, k], next_ref[f, k]
             one = jnp.where(first, following, near)
             two = jnp.where(first, near, following)
-            one_up, two_up = pltpu.roll(one, width - 1, 1), pltpu.roll(two, width - 1, 1)
-            one = ahead * jnp.where(lane < width - 1, one_up, two_up) + here * one
-            two = ahead * two_up + here * two
-            ghost.append(jnp.where(lane < width - start, pltpu.roll(one, back, 1), pltpu.roll(two, back, 1)))
+            two = pltpu.roll(two, back, 1)
+            one = jnp.where(lane < width - start, pltpu.roll(one, back, 1), two)
+            two = pltpu.roll(jnp.where(lane == 0, two, one), width - 1, 1)
+            ghost.append(ahead * two + here * one)
         boosted = list(ghost)
         boosted[2] = ghost[2] + ghost[0] * delta
         boosted[7] = ghost[7] + ghost[2] * delta + 0.5 * ghost[0] * delta * delta
@@ -379,7 +377,16 @@
             ghost_ref[f, k] = prim[f]
         return carry
 
-    lax.fori_loop(0, 2, body, 0)
+    loop(2, body)
+
+
+def in_loop(count, body):
+    lax.fori_loop(0, count, body, 0)
+
+
+def unrolled(count, body):
+    for n in range(count):
+        body(n, 0)
 
 
 def edge_kernel(second, beside, shear_any, *refs):
@@ -403,6 +410,7 @@
     coef = 0.5 * step
     _, _, first, last = whereabouts(rows)
     even = at_even_block()
+    loop = unrolled if second else in_loop
 
     def gather(f, carry):
         for k in range(2):
@@ -415,6 +423,9 @@
         return carry
 
     lax.fori_loop(0, FIELDS, gather, 0)
+    if second:
+        shear_copy.wait()
+        sheared_rows(loop, first, shear_smem, near_ref, next_ref, ghost_ref)
     cells = [[e_ref[f, k] for f in range(FIELDS)] for k in range(5)]
     sides = [three_states(cells[k : k + 3]) for k in range(3)]
     one = face(sides[0][0], sides[1][1], 1)
@@ -437,8 +448,9 @@
 
         lax.fori_loop(0, FIELDS, scatter, 0)
 
-    shear_copy.wait()
-    sheared_rows(first, shear_smem, near_ref, next_ref, ghost_ref)
+    if not second:
+        shear_copy.wait()
+        sheared_rows(loop, first, shear_smem, near_ref, next_ref, ghost_ref)
     def place(f, carry):
         x_ref[0, f, 0:2] = jnp.where(first, ghost_ref[f], xl_ref[f])
         x_ref[1, f, 3:5] = jnp.where(last, ghost_ref[f], xr_ref[f])
@@ -449,8 +461,10 @@
     lax.fori_loop(0, FIELDS, place, 0)
 
     def radial(n, carry):
-        end = lax.div(n, 2)
-        at = pl.ds(pl.multiple_of(lax.rem(n, 2) * (high // 2), 8), high // 2)
+        if second:
+            end, at = n // 2, pl.ds(n % 2 * (high // 2), high // 2)
+        else:
+            end, at = lax.div(n, 2), pl.ds(pl.multiple_of(lax.rem(n, 2) * (high // 2), 8), high // 2)
         cells = [[x_ref[end, f, k, at] for f in range(FIELDS)] for k in range(5)]
         sides = [three_states(cells[k : k + 3]) for k in range(3)]
         one = face(sides[0][0], sides[1][1], 0)
@@ -460,8 +474,8 @@
             x_ref[end, f, 1, at] = coef * jnp.where(end == 0, -two[f], one[f])
         return carry
 
-    lax.fori_loop(0, 4, radial, 0)
-    batch = FIELDS // 2
+    loop(4, radial)
+    batch = FIELDS // 4
 
     if not second:
         lane = lanes_of((width, width))
@@ -487,16 +501,16 @@
             return carry
 
         lax.fori_loop(0, FIELDS, correct_rows, 0)
-        strips = width // 16
+        block = width // 2
 
         def primitives(n, carry):
-            g, at = lax.div(n, strips), pl.ds(pl.multiple_of(PAD + 16 * lax.rem(n, strips), 8), 16)
+            g, at = lax.div(n, 2), pl.ds(pl.multiple_of(PAD + block * lax.rem(n, 2), 8), block)
             prim = to_primitive([w1_ref[f, g, at] for f in range(FIELDS)])
             for f in range(FIELDS):
                 w1_ref[f, g, at] = prim[f]
             return carry
 
-        lax.fori_loop(0, groups * strips, primitives, 0, unroll=4)
+        lax.fori_loop(0, 2 * groups, primitives, 0)
 
         def turn_rows(n, carry):
             for k in range(batch):
@@ -512,36 +526,29 @@
         send_rows(rows, rows1_ref, *sends)
         return
 
-    def finish(n, carry):
-        g = lax.div(n, 2)
+    batch = FIELDS // 2
+    copies = []
+    for g in [*range(1, groups - 1), 0, groups - 1]:
         at = pl.ds(g * size, size)
-        fields = [lax.rem(n, 2) * batch + f for f in range(batch)]
-        for f in fields:
-            head = dy_ref[f, g, PAD : 2 * PAD] + c_ref[f, g, 0:PAD]
-            tail = dy_ref[f, g, width : PAD + width] + c_ref[f, g, PAD : 2 * PAD]
-            strip = jnp.concatenate([head, dy_ref[f, g, 2 * PAD : width], tail], axis=0)
-            out_ref[f, at] = v_ref[f, at] - strip.T.reshape(size, high, width)
-
-        @pl.when(g == 0)
-        def _():
-            for f in fields:
-                out_ref[f, 0] = out_ref[f, 0] - x_ref[0, f, 0]
-                out_ref[f, 1] = out_ref[f, 1] - x_ref[0, f, 1]
-
-        @pl.when(g == groups - 1)
-        def _():
-            for f in fields:
-                out_ref[f, rows - 1] = out_ref[f, rows - 1] - x_ref[1, f, 0]
-                out_ref[f, rows - 2] = out_ref[f, rows - 2] - x_ref[1, f, 1]
-
-        part = pl.ds(fields[0], batch)
-        pltpu.make_async_copy(out_ref.at[part, at], out_hbm.at[part, at], sems.at[n]).start()
-        return carry
-
-    lax.fori_loop(0, 2 * groups, finish, 0)
-    for n in range(2 * groups):
-        at, part = pl.ds(n // 2 * size, size), pl.ds(n % 2 * batch, batch)
-        pltpu.make_async_copy(out_ref.at[part, at], out_hbm.at[part, at], sems.at[n]).wait()
+        for half in range(2):
+            for f in range(half * batch, (half + 1) * batch):
+                head = dy_ref[f, g, PAD : 2 * PAD] + c_ref[f, g, 0:PAD]
+                tail = dy_ref[f, g, width : PAD + width] + c_ref[f, g, PAD : 2 * PAD]
+                strip = jnp.concatenate([head, dy_ref[f, g, 2 * PAD : width], tail], axis=0)
+                strip = strip.T.reshape(size, high, width)
+                value = [v_ref[f, g * size + i] - strip[i] for i in range(size)]
+                if g == 0:
+                    value[0], value[1] = value[0] - x_ref[0, f, 0], value[1] - x_ref[0, f, 1]
+                if g == groups - 1:
+                    value[-1], value[-2] = value[-1] - x_ref[1, f, 0], value[-2] - x_ref[1, f, 1]
+                for i in range(size):
+                    out_ref[f, g * size + i] = value[i]
+            part = pl.ds(half * batch, batch)
+            copy = pltpu.make_async_copy(out_ref.at[part, at], out_hbm.at[part, at], sems.at[len(copies)])
+            copy.start()
+            copies.append(copy)
+    for copy in copies:
+        copy.wait()
 
 
 def gather_kernel(even_ref, odd_ref, *refs):
@@ -603,7 +610,7 @@
     tile = (FIELDS, high, width)
     padded = (FIELDS, high + 2 * PAD, width)
     column = (FIELDS, PAD + width, width)
-    return [padded] * 3 + [tile] * 3 + [column] * 3
+    return [padded] * 3 + [tile] * 4 + [column] * 3
 
 
 def edge_scratch(full, groups):

time: 46.3 us -> 44.8 us (0.968); the launches traced: 45.4 us -> 44.6 us
  Pallas kernels: 24.8 us -> 23.3 us
  starting transfers between devices: 18.2 us -> 18.7 us
    ppermute x2, starting transfers between devices: 6.29 us -> 2.31 us  [exchange(): lax.ppermute(odd, 'gy', pairs(1))]
    ppermute x2, starting transfers between devices: 1.91 us -> 5.34 us  [exchange(): lax.ppermute(even, 'gy', pairs(0))]
    ppermute x2, starting transfers between devices: 0.9 us -> 3.58 us  [exchange(): return (even, odd, lax.ppermute(swap[0], 'gx', [(0, 1), (1, 0)]))]
    ppermute x4, starting transfers between devices: 9.13 us -> 7.5 us  [crossing(): return lax.ppermute(shear, ('gx', 'gy'), pairs)]
    pallas_call x6, Pallas kernels: 24.8 us -> 23.3 us  [call(): pl.pallas_call(kernel, name=name, out_shape=[jax.ShapeDtypeStruct(s, jnp....]
  transfers between devices with their start and end apart: 10 -> 10, of which waited for: 0 -> 0; matrix products, arithmetic and copies ran while one was open for 0% -> 0% of each run, Pallas kernels for 36% -> 35%
where the time goes in v5:
time: 44.8 us; the launch traced here: 44.6 us
  Pallas kernels  23.3 us (52%)
  starting transfers between devices  18.7 us (42%)
  between operations  1.56 us (3%)
  loops' own time  0.95 us (2%)
    pallas_call x6, Pallas kernels, call(): pl.pallas_call(kernel, name=name, out_shape=[jax.ShapeDtypeStruct(s, jnp....  23.3 us
    ppermute x4, starting transfers between devices, crossing(): return lax.ppermute(shear, ('gx', 'gy'), pairs)  7.5 us
    ppermute x2, starting transfers between devices, exchange(): lax.ppermute(even, 'gy', pairs(0))  5.34 us
    ppermute x2, starting transfers between devices, exchange(): return (even, odd, lax.ppermute(swap[0], 'gx', [(0, 1), (1, 0)]))  3.58 us
    ppermute x2, starting transfers between devices, exchange(): lax.ppermute(odd, 'gy', pairs(1))  2.31 us
    another operation x1, loops' own time, sections(): lax.switch(block, branches, drift, w0, wt0, cols, even, odd, rows, shear,...  0.95 us
  transfers between devices with their start and end apart: 10, of which 0 were waited for; matrix products, arithmetic and copies ran while one was open for 0% of the time, Pallas kernels for 35%

profile of v5, /device:TPU:1, one launch (start us, length us, event | category | flops | bytes accessed | tf_op | source)
XLA Modules:
  0.0 44.6 jit_solution(13532079411191116943)
XLA Ops:
  1.3 0.1 pad_add_fusion.shear_any
  1.4 2.3 %prepare.1 = (f32[8,32,16,128]{3,2,1,0:T(8,128)S(1)}, f32[8,5,144,128]{3,2,1,0:T(8,128)S(1)}, f32[8,24,128]{2,1,0:T(8,128)S(1)}, f32[8,8,128]{2,1,0:T(8,128)S(1)...) custom-call(f32[32,16,128]{2,1,0:T(8,128)} %rho_hbm.1, ...), custom_call_target="tpu_custom_call" | custom-call | tf_op jit(solution)/shard_map/prepare/pallas_call | solution.py:571
  3.7 38.3 %conditional.1 = (f32[8,32,16,128]{3,2,1,0:T(8,128)S(1)}, f32[8,5,144,128]{3,2,1,0:T(8,128)S(1)}, f32[8,6,16,128]{3,2,1,0:T(8,128)S(1)}, f32[8,24,128]{2,1,0:T(8...) conditional(s32[]{:T(128)} %clamp.3, ...), branch_computations={%region_0.1_spmd, %region_1.2_spmd, %region_2.3_spmd, %region_3.4_... | conditional | bytes 3670464 | solution.py:661
  3.9 0.1 collective-permute-start.134
  4.1 5.7 %collective-permute-start.133 = (f32[8,2,16,128]{3,2,1,0:T(8,128)S(1)}, f32[8,2,16,128]{3,2,1,0:T(8,128)S(1)}, u32[]{:S(2)}, u32[]{:S(2)}) collective-permute-start(f32[8,2,16,128]{3,2,1,0:T(8,128)S(1)} %get-tuple-element.560), channel_id=1, source_target_pairs={{16,14},{0,18},{17,15},{1,19},{18,0},{2,20},{19,1},{3,21},{20,2},{... | collective-permute-start | bytes 393224 | tf_op jit(solution)/shard_map/cond/branch_13_fun/ppermute | solution.py:605
  9.7 1.5 %collective-permute-start.132 = (f32[8,2,16,128]{3,2,1,0:T(8,128)S(1)}, f32[8,2,16,128]{3,2,1,0:T(8,128)S(1)}, u32[]{:S(2)}, u32[]{:S(2)}) collective-permute-start(f32[8,2,16,128]{3,2,1,0:T(8,128)S(1)} %get-tuple-element.560), channel_id=1, source_target_pairs={{16,13},{0,19},{17,14},{1,20},{18,15},{2,21},{19,0},{3,22},{20,1},... | collective-permute-start | bytes 393224 | tf_op jit(solution)/shard_map/cond/branch_13_fun/ppermute | solution.py:605
  11.3 0.0 collective-permute-start.130
  11.3 2.3 %collective-permute-start.131 = (f32[8,8,128]{2,1,0:T(8,128)S(1)}, f32[8,8,128]{2,1,0:T(8,128)S(1)}, u32[]{:S(2)}, u32[]{:S(2)}) collective-permute-start(f32[8,8,128]{2,1,0:T(8,128)S(1)} %get-tuple-element.559), channel_id=1, source_target_pairs={{1,2},{3,4},{5,6},{7,8},{9,10},{11,12},{13,14},{15,0},{2,1},{4,3},... | collective-permute-start | bytes 98312 | tf_op jit(solution)/shard_map/cond/branch_13_fun/ppermute | solution.py:590
  13.6 7.9 %inner_1.29.refs_0_ = f32[8,5,144,128]{3,2,1,0:T(8,128)S(1)} custom-call(f32[8,32,16,128]{3,2,1,0:T(8,128)S(1)} %get-tuple-element.554.refs_0_.refs_1_, f32[8,5,144,128]{3,2,1,0:T(8,128)S(1)} %get-tuple-element.555.refs_1_), custom_call_target="tpu_custom_call" | custom-call | tf_op jit(solution)/shard_map/cond/branch_13_fun/inner_1/pallas_call | solution.py:571
  21.5 0.0 collective-permute-done.130.refs_3_
  21.5 0.0 collective-permute-done.131.refs_4_
  21.5 0.0 collective-permute-done.134.refs_7_
  21.5 0.0 collective-permute-done.133.refs_6_
  21.5 0.0 collective-permute-done.132.refs_5_
  21.5 2.8 %edge_1.29 = (f32[8,5,144,128]{3,2,1,0:T(8,128)S(1)}, f32[8,24,128]{2,1,0:T(8,128)S(1)}, f32[8,8,128]{2,1,0:T(8,128)S(1)}, f32[8,8,128]{2,1,0:T(8,128)S(1)}, f32...) custom-call(s32[2]{0:T(128)S(1)} %get-tuple-element.553.shear_any, ...), custom_call_target="tpu_custom_call", output_to_operand_aliasing={{0}: (1, {})} | custom-call | tf_op jit(solution)/shard_map/cond/branch_13_fun/edge_1/pallas_call | solution.py:571
  24.3 3.5 %collective-permute-start.139 = (f32[8,2,16,128]{3,2,1,0:T(8,128)S(1)}, f32[8,2,16,128]{3,2,1,0:T(8,128)S(1)}, u32[]{:S(2)}, u32[]{:S(2)}) collective-permute-start(f32[8,2,16,128]{3,2,1,0:T(8,128)S(1)} %get-tuple-element.570), channel_id=1, source_target_pairs={{0,16},{16,0},{1,17},{17,1},{2,18},{18,2},{3,19},{19,3},{4,20},{20... | collective-permute-start | bytes 393224 | tf_op jit(solution)/shard_map/cond/branch_13_fun/ppermute | solution.py:592
  27.7 0.0 collective-permute-start.138
  27.7 0.3 collective-permute-start.137
  28.0 5.3 %collective-permute-start.135 = (f32[8,8,128]{2,1,0:T(8,128)S(1)}, f32[8,8,128]{2,1,0:T(8,128)S(1)}, u32[]{:S(2)}, u32[]{:S(2)}) collective-permute-start(f32[8,8,128]{2,1,0:T(8,128)S(1)} %get-tuple-element.567), channel_id=1, source_target_pairs={{0,1},{2,3},{4,5},{6,7},{8,9},{10,11},{12,13},{14,15},{1,0},{3,2},... | collective-permute-start | bytes 98312 | tf_op jit(solution)/shard_map/cond/branch_13_fun/ppermute | solution.py:590
  33.4 0.0 collective-permute-start.136
  33.4 7.9 %inner_2.29 = (f32[8,32,16,128]{3,2,1,0:T(8,128)S(1)}, f32[8,5,144,128]{3,2,1,0:T(8,128)S(1)}) custom-call(f32[8,5,144,128]{3,2,1,0:T(8,128)S(1)} %get-tuple-element.562.refs_0_, f32[8,32,16,128]{3,2,1,0:T(8,128)S(1)} %get-tuple-element.554.refs_0_.refs_1_), custom_call_target="tpu_custom_call" | custom-call | tf_op jit(solution)/shard_map/cond/branch_13_fun/inner_2/pallas_call | solution.py:571
  41.3 0.0 collective-permute-done.135.even_ref
  41.3 0.0 collective-permute-done.136.odd_ref
  41.3 0.0 collective-permute-done.139.refs_2_
  41.3 0.0 collective-permute-done.138.refs_1_
  41.3 0.0 collective-permute-done.137.refs_0_
  41.3 0.1 gather.29
  41.9 2.4 %edge_2.1 = f32[8,32,16,128]{3,2,1,0:T(8,128)} custom-call(s32[2]{0:T(128)S(1)} %pad_add_fusion.shear_any, f32[8,32,16,128]{3,2,1,0:T(8,128)S(1)} %get-tuple-element.635.refs_0_, f32[8,5,144,128]{3,2,1,0:T(8,128)S(1)} %get-tuple-element.636.refs_1_, f32[8,6,16,128]{3,2,1,0:T(8,128)S(1)} %get-tuple-element.637.refs_2_, ...), custom_call_target="tpu_custom_call" | custom-call | tf_op jit(solution)/shard_map/edge_2/pallas_call | solution.py:571
Async XLA Ops:
  3.9 17.5 %collective-permute-start.134 = (f32[8,2,16,128]{3,2,1,0:T(8,128)S(1)}, f32[8,2,16,128]{3,2,1,0:T(8,128)S(1)}, u32[]{:S(2)}, u32[]{:S(2)}) collective-permute-start(f32[8,2,16,128]{3,2,1,0:T(8,128)S(1)} %get-tuple-element.561), channel_id=1, source_target_pairs={{0,16},{16,0},{1,17},{17,1},{2,18},{18,2},{3,19},{19,3},{4,20},{20... | collective-permute-start | bytes 393224 | tf_op jit(solution)/shard_map/cond/branch_13_fun/ppermute | solution.py:592
  4.1 17.4 %collective-permute-start.133 = (f32[8,2,16,128]{3,2,1,0:T(8,128)S(1)}, f32[8,2,16,128]{3,2,1,0:T(8,128)S(1)}, u32[]{:S(2)}, u32[]{:S(2)}) collective-permute-start(f32[8,2,16,128]{3,2,1,0:T(8,128)S(1)} %get-tuple-element.560), channel_id=1, source_target_pairs={{16,14},{0,18},{17,15},{1,19},{18,0},{2,20},{19,1},{3,21},{20,2},{... | collective-permute-start | bytes 393224 | tf_op jit(solution)/shard_map/cond/branch_13_fun/ppermute | solution.py:605
  9.7 11.8 %collective-permute-start.132 = (f32[8,2,16,128]{3,2,1,0:T(8,128)S(1)}, f32[8,2,16,128]{3,2,1,0:T(8,128)S(1)}, u32[]{:S(2)}, u32[]{:S(2)}) collective-permute-start(f32[8,2,16,128]{3,2,1,0:T(8,128)S(1)} %get-tuple-element.560), channel_id=1, source_target_pairs={{16,13},{0,19},{17,14},{1,20},{18,15},{2,21},{19,0},{3,22},{20,1},... | collective-permute-start | bytes 393224 | tf_op jit(solution)/shard_map/cond/branch_13_fun/ppermute | solution.py:605
  11.3 10.2 %collective-permute-start.130 = (f32[8,8,128]{2,1,0:T(8,128)S(1)}, f32[8,8,128]{2,1,0:T(8,128)S(1)}, u32[]{:S(2)}, u32[]{:S(2)}) collective-permute-start(f32[8,8,128]{2,1,0:T(8,128)S(1)} %get-tuple-element.558), channel_id=1, source_target_pairs={{0,1},{2,3},{4,5},{6,7},{8,9},{10,11},{12,13},{14,15},{1,0},{3,2},... | collective-permute-start | bytes 98312 | tf_op jit(solution)/shard_map/cond/branch_13_fun/ppermute | solution.py:590
  11.3 10.2 %collective-permute-start.131 = (f32[8,8,128]{2,1,0:T(8,128)S(1)}, f32[8,8,128]{2,1,0:T(8,128)S(1)}, u32[]{:S(2)}, u32[]{:S(2)}) collective-permute-start(f32[8,8,128]{2,1,0:T(8,128)S(1)} %get-tuple-element.559), channel_id=1, source_target_pairs={{1,2},{3,4},{5,6},{7,8},{9,10},{11,12},{13,14},{15,0},{2,1},{4,3},... | collective-permute-start | bytes 98312 | tf_op jit(solution)/shard_map/cond/branch_13_fun/ppermute | solution.py:590
  24.3 17.0 %collective-permute-start.139 = (f32[8,2,16,128]{3,2,1,0:T(8,128)S(1)}, f32[8,2,16,128]{3,2,1,0:T(8,128)S(1)}, u32[]{:S(2)}, u32[]{:S(2)}) collective-permute-start(f32[8,2,16,128]{3,2,1,0:T(8,128)S(1)} %get-tuple-element.570), channel_id=1, source_target_pairs={{0,16},{16,0},{1,17},{17,1},{2,18},{18,2},{3,19},{19,3},{4,20},{20... | collective-permute-start | bytes 393224 | tf_op jit(solution)/shard_map/cond/branch_13_fun/ppermute | solution.py:592
  27.7 13.6 %collective-permute-start.138 = (f32[8,2,16,128]{3,2,1,0:T(8,128)S(1)}, f32[8,2,16,128]{3,2,1,0:T(8,128)S(1)}, u32[]{:S(2)}, u32[]{:S(2)}) collective-permute-start(f32[8,2,16,128]{3,2,1,0:T(8,128)S(1)} %get-tuple-element.569), channel_id=1, source_target_pairs={{16,14},{0,18},{17,15},{1,19},{18,0},{2,20},{19,1},{3,21},{20,2},{... | collective-permute-start | bytes 393224 | tf_op jit(solution)/shard_map/cond/branch_13_fun/ppermute | solution.py:605
  27.7 13.6 %collective-permute-start.137 = (f32[8,2,16,128]{3,2,1,0:T(8,128)S(1)}, f32[8,2,16,128]{3,2,1,0:T(8,128)S(1)}, u32[]{:S(2)}, u32[]{:S(2)}) collective-permute-start(f32[8,2,16,128]{3,2,1,0:T(8,128)S(1)} %get-tuple-element.569), channel_id=1, source_target_pairs={{16,13},{0,19},{17,14},{1,20},{18,15},{2,21},{19,0},{3,22},{20,1},... | collective-permute-start | bytes 393224 | tf_op jit(solution)/shard_map/cond/branch_13_fun/ppermute | solution.py:605
  28.0 13.2 %collective-permute-start.135 = (f32[8,8,128]{2,1,0:T(8,128)S(1)}, f32[8,8,128]{2,1,0:T(8,128)S(1)}, u32[]{:S(2)}, u32[]{:S(2)}) collective-permute-start(f32[8,8,128]{2,1,0:T(8,128)S(1)} %get-tuple-element.567), channel_id=1, source_target_pairs={{0,1},{2,3},{4,5},{6,7},{8,9},{10,11},{12,13},{14,15},{1,0},{3,2},... | collective-permute-start | bytes 98312 | tf_op jit(solution)/shard_map/cond/branch_13_fun/ppermute | solution.py:590
  33.4 7.9 %collective-permute-start.136 = (f32[8,8,128]{2,1,0:T(8,128)S(1)}, f32[8,8,128]{2,1,0:T(8,128)S(1)}, u32[]{:S(2)}, u32[]{:S(2)}) collective-permute-start(f32[8,8,128]{2,1,0:T(8,128)S(1)} %get-tuple-element.568), channel_id=1, source_target_pairs={{1,2},{3,4},{5,6},{7,8},{9,10},{11,12},{13,14},{15,0},{2,1},{4,3},... | collective-permute-start | bytes 98312 | tf_op jit(solution)/shard_map/cond/branch_13_fun/ppermute | solution.py:590

commit v6 on v5

--- a/solution.py
+++ b/solution.py
@@ -221,7 +221,7 @@
     else:
         w_ref, wt_ref, vt_ref, v_ref, *refs = refs
         dy_ref = vt_ref
-    hz_ref, rz_ref, fz_ref, wl_ref, dx_ref, fx_ref, half_ref, uy_ref, ly_ref, fy_ref = refs
+    hz_ref, rz_ref, fz_ref, wl_ref, dx_ref, fx_ref, half_ref, uy_ref, ly_ref, fy_ref, ry_ref = refs
     rows, high, width = w_ref.shape[1:]
     per_group = width // high
     groups = rows // per_group
@@ -265,6 +265,7 @@
             fx_ref[f] = here
 
         left = []
+        w = load_row(w_ref, i)
         for f in range(FIELDS):
             wrapped(hz_ref, f, half[f], True, True)
             slope = limited(hz_ref[f, next_row] - half[f], half[f] - hz_ref[f, last_row])
@@ -293,7 +294,7 @@
 
     size = 2 * groups * width // rows
     strips = width // size
-    row = lax.broadcasted_iota(jnp.int32, (size, width), 0)
+    row = lax.broadcasted_iota(jnp.int32, (size // 2, width), 0)
 
     def body_y(n, carry):
         for m in (2 * n, 2 * n + 1):
@@ -303,23 +304,27 @@
                 turn_result(rows - early + m)
         g, start = lax.div(n, strips), size * lax.rem(n, strips)
         at = pl.multiple_of(start + PAD, 8)
-        left, right = [], []
         for f in range(FIELDS):
             w = wt_ref[f, g, pl.ds(at, size)]
             up = 0.5 * (wt_ref[f, g, pl.ds(at + 1, size)] - w)
             slope = limited(up, behind(uy_ref, f, at, up))
-            left.append(behind(ly_ref, f, at, w + slope))
-            right.append(w - slope)
-        fy = face(left, right, 1)
-        cell = row + start
-        scale = jnp.where(jnp.logical_and(cell >= 2, cell <= width - 2), coef, 0.0)
-        for f in range(FIELDS):
-            here = scale * fy[f]
-            change = here - behind(fy_ref, f, at, here)
-            if second:
-                dy_ref[f, g, pl.ds(at - 1, size)] = change
-            else:
-                vt_ref[f, g, pl.ds(at - 1, size)] = vt_ref[f, g, pl.ds(at - 1, size)] - change
+            ly_ref[f, pl.ds(at, size)] = w + slope
+            ry_ref[f] = w - slope
+        for part in range(2):
+            half = size // 2
+            to = at + part * half
+            left = [ly_ref[f, pl.ds(to - 1, half)] for f in range(FIELDS)]
+            right = [ry_ref[f, part * half : (part + 1) * half] for f in range(FIELDS)]
+            fy = face(left, right, 1)
+            cell = row + (start + part * half)
+            scale = jnp.where(jnp.logical_and(cell >= 2, cell <= width - 2), coef, 0.0)
+            for f in range(FIELDS):
+                here = scale * fy[f]
+                change = here - behind(fy_ref, f, to, here)
+                if second:
+                    dy_ref[f, g, pl.ds(to - 1, half)] = change
+                else:
+                    vt_ref[f, g, pl.ds(to - 1, half)] = vt_ref[f, g, pl.ds(to - 1, half)] - change
         return carry
 
     def azimuthal():
@@ -347,7 +352,7 @@
         azimuthal()
 
 
-def sheared_rows(loop, first, shear_ref, near_ref, next_ref, ghost_ref):
+def sheared_rows(first, shear_ref, near_ref, next_ref, ghost_ref):
     high, width = near_ref.shape[2:]
     rest = lax.rem(shear_ref[0], width)
     start = jnp.where(first, width - 1 - rest, rest)
@@ -359,7 +364,7 @@
     delta = jnp.where(first, 1.0, -1.0)
     lane = lanes_of((high, width))
 
-    def body(k, carry):
+    for k in range(2):
         ghost = []
         for f in range(FIELDS):
             near, following = near_ref[f, k], next_ref[f, k]
@@ -375,9 +380,6 @@
         prim = to_primitive(boosted)
         for f in range(FIELDS):
             ghost_ref[f, k] = prim[f]
-        return carry
-
-    loop(2, body)
 
 
 def in_loop(count, body):
@@ -423,9 +425,8 @@
         return carry
 
     lax.fori_loop(0, FIELDS, gather, 0)
-    if second:
-        shear_copy.wait()
-        sheared_rows(loop, first, shear_smem, near_ref, next_ref, ghost_ref)
+    shear_copy.wait()
+    sheared_rows(first, shear_smem, near_ref, next_ref, ghost_ref)
     cells = [[e_ref[f, k] for f in range(FIELDS)] for k in range(5)]
     sides = [three_states(cells[k : k + 3]) for k in range(3)]
     one = face(sides[0][0], sides[1][1], 1)
@@ -448,9 +449,6 @@
 
         lax.fori_loop(0, FIELDS, scatter, 0)
 
-    if not second:
-        shear_copy.wait()
-        sheared_rows(loop, first, shear_smem, near_ref, next_ref, ghost_ref)
     def place(f, carry):
         x_ref[0, f, 0:2] = jnp.where(first, ghost_ref[f], xl_ref[f])
         x_ref[1, f, 3:5] = jnp.where(last, ghost_ref[f], xr_ref[f])
@@ -610,7 +608,7 @@
     tile = (FIELDS, high, width)
     padded = (FIELDS, high + 2 * PAD, width)
     column = (FIELDS, PAD + width, width)
-    return [padded] * 3 + [tile] * 4 + [column] * 3
+    return [padded] * 3 + [tile] * 4 + [column] * 3 + [(FIELDS, 2 * high, width)]
 
 
 def edge_scratch(full, groups):

time: 44.8 us -> 44.1 us (0.984)
  Pallas kernels: 23.3 us -> 22.6 us
    ppermute x2, starting transfers between devices: 3.58 us -> 4.48 us  [exchange(): return (even, odd, lax.ppermute(swap[0], 'gx', [(0, 1), (1, 0)]))]
    ppermute x2, starting transfers between devices: 2.31 us -> 1.41 us  [exchange(): lax.ppermute(odd, 'gy', pairs(1))]
    pallas_call x6, Pallas kernels: 23.3 us -> 22.6 us  [call(): pl.pallas_call(kernel, name=name, out_shape=[jax.ShapeDtypeStruct(s, jnp....]
where the time goes in v6:
time: 44.1 us; the launch traced here: 43.9 us
  Pallas kernels  22.6 us (51%)
  starting transfers between devices  18.7 us (42%)
  between operations  1.56 us (4%)
  loops' own time  0.94 us (2%)
    pallas_call x6, Pallas kernels, call(): pl.pallas_call(kernel, name=name, out_shape=[jax.ShapeDtypeStruct(s, jnp....  22.6 us
    ppermute x4, starting transfers between devices, crossing(): return lax.ppermute(shear, ('gx', 'gy'), pairs)  7.5 us
    ppermute x2, starting transfers between devices, exchange(): lax.ppermute(even, 'gy', pairs(0))  5.34 us
    ppermute x2, starting transfers between devices, exchange(): return (even, odd, lax.ppermute(swap[0], 'gx', [(0, 1), (1, 0)]))  4.48 us
    ppermute x2, starting transfers between devices, exchange(): lax.ppermute(odd, 'gy', pairs(1))  1.41 us
    another operation x1, loops' own time, sections(): lax.switch(block, branches, drift, w0, wt0, cols, even, odd, rows, shear,...  0.94 us
  transfers between devices with their start and end apart: 10, of which 0 were waited for; matrix products, arithmetic and copies ran while one was open for 0% of the time, Pallas kernels for 35%

profile of v6, /device:TPU:1, one launch (start us, length us, event | category | flops | bytes accessed | tf_op | source)
XLA Modules:
  0.0 43.9 jit_solution(13750366407919640440)
XLA Ops:
  1.3 0.1 pad_add_fusion.shear_any
  1.4 2.3 %prepare.1 = (f32[8,32,16,128]{3,2,1,0:T(8,128)S(1)}, f32[8,5,144,128]{3,2,1,0:T(8,128)S(1)}, f32[8,24,128]{2,1,0:T(8,128)S(1)}, f32[8,8,128]{2,1,0:T(8,128)S(1)...) custom-call(f32[32,16,128]{2,1,0:T(8,128)} %rho_hbm.1, ...), custom_call_target="tpu_custom_call" | custom-call | tf_op jit(solution)/shard_map/prepare/pallas_call | solution.py:569
  3.7 37.6 %conditional.1 = (f32[8,32,16,128]{3,2,1,0:T(8,128)S(1)}, f32[8,5,144,128]{3,2,1,0:T(8,128)S(1)}, f32[8,6,16,128]{3,2,1,0:T(8,128)S(1)}, f32[8,24,128]{2,1,0:T(8...) conditional(s32[]{:T(128)} %clamp.3, ...), branch_computations={%region_0.1_spmd, %region_1.2_spmd, %region_2.3_spmd, %region_3.4_... | conditional | bytes 3670464 | solution.py:659
  4.2 0.1 collective-permute-start.144
  4.3 6.6 %collective-permute-start.143 = (f32[8,2,16,128]{3,2,1,0:T(8,128)S(1)}, f32[8,2,16,128]{3,2,1,0:T(8,128)S(1)}, u32[]{:S(2)}, u32[]{:S(2)}) collective-permute-start(f32[8,2,16,128]{3,2,1,0:T(8,128)S(1)} %get-tuple-element.580), channel_id=1, source_target_pairs={{16,15},{0,17},{17,0},{1,18},{18,1},{2,19},{19,2},{3,20},{20,3},{4... | collective-permute-start | bytes 393224 | tf_op jit(solution)/shard_map/cond/branch_14_fun/ppermute | solution.py:603
  10.9 0.6 %collective-permute-start.142 = (f32[8,2,16,128]{3,2,1,0:T(8,128)S(1)}, f32[8,2,16,128]{3,2,1,0:T(8,128)S(1)}, u32[]{:S(2)}, u32[]{:S(2)}) collective-permute-start(f32[8,2,16,128]{3,2,1,0:T(8,128)S(1)} %get-tuple-element.580), channel_id=1, source_target_pairs={{16,14},{0,18},{17,15},{1,19},{18,0},{2,20},{19,1},{3,21},{20,2},{... | collective-permute-start | bytes 393224 | tf_op jit(solution)/shard_map/cond/branch_14_fun/ppermute | solution.py:603
  11.5 0.0 collective-permute-start.140
  11.5 1.4 %collective-permute-start.141 = (f32[8,8,128]{2,1,0:T(8,128)S(1)}, f32[8,8,128]{2,1,0:T(8,128)S(1)}, u32[]{:S(2)}, u32[]{:S(2)}) collective-permute-start(f32[8,8,128]{2,1,0:T(8,128)S(1)} %get-tuple-element.579), channel_id=1, source_target_pairs={{1,2},{3,4},{5,6},{7,8},{9,10},{11,12},{13,14},{15,0},{2,1},{4,3},... | collective-permute-start | bytes 98312 | tf_op jit(solution)/shard_map/cond/branch_14_fun/ppermute | solution.py:588
  12.9 7.6 %inner_1.30.refs_0_ = f32[8,5,144,128]{3,2,1,0:T(8,128)S(1)} custom-call(f32[8,32,16,128]{3,2,1,0:T(8,128)S(1)} %get-tuple-element.574.refs_0_.refs_1_, f32[8,5,144,128]{3,2,1,0:T(8,128)S(1)} %get-tuple-element.575.refs_1_), custom_call_target="tpu_custom_call" | custom-call | tf_op jit(solution)/shard_map/cond/branch_14_fun/inner_1/pallas_call | solution.py:569
  20.5 0.0 collective-permute-done.140.refs_3_
  20.6 0.0 collective-permute-done.141.refs_4_
  20.6 0.0 collective-permute-done.144.refs_7_
  20.6 0.0 collective-permute-done.143.refs_6_
  20.6 0.0 collective-permute-done.142.refs_5_
  20.6 2.6 %edge_1.30 = (f32[8,5,144,128]{3,2,1,0:T(8,128)S(1)}, f32[8,24,128]{2,1,0:T(8,128)S(1)}, f32[8,8,128]{2,1,0:T(8,128)S(1)}, f32[8,8,128]{2,1,0:T(8,128)S(1)}, f32...) custom-call(s32[2]{0:T(128)S(1)} %get-tuple-element.573.shear_any, ...), custom_call_target="tpu_custom_call", output_to_operand_aliasing={{0}: (1, {})} | custom-call | tf_op jit(solution)/shard_map/cond/branch_14_fun/edge_1/pallas_call | solution.py:569
  23.2 4.4 %collective-permute-start.149 = (f32[8,2,16,128]{3,2,1,0:T(8,128)S(1)}, f32[8,2,16,128]{3,2,1,0:T(8,128)S(1)}, u32[]{:S(2)}, u32[]{:S(2)}) collective-permute-start(f32[8,2,16,128]{3,2,1,0:T(8,128)S(1)} %get-tuple-element.590), channel_id=1, source_target_pairs={{0,16},{16,0},{1,17},{17,1},{2,18},{18,2},{3,19},{19,3},{4,20},{20... | collective-permute-start | bytes 393224 | tf_op jit(solution)/shard_map/cond/branch_14_fun/ppermute | solution.py:590
  27.6 0.0 collective-permute-start.148
  27.6 0.3 collective-permute-start.147
  27.9 5.3 %collective-permute-start.145 = (f32[8,8,128]{2,1,0:T(8,128)S(1)}, f32[8,8,128]{2,1,0:T(8,128)S(1)}, u32[]{:S(2)}, u32[]{:S(2)}) collective-permute-start(f32[8,8,128]{2,1,0:T(8,128)S(1)} %get-tuple-element.587), channel_id=1, source_target_pairs={{0,1},{2,3},{4,5},{6,7},{8,9},{10,11},{12,13},{14,15},{1,0},{3,2},... | collective-permute-start | bytes 98312 | tf_op jit(solution)/shard_map/cond/branch_14_fun/ppermute | solution.py:588
  33.2 0.0 collective-permute-start.146
  33.2 7.6 %inner_2.30 = (f32[8,32,16,128]{3,2,1,0:T(8,128)S(1)}, f32[8,5,144,128]{3,2,1,0:T(8,128)S(1)}) custom-call(f32[8,5,144,128]{3,2,1,0:T(8,128)S(1)} %get-tuple-element.582.refs_0_, f32[8,32,16,128]{3,2,1,0:T(8,128)S(1)} %get-tuple-element.574.refs_0_.refs_1_), custom_call_target="tpu_custom_call" | custom-call | tf_op jit(solution)/shard_map/cond/branch_14_fun/inner_2/pallas_call | solution.py:569
  40.8 0.0 collective-permute-done.145.even_ref
  40.8 0.0 collective-permute-done.146.odd_ref
  40.8 0.0 collective-permute-done.149.refs_2_
  40.9 0.0 collective-permute-done.148.refs_1_
  40.9 0.0 collective-permute-done.147.refs_0_
  40.9 0.1 gather.30
  41.3 2.4 %edge_2.1 = f32[8,32,16,128]{3,2,1,0:T(8,128)} custom-call(s32[2]{0:T(128)S(1)} %pad_add_fusion.shear_any, f32[8,32,16,128]{3,2,1,0:T(8,128)S(1)} %get-tuple-element.635.refs_0_, f32[8,5,144,128]{3,2,1,0:T(8,128)S(1)} %get-tuple-element.636.refs_1_, f32[8,6,16,128]{3,2,1,0:T(8,128)S(1)} %get-tuple-element.637.refs_2_, ...), custom_call_target="tpu_custom_call" | custom-call | tf_op jit(solution)/shard_map/edge_2/pallas_call | solution.py:569
Async XLA Ops:
  4.2 16.4 %collective-permute-start.144 = (f32[8,2,16,128]{3,2,1,0:T(8,128)S(1)}, f32[8,2,16,128]{3,2,1,0:T(8,128)S(1)}, u32[]{:S(2)}, u32[]{:S(2)}) collective-permute-start(f32[8,2,16,128]{3,2,1,0:T(8,128)S(1)} %get-tuple-element.581), channel_id=1, source_target_pairs={{0,16},{16,0},{1,17},{17,1},{2,18},{18,2},{3,19},{19,3},{4,20},{20... | collective-permute-start | bytes 393224 | tf_op jit(solution)/shard_map/cond/branch_14_fun/ppermute | solution.py:590
  4.3 16.3 %collective-permute-start.143 = (f32[8,2,16,128]{3,2,1,0:T(8,128)S(1)}, f32[8,2,16,128]{3,2,1,0:T(8,128)S(1)}, u32[]{:S(2)}, u32[]{:S(2)}) collective-permute-start(f32[8,2,16,128]{3,2,1,0:T(8,128)S(1)} %get-tuple-element.580), channel_id=1, source_target_pairs={{16,15},{0,17},{17,0},{1,18},{18,1},{2,19},{19,2},{3,20},{20,3},{4... | collective-permute-start | bytes 393224 | tf_op jit(solution)/shard_map/cond/branch_14_fun/ppermute | solution.py:603
  10.9 9.7 %collective-permute-start.142 = (f32[8,2,16,128]{3,2,1,0:T(8,128)S(1)}, f32[8,2,16,128]{3,2,1,0:T(8,128)S(1)}, u32[]{:S(2)}, u32[]{:S(2)}) collective-permute-start(f32[8,2,16,128]{3,2,1,0:T(8,128)S(1)} %get-tuple-element.580), channel_id=1, source_target_pairs={{16,14},{0,18},{17,15},{1,19},{18,0},{2,20},{19,1},{3,21},{20,2},{... | collective-permute-start | bytes 393224 | tf_op jit(solution)/shard_map/cond/branch_14_fun/ppermute | solution.py:603
  11.5 9.0 %collective-permute-start.140 = (f32[8,8,128]{2,1,0:T(8,128)S(1)}, f32[8,8,128]{2,1,0:T(8,128)S(1)}, u32[]{:S(2)}, u32[]{:S(2)}) collective-permute-start(f32[8,8,128]{2,1,0:T(8,128)S(1)} %get-tuple-element.578), channel_id=1, source_target_pairs={{0,1},{2,3},{4,5},{6,7},{8,9},{10,11},{12,13},{14,15},{1,0},{3,2},... | collective-permute-start | bytes 98312 | tf_op jit(solution)/shard_map/cond/branch_14_fun/ppermute | solution.py:588
  11.5 9.0 %collective-permute-start.141 = (f32[8,8,128]{2,1,0:T(8,128)S(1)}, f32[8,8,128]{2,1,0:T(8,128)S(1)}, u32[]{:S(2)}, u32[]{:S(2)}) collective-permute-start(f32[8,8,128]{2,1,0:T(8,128)S(1)} %get-tuple-element.579), channel_id=1, source_target_pairs={{1,2},{3,4},{5,6},{7,8},{9,10},{11,12},{13,14},{15,0},{2,1},{4,3},... | collective-permute-start | bytes 98312 | tf_op jit(solution)/shard_map/cond/branch_14_fun/ppermute | solution.py:588
  23.2 17.6 %collective-permute-start.149 = (f32[8,2,16,128]{3,2,1,0:T(8,128)S(1)}, f32[8,2,16,128]{3,2,1,0:T(8,128)S(1)}, u32[]{:S(2)}, u32[]{:S(2)}) collective-permute-start(f32[8,2,16,128]{3,2,1,0:T(8,128)S(1)} %get-tuple-element.590), channel_id=1, source_target_pairs={{0,16},{16,0},{1,17},{17,1},{2,18},{18,2},{3,19},{19,3},{4,20},{20... | collective-permute-start | bytes 393224 | tf_op jit(solution)/shard_map/cond/branch_14_fun/ppermute | solution.py:590
  27.6 13.3 %collective-permute-start.148 = (f32[8,2,16,128]{3,2,1,0:T(8,128)S(1)}, f32[8,2,16,128]{3,2,1,0:T(8,128)S(1)}, u32[]{:S(2)}, u32[]{:S(2)}) collective-permute-start(f32[8,2,16,128]{3,2,1,0:T(8,128)S(1)} %get-tuple-element.589), channel_id=1, source_target_pairs={{16,15},{0,17},{17,0},{1,18},{18,1},{2,19},{19,2},{3,20},{20,3},{4... | collective-permute-start | bytes 393224 | tf_op jit(solution)/shard_map/cond/branch_14_fun/ppermute | solution.py:603
  27.6 13.3 %collective-permute-start.147 = (f32[8,2,16,128]{3,2,1,0:T(8,128)S(1)}, f32[8,2,16,128]{3,2,1,0:T(8,128)S(1)}, u32[]{:S(2)}, u32[]{:S(2)}) collective-permute-start(f32[8,2,16,128]{3,2,1,0:T(8,128)S(1)} %get-tuple-element.589), channel_id=1, source_target_pairs={{16,14},{0,18},{17,15},{1,19},{18,0},{2,20},{19,1},{3,21},{20,2},{... | collective-permute-start | bytes 393224 | tf_op jit(solution)/shard_map/cond/branch_14_fun/ppermute | solution.py:603
  27.9 13.0 %collective-permute-start.145 = (f32[8,8,128]{2,1,0:T(8,128)S(1)}, f32[8,8,128]{2,1,0:T(8,128)S(1)}, u32[]{:S(2)}, u32[]{:S(2)}) collective-permute-start(f32[8,8,128]{2,1,0:T(8,128)S(1)} %get-tuple-element.587), channel_id=1, source_target_pairs={{0,1},{2,3},{4,5},{6,7},{8,9},{10,11},{12,13},{14,15},{1,0},{3,2},... | collective-permute-start | bytes 98312 | tf_op jit(solution)/shard_map/cond/branch_14_fun/ppermute | solution.py:588
  33.2 7.6 %collective-permute-start.146 = (f32[8,8,128]{2,1,0:T(8,128)S(1)}, f32[8,8,128]{2,1,0:T(8,128)S(1)}, u32[]{:S(2)}, u32[]{:S(2)}) collective-permute-start(f32[8,8,128]{2,1,0:T(8,128)S(1)} %get-tuple-element.588), channel_id=1, source_target_pairs={{1,2},{3,4},{5,6},{7,8},{9,10},{11,12},{13,14},{15,0},{2,1},{4,3},... | collective-permute-start | bytes 98312 | tf_op jit(solution)/shard_map/cond/branch_14_fun/ppermute | solution.py:588

commit v7 on v6

--- a/solution.py
+++ b/solution.py
@@ -479,8 +479,8 @@
         lane = lanes_of((width, width))
 
         def correct(n, carry):
-            for k in range(batch):
-                f = n * batch + k
+            for k in range(2 * batch):
+                f = 2 * n * batch + k
                 strip = [x_ref[0, f, 0], x_ref[0, f, 1], jnp.zeros((width - 4 * high, width), jnp.float32)]
                 strip = jnp.concatenate(strip + [x_ref[1, f, 1], x_ref[1, f, 0]], axis=0).T
                 at = slice(PAD, PAD + width)
@@ -488,7 +488,7 @@
                 w1_ref[f, groups - 1, at] = vt_ref[f, groups - 1, at] - jnp.where(lane < width // 2, 0.0, strip)
             return carry
 
-        lax.fori_loop(0, FIELDS // batch, correct, 0)
+        lax.fori_loop(0, FIELDS // (2 * batch), correct, 0)
 
         def correct_rows(f, carry):
             for g in range(groups):

time: 44.1 us -> 42.9 us (0.973); the launches traced: 43.9 us -> 42.3 us
  starting transfers between devices: 18.7 us -> 17.5 us
    ppermute x2, starting transfers between devices: 4.48 us -> 1.78 us  [exchange(): return (even, odd, lax.ppermute(swap[0], 'gx', [(0, 1), (1, 0)]))]
    ppermute x2, starting transfers between devices: 1.41 us -> 3.78 us  [exchange(): lax.ppermute(odd, 'gy', pairs(1))]
    ppermute x2, starting transfers between devices: 5.34 us -> 3.82 us  [exchange(): lax.ppermute(even, 'gy', pairs(0))]
    ppermute x4, starting transfers between devices: 7.5 us -> 8.12 us  [crossing(): return lax.ppermute(shear, ('gx', 'gy'), pairs)]
  transfers between devices with their start and end apart: 10 -> 10, of which waited for: 0 -> 0; matrix products, arithmetic and copies ran while one was open for 0% -> 0% of each run, Pallas kernels for 35% -> 36%
where the time goes in v7:
time: 42.9 us; the launch traced here: 42.3 us
  Pallas kernels  22.4 us (52%)
  starting transfers between devices  17.5 us (41%)
  between operations  1.56 us (4%)
  loops' own time  0.68 us (2%)
    pallas_call x6, Pallas kernels, call(): pl.pallas_call(kernel, name=name, out_shape=[jax.ShapeDtypeStruct(s, jnp....  22.4 us
    ppermute x4, starting transfers between devices, crossing(): return lax.ppermute(shear, ('gx', 'gy'), pairs)  8.12 us
    ppermute x2, starting transfers between devices, exchange(): lax.ppermute(even, 'gy', pairs(0))  3.82 us
    ppermute x2, starting transfers between devices, exchange(): lax.ppermute(odd, 'gy', pairs(1))  3.78 us
    ppermute x2, starting transfers between devices, exchange(): return (even, odd, lax.ppermute(swap[0], 'gx', [(0, 1), (1, 0)]))  1.78 us
  transfers between devices with their start and end apart: 10, of which 0 were waited for; matrix products, arithmetic and copies ran while one was open for 0% of the time, Pallas kernels for 36%

profile of v7, /device:TPU:1, one launch (start us, length us, event | category | flops | bytes accessed | tf_op | source)
XLA Modules:
  0.0 42.3 jit_solution(13682124393723386747)
XLA Ops:
  1.3 0.1 pad_add_fusion.shear_any
  1.4 2.3 %prepare.1 = (f32[8,32,16,128]{3,2,1,0:T(8,128)S(1)}, f32[8,5,144,128]{3,2,1,0:T(8,128)S(1)}, f32[8,24,128]{2,1,0:T(8,128)S(1)}, f32[8,8,128]{2,1,0:T(8,128)S(1)...) custom-call(f32[32,16,128]{2,1,0:T(8,128)} %rho_hbm.1, ...), custom_call_target="tpu_custom_call" | custom-call | tf_op jit(solution)/shard_map/prepare/pallas_call | solution.py:569
  3.7 35.9 %conditional.1 = (f32[8,32,16,128]{3,2,1,0:T(8,128)S(1)}, f32[8,5,144,128]{3,2,1,0:T(8,128)S(1)}, f32[8,6,16,128]{3,2,1,0:T(8,128)S(1)}, f32[8,24,128]{2,1,0:T(8...) conditional(s32[]{:T(128)} %clamp.3, ...), branch_computations={%region_0.1_spmd, %region_1.2_spmd, %region_2.3_spmd, %region_3.4_... | conditional | bytes 3670464 | solution.py:659
  3.9 0.1 collective-permute-start.94
  4.0 4.7 %collective-permute-start.93 = (f32[8,2,16,128]{3,2,1,0:T(8,128)S(1)}, f32[8,2,16,128]{3,2,1,0:T(8,128)S(1)}, u32[]{:S(2)}, u32[]{:S(2)}) collective-permute-start(f32[8,2,16,128]{3,2,1,0:T(8,128)S(1)} %get-tuple-element.480), channel_id=1, source_target_pairs={{16,10},{0,22},{17,11},{1,23},{18,12},{2,24},{19,13},{3,25},{20,14... | collective-permute-start | bytes 393224 | tf_op jit(solution)/shard_map/cond/branch_9_fun/ppermute | solution.py:603
  8.7 2.5 %collective-permute-start.92 = (f32[8,2,16,128]{3,2,1,0:T(8,128)S(1)}, f32[8,2,16,128]{3,2,1,0:T(8,128)S(1)}, u32[]{:S(2)}, u32[]{:S(2)}) collective-permute-start(f32[8,2,16,128]{3,2,1,0:T(8,128)S(1)} %get-tuple-element.480), channel_id=1, source_target_pairs={{16,9},{0,23},{17,10},{1,24},{18,11},{2,25},{19,12},{3,26},{20,13}... | collective-permute-start | bytes 393224 | tf_op jit(solution)/shard_map/cond/branch_9_fun/ppermute | solution.py:603
  11.3 0.0 collective-permute-start.90
  11.3 3.2 %collective-permute-start.91 = (f32[8,8,128]{2,1,0:T(8,128)S(1)}, f32[8,8,128]{2,1,0:T(8,128)S(1)}, u32[]{:S(2)}, u32[]{:S(2)}) collective-permute-start(f32[8,8,128]{2,1,0:T(8,128)S(1)} %get-tuple-element.479), channel_id=1, source_target_pairs={{1,2},{3,4},{5,6},{7,8},{9,10},{11,12},{13,14},{15,0},{2,1},{4,3},... | collective-permute-start | bytes 98312 | tf_op jit(solution)/shard_map/cond/branch_9_fun/ppermute | solution.py:588
  14.5 7.6 %inner_1.25.refs_0_ = f32[8,5,144,128]{3,2,1,0:T(8,128)S(1)} custom-call(f32[8,32,16,128]{3,2,1,0:T(8,128)S(1)} %get-tuple-element.474.refs_0_.refs_1_, f32[8,5,144,128]{3,2,1,0:T(8,128)S(1)} %get-tuple-element.475.refs_1_), custom_call_target="tpu_custom_call" | custom-call | tf_op jit(solution)/shard_map/cond/branch_9_fun/inner_1/pallas_call | solution.py:569
  22.1 0.0 collective-permute-done.90.refs_3_
  22.1 0.0 collective-permute-done.91.refs_4_
  22.1 0.0 collective-permute-done.94.refs_7_
  22.1 0.0 collective-permute-done.93.refs_6_
  22.1 0.0 collective-permute-done.92.refs_5_
  22.1 2.4 %edge_1.25 = (f32[8,5,144,128]{3,2,1,0:T(8,128)S(1)}, f32[8,24,128]{2,1,0:T(8,128)S(1)}, f32[8,8,128]{2,1,0:T(8,128)S(1)}, f32[8,8,128]{2,1,0:T(8,128)S(1)}, f32...) custom-call(s32[2]{0:T(128)S(1)} %get-tuple-element.473.shear_any, ...), custom_call_target="tpu_custom_call", output_to_operand_aliasing={{0}: (1, {})} | custom-call | tf_op jit(solution)/shard_map/cond/branch_9_fun/edge_1/pallas_call | solution.py:569
  24.6 1.7 %collective-permute-start.99 = (f32[8,2,16,128]{3,2,1,0:T(8,128)S(1)}, f32[8,2,16,128]{3,2,1,0:T(8,128)S(1)}, u32[]{:S(2)}, u32[]{:S(2)}) collective-permute-start(f32[8,2,16,128]{3,2,1,0:T(8,128)S(1)} %get-tuple-element.490), channel_id=1, source_target_pairs={{0,16},{16,0},{1,17},{17,1},{2,18},{18,2},{3,19},{19,3},{4,20},{20... | collective-permute-start | bytes 393224 | tf_op jit(solution)/shard_map/cond/branch_9_fun/ppermute | solution.py:590
  26.2 0.0 collective-permute-start.98
  26.2 0.9 %collective-permute-start.97 = (f32[8,2,16,128]{3,2,1,0:T(8,128)S(1)}, f32[8,2,16,128]{3,2,1,0:T(8,128)S(1)}, u32[]{:S(2)}, u32[]{:S(2)}) collective-permute-start(f32[8,2,16,128]{3,2,1,0:T(8,128)S(1)} %get-tuple-element.489), channel_id=1, source_target_pairs={{16,9},{0,23},{17,10},{1,24},{18,11},{2,25},{19,12},{3,26},{20,13}... | collective-permute-start | bytes 393224 | tf_op jit(solution)/shard_map/cond/branch_9_fun/ppermute | solution.py:603
  27.1 3.8 %collective-permute-start.95 = (f32[8,8,128]{2,1,0:T(8,128)S(1)}, f32[8,8,128]{2,1,0:T(8,128)S(1)}, u32[]{:S(2)}, u32[]{:S(2)}) collective-permute-start(f32[8,8,128]{2,1,0:T(8,128)S(1)} %get-tuple-element.487), channel_id=1, source_target_pairs={{0,1},{2,3},{4,5},{6,7},{8,9},{10,11},{12,13},{14,15},{1,0},{3,2},... | collective-permute-start | bytes 98312 | tf_op jit(solution)/shard_map/cond/branch_9_fun/ppermute | solution.py:588
  31.0 0.6 %collective-permute-start.96 = (f32[8,8,128]{2,1,0:T(8,128)S(1)}, f32[8,8,128]{2,1,0:T(8,128)S(1)}, u32[]{:S(2)}, u32[]{:S(2)}) collective-permute-start(f32[8,8,128]{2,1,0:T(8,128)S(1)} %get-tuple-element.488), channel_id=1, source_target_pairs={{1,2},{3,4},{5,6},{7,8},{9,10},{11,12},{13,14},{15,0},{2,1},{4,3},... | collective-permute-start | bytes 98312 | tf_op jit(solution)/shard_map/cond/branch_9_fun/ppermute | solution.py:588
  31.5 7.6 %inner_2.25 = (f32[8,32,16,128]{3,2,1,0:T(8,128)S(1)}, f32[8,5,144,128]{3,2,1,0:T(8,128)S(1)}) custom-call(f32[8,5,144,128]{3,2,1,0:T(8,128)S(1)} %get-tuple-element.482.refs_0_, f32[8,32,16,128]{3,2,1,0:T(8,128)S(1)} %get-tuple-element.474.refs_0_.refs_1_), custom_call_target="tpu_custom_call" | custom-call | tf_op jit(solution)/shard_map/cond/branch_9_fun/inner_2/pallas_call | solution.py:569
  39.2 0.0 collective-permute-done.95.even_ref
  39.2 0.0 collective-permute-done.96.odd_ref
  39.2 0.0 collective-permute-done.99.refs_2_
  39.2 0.0 collective-permute-done.98.refs_1_
  39.2 0.0 collective-permute-done.97.refs_0_
  39.2 0.1 gather.25
  39.6 2.4 %edge_2.1 = f32[8,32,16,128]{3,2,1,0:T(8,128)} custom-call(s32[2]{0:T(128)S(1)} %pad_add_fusion.shear_any, f32[8,32,16,128]{3,2,1,0:T(8,128)S(1)} %get-tuple-element.635.refs_0_, f32[8,5,144,128]{3,2,1,0:T(8,128)S(1)} %get-tuple-element.636.refs_1_, f32[8,6,16,128]{3,2,1,0:T(8,128)S(1)} %get-tuple-element.637.refs_2_, ...), custom_call_target="tpu_custom_call" | custom-call | tf_op jit(solution)/shard_map/edge_2/pallas_call | solution.py:569
Async XLA Ops:
  3.9 18.2 %collective-permute-start.94 = (f32[8,2,16,128]{3,2,1,0:T(8,128)S(1)}, f32[8,2,16,128]{3,2,1,0:T(8,128)S(1)}, u32[]{:S(2)}, u32[]{:S(2)}) collective-permute-start(f32[8,2,16,128]{3,2,1,0:T(8,128)S(1)} %get-tuple-element.481), channel_id=1, source_target_pairs={{0,16},{16,0},{1,17},{17,1},{2,18},{18,2},{3,19},{19,3},{4,20},{20... | collective-permute-start | bytes 393224 | tf_op jit(solution)/shard_map/cond/branch_9_fun/ppermute | solution.py:590
  4.0 18.1 %collective-permute-start.93 = (f32[8,2,16,128]{3,2,1,0:T(8,128)S(1)}, f32[8,2,16,128]{3,2,1,0:T(8,128)S(1)}, u32[]{:S(2)}, u32[]{:S(2)}) collective-permute-start(f32[8,2,16,128]{3,2,1,0:T(8,128)S(1)} %get-tuple-element.480), channel_id=1, source_target_pairs={{16,10},{0,22},{17,11},{1,23},{18,12},{2,24},{19,13},{3,25},{20,14... | collective-permute-start | bytes 393224 | tf_op jit(solution)/shard_map/cond/branch_9_fun/ppermute | solution.py:603
  8.7 13.4 %collective-permute-start.92 = (f32[8,2,16,128]{3,2,1,0:T(8,128)S(1)}, f32[8,2,16,128]{3,2,1,0:T(8,128)S(1)}, u32[]{:S(2)}, u32[]{:S(2)}) collective-permute-start(f32[8,2,16,128]{3,2,1,0:T(8,128)S(1)} %get-tuple-element.480), channel_id=1, source_target_pairs={{16,9},{0,23},{17,10},{1,24},{18,11},{2,25},{19,12},{3,26},{20,13}... | collective-permute-start | bytes 393224 | tf_op jit(solution)/shard_map/cond/branch_9_fun/ppermute | solution.py:603
  11.3 10.8 %collective-permute-start.90 = (f32[8,8,128]{2,1,0:T(8,128)S(1)}, f32[8,8,128]{2,1,0:T(8,128)S(1)}, u32[]{:S(2)}, u32[]{:S(2)}) collective-permute-start(f32[8,8,128]{2,1,0:T(8,128)S(1)} %get-tuple-element.478), channel_id=1, source_target_pairs={{0,1},{2,3},{4,5},{6,7},{8,9},{10,11},{12,13},{14,15},{1,0},{3,2},... | collective-permute-start | bytes 98312 | tf_op jit(solution)/shard_map/cond/branch_9_fun/ppermute | solution.py:588
  11.3 10.8 %collective-permute-start.91 = (f32[8,8,128]{2,1,0:T(8,128)S(1)}, f32[8,8,128]{2,1,0:T(8,128)S(1)}, u32[]{:S(2)}, u32[]{:S(2)}) collective-permute-start(f32[8,8,128]{2,1,0:T(8,128)S(1)} %get-tuple-element.479), channel_id=1, source_target_pairs={{1,2},{3,4},{5,6},{7,8},{9,10},{11,12},{13,14},{15,0},{2,1},{4,3},... | collective-permute-start | bytes 98312 | tf_op jit(solution)/shard_map/cond/branch_9_fun/ppermute | solution.py:588
  24.6 14.6 %collective-permute-start.99 = (f32[8,2,16,128]{3,2,1,0:T(8,128)S(1)}, f32[8,2,16,128]{3,2,1,0:T(8,128)S(1)}, u32[]{:S(2)}, u32[]{:S(2)}) collective-permute-start(f32[8,2,16,128]{3,2,1,0:T(8,128)S(1)} %get-tuple-element.490), channel_id=1, source_target_pairs={{0,16},{16,0},{1,17},{17,1},{2,18},{18,2},{3,19},{19,3},{4,20},{20... | collective-permute-start | bytes 393224 | tf_op jit(solution)/shard_map/cond/branch_9_fun/ppermute | solution.py:590
  26.2 13.0 %collective-permute-start.98 = (f32[8,2,16,128]{3,2,1,0:T(8,128)S(1)}, f32[8,2,16,128]{3,2,1,0:T(8,128)S(1)}, u32[]{:S(2)}, u32[]{:S(2)}) collective-permute-start(f32[8,2,16,128]{3,2,1,0:T(8,128)S(1)} %get-tuple-element.489), channel_id=1, source_target_pairs={{16,10},{0,22},{17,11},{1,23},{18,12},{2,24},{19,13},{3,25},{20,14... | collective-permute-start | bytes 393224 | tf_op jit(solution)/shard_map/cond/branch_9_fun/ppermute | solution.py:603
  26.2 13.0 %collective-permute-start.97 = (f32[8,2,16,128]{3,2,1,0:T(8,128)S(1)}, f32[8,2,16,128]{3,2,1,0:T(8,128)S(1)}, u32[]{:S(2)}, u32[]{:S(2)}) collective-permute-start(f32[8,2,16,128]{3,2,1,0:T(8,128)S(1)} %get-tuple-element.489), channel_id=1, source_target_pairs={{16,9},{0,23},{17,10},{1,24},{18,11},{2,25},{19,12},{3,26},{20,13}... | collective-permute-start | bytes 393224 | tf_op jit(solution)/shard_map/cond/branch_9_fun/ppermute | solution.py:603
  27.1 12.0 %collective-permute-start.95 = (f32[8,8,128]{2,1,0:T(8,128)S(1)}, f32[8,8,128]{2,1,0:T(8,128)S(1)}, u32[]{:S(2)}, u32[]{:S(2)}) collective-permute-start(f32[8,8,128]{2,1,0:T(8,128)S(1)} %get-tuple-element.487), channel_id=1, source_target_pairs={{0,1},{2,3},{4,5},{6,7},{8,9},{10,11},{12,13},{14,15},{1,0},{3,2},... | collective-permute-start | bytes 98312 | tf_op jit(solution)/shard_map/cond/branch_9_fun/ppermute | solution.py:588
  31.0 8.2 %collective-permute-start.96 = (f32[8,8,128]{2,1,0:T(8,128)S(1)}, f32[8,8,128]{2,1,0:T(8,128)S(1)}, u32[]{:S(2)}, u32[]{:S(2)}) collective-permute-start(f32[8,8,128]{2,1,0:T(8,128)S(1)} %get-tuple-element.488), channel_id=1, source_target_pairs={{1,2},{3,4},{5,6},{7,8},{9,10},{11,12},{13,14},{15,0},{2,1},{4,3},... | collective-permute-start | bytes 98312 | tf_op jit(solution)/shard_map/cond/branch_9_fun/ppermute | solution.py:588
